TPU v7x, 32 devices: a whole 2x2x4 slice. The times are simulated.
32 devices in a mesh: groups: 2 (over y), ctx: 8 (over z, x), lane: 2 (over core).
Axes of the slice: x: 2, y: 2, z: 4, core: 2. Of those that a mesh axis runs over, the one named last changes fastest.
Arguments:
- pre_conv: bfloat16 [4, 1024, 2560], P(('groups', 'lane'), 'ctx'), parts along dimension 0, as said below
- step_size: float32 [4, 64, 1024], P(('groups', 'lane'), None, 'ctx'), parts along dimension 0, as said below
- lengths: int32 [4, 4], P(('groups', 'lane')), parts along dimension 0, may hold values from 1 to 4, 8 in all within a row
- conv_weight: bfloat16 [4, 2560], replicated, as said below
- conv_bias: bfloat16 [2560], replicated, as said below
- decay_rate: float32 [64], replicated, as said below
- skip_gain: float32 [64], replicated, may hold values from 0.5 to 1.5
Outputs:
- mamba_out: bfloat16 [4, 1024, 2048], P(('groups', 'lane'), 'ctx'), parts along dimension 0
There are 2 independent parts, one for each index of `groups`. A program takes and returns all parts, laid end to end along the dimension named above; an argument that names none is the same for every part. Nothing has to cross between parts.
Inputs may be any that keep to these rules, and one draw needn't show every extreme that they name: Each lane's row of lengths sums to 8; every entry is at least 1. `step_size`: positive step sizes. `decay_rate`: positive rates. `pre_conv`: entries of order one. `conv_weight`: taps of order one. `conv_bias`: entries of order one.
All inputs are finite; a program needn't handle non-finite values.
Results may differ from a plain program's by a relative error of at most 0.0054.
Values may be sent and summed in bfloat16 or wider, within the bound.
No kernel may reach another device: no remote copies, remote signals or barrier semaphores. Data moves between devices by JAX's collectives and lax.ppermute only.
A program may use at most 256 MiB of HBM per device.

v0:
```python
import jax
import jax.numpy as jnp
from jax import lax
from jax.sharding import PartitionSpec as P

HEADS = 64
HEAD_DIM = 32
STATE = 64
BC_GROUPS = 4


def shifted(value, axis, steps):
    count = lax.axis_size(axis)
    first, last = (max(0, -steps), min(count, count - steps))
    return lax.ppermute(value, axis, [(source, source + steps) for source in range(first, last)])


def carried_in(array, axis, combine, identity):
    length, index = (lax.axis_size(axis), lax.axis_index(axis))
    everything = jax.tree.map(
        lambda part, kind: lax.all_gather(part.astype(kind), axis),
        array,
        (jnp.bfloat16, jnp.bfloat16),
    )
    start = jax.tree.map(
        lambda part, zero: jnp.broadcast_to(jnp.asarray(zero, part.dtype), part.shape),
        array,
        identity,
    )

    def step(k, before):
        reached = k < index
        new = combine(
            before, jax.tree.map(lambda part, own: part[k].astype(own.dtype), everything, array)
        )
        return jax.tree.map(lambda a, b: jnp.where(reached, a, b), new, before)

    return lax.fori_loop(0, length, step, start)


def convolve(padded, conv_weight, conv_bias, count_rows):
    total = conv_bias.astype(jnp.float32)[None, :]
    for offset in range(conv_weight.shape[0]):
        total = (
            total
            + padded[offset : offset + count_rows].astype(jnp.float32)
            * conv_weight[offset].astype(jnp.float32)[None, :]
        )
    return jax.nn.silu(total).astype(jnp.bfloat16)


def group_terms(values, keys_in, queries, decay_rate, step_rows):
    heads_group = step_rows.shape[0]
    count_rows = step_rows.shape[1]
    values = values.reshape(count_rows, heads_group, -1)
    cumulative = jnp.cumsum(-step_rows * decay_rate[:, None], axis=1)
    scores = jnp.einsum("tn,sn->ts", queries, keys_in, preferred_element_type=jnp.float32)
    later = lax.broadcasted_iota(jnp.int32, (count_rows, count_rows), 0)
    earlier = lax.broadcasted_iota(jnp.int32, (count_rows, count_rows), 1)
    spread = jnp.where(
        (later >= earlier)[None], cumulative[:, :, None] - cumulative[:, None, :], -1e30
    )
    weights = (jnp.exp(spread) * scores[None]).astype(jnp.bfloat16)
    scaled = (values * step_rows.T[:, :, None]).astype(jnp.bfloat16)
    diagonal_part = jnp.einsum("hts,shp->thp", weights, scaled, preferred_element_type=jnp.float32)
    tail_weight = jnp.exp(cumulative[:, -1:] - cumulative)
    written = (values * (step_rows * tail_weight).T[:, :, None]).astype(jnp.bfloat16)
    local_state = jnp.einsum("tn,thp->hpn", keys_in, written, preferred_element_type=jnp.float32)
    return (diagonal_part, local_state, jnp.exp(cumulative[:, -1]), jnp.exp(cumulative), values)


def finish_group(diagonal_part, entry_decay, queries, incoming, values, skip_gain):
    incoming_rounded = incoming.astype(jnp.bfloat16)
    carried_part = jnp.einsum(
        "tn,hpn->thp", queries, incoming_rounded, preferred_element_type=jnp.float32
    )
    carried_part = carried_part * entry_decay.T[:, :, None]
    return diagonal_part + carried_part + skip_gain[None, :, None] * values.astype(jnp.float32)


def combine(earlier, later):
    return (earlier[0] * later[0], later[0][:, None, None] * earlier[1] + later[1])


def shards(pre_conv, step_size, lengths, conv_weight, conv_bias, decay_rate, skip_gain):
    count_rows = pre_conv.shape[1]
    kernel_len = conv_weight.shape[0]
    heads_group = HEADS // BC_GROUPS
    position = lax.axis_index("ctx")
    sizes_row = lengths[0]
    starts = jnp.cumsum(sizes_row) - sizes_row
    fresh = jnp.any(starts == position)
    retain = jnp.where(fresh, 0.0, 1.0).astype(jnp.float32)
    own_rows = pre_conv[0]
    previous = shifted(own_rows[count_rows - kernel_len + 1 :], "ctx", 1)
    previous = jnp.where(fresh, jnp.zeros_like(previous), previous)
    convolved = convolve(
        jnp.concatenate([previous, own_rows], axis=0), conv_weight, conv_bias, count_rows
    )
    values = convolved[:, : HEADS * HEAD_DIM]
    keys_all = convolved[:, HEADS * HEAD_DIM : HEADS * HEAD_DIM + BC_GROUPS * STATE]
    queries_all = convolved[:, HEADS * HEAD_DIM + BC_GROUPS * STATE :]
    step_rows = step_size[0]
    results = []
    pieces = []
    for bc_group in range(BC_GROUPS):
        low = bc_group * heads_group
        high = low + heads_group
        pieces.append(
            group_terms(
                values[:, low * HEAD_DIM : high * HEAD_DIM],
                keys_all[:, bc_group * STATE : (bc_group + 1) * STATE],
                queries_all[:, bc_group * STATE : (bc_group + 1) * STATE],
                decay_rate[low:high],
                step_rows[low:high],
            )
        )
    decays = jnp.concatenate([piece[2] for piece in pieces], axis=0) * retain
    states = jnp.concatenate([piece[1] for piece in pieces], axis=0)
    identity = (jnp.ones_like(decays), jnp.zeros_like(states))
    totals = carried_in((decays, states), "ctx", combine, identity)
    incoming = totals[1] * retain
    for bc_group in range(BC_GROUPS):
        low = bc_group * heads_group
        high = low + heads_group
        piece = pieces[bc_group]
        results.append(
            finish_group(
                piece[0],
                piece[3],
                queries_all[:, bc_group * STATE : (bc_group + 1) * STATE],
                incoming[low:high],
                piece[4],
                skip_gain[low:high],
            )
        )
    output = (
        jnp.concatenate(results, axis=1).reshape(count_rows, HEADS * HEAD_DIM).astype(jnp.bfloat16)
    )
    return output[None]


def solution(mesh):
    in_specs = (
        P(("groups", "lane"), "ctx", None),
        P(("groups", "lane"), None, "ctx"),
        P(("groups", "lane"), None),
        P(),
        P(),
        P(),
        P(),
    )
    out_specs = P(("groups", "lane"), "ctx", None)
    return jax.shard_map(shards, mesh=mesh, in_specs=in_specs, out_specs=out_specs, check_vma=False)
```

profile of v0, /device:TPU:0, one launch (start us, length us, event | category | flops | bytes accessed | tf_op | source)
XLA Modules:
  0.0 120.9 jit_solution(5062469529235466685)
XLA Ops:
  6.5 0.8 slice_bitcast_fusion
  7.3 4.8 %collective-permute-start = (bf16[3,2560]{1,0:T(4,128)(2,1)S(1)}, bf16[3,2560]{1,0:T(4,128)(2,1)S(1)}, u32[]{:S(2)}, u32[]{:S(2)}) collective-permute-start(bf16[3,2560]{1,0:T(4,128)(2,1)S(1)} %slice_bitcast_fusion), channel_id=1, source_target_pairs={{0,2},{2,4},{4,6},{6,8},{8,10},{10,12},{12,14},{1,3},{3,5},{5,7},{... | collective-permute-start | bytes 46088 | tf_op jit(solution)/shard_map/ppermute | solution.py:15
  12.2 0.9 fusion.111
  13.1 0.8 fusion.102
  13.9 0.3 reduce_window_sum.39
  14.2 0.2 slice_reduce_fusion
  14.4 0.3 reduce_window_sum.38
  14.7 0.2 slice_reduce_fusion.1
  14.8 0.3 reduce_window_sum.37
  15.1 0.2 slice_reduce_fusion.2
  15.3 0.3 reduce_window_sum.36
  15.6 0.2 slice_reduce_fusion.3
  15.8 1.0 convert_reduce_fusion.3
  16.8 0.8 reduce-window.9
  17.6 0.8 fusion.101
  18.5 1.3 %compare_reduce_fusion = pred[]{:T(512)} fusion(s32[1,4]{1,0:T(1,128)} %param.11, s32[4,1]{0,1:T(1,128)S(1)} %reduce-window.9, s32[]{:T(128)} %axis_index.19), kind=kLoop, calls=%fused_computation.162 | loop fusion | flops 11 | bytes 37 | tf_op jit(solution)/shard_map/reduce_or | solution.py:92
  19.8 1.4 %copy.19 = bf16[1,128,2560]{1,2,0:T(8,128)(2,1)S(1)} copy(bf16[1,128,2560]{2,1,0:T(8,128)(2,1)} %param.9) | data formatting | bytes 1310720 | tf_op args[0]
  21.2 0.6 broadcast_select_fusion
  21.9 0.4 copy.20
  22.2 3.1 %multiply_convert_fusion = bf16[128,2560]{0,1:T(8,128)(2,1)S(1)} fusion(bf16[128,2560]{0,1:T(8,128)(2,1)S(1)} %bitcast.138, bf16[3,2560]{0,1:T(8,128)(2,1)S(1)} %copy.20, f32[2560]{0:T(1024)S(1)} %get-tuple-element.120, f32[2560]{0:T(1024)S(1)} %get-tuple-element.121, f32[2560]{0:T(1024)S(1)} %get-tuple-element.119, f32[2560]{0:T(1024)S(1)} %get-tuple-element.118, ...), kind=kLoop, calls=%fused_computation.7 | loop fusion | flops 8519680 | bytes 1377280 | tf_op jit(solution)/shard_map/convert_element_type | solution.py:49
  25.4 0.2 fusion.13
  25.6 0.2 fusion.14
  25.9 0.2 fusion.16
  26.1 0.9 pad_maximum_fusion.1
  27.8 18.7 %all-gather = bf16[8,1,64]{2,1,0:T(2,128)(2,1)S(1)} all-gather(bf16[1,1,64]{2,1,0:T(2,128)(2,1)S(1)} %fusion.104), channel_id=1, replica_groups=mesh['groups'=2,'ctx'=8,'lane'=2] {'ctx'}, dimensions={0}, use_global_device_ids=true | all-gather | bytes 1152 | tf_op jit(solution)/shard_map/all_gather | solution.py:21
  46.6 0.2 fusion.91
  46.8 0.2 fusion.82
  47.0 0.2 fusion.79
  47.2 0.2 fusion.76
  47.3 0.5 convolution_bitcast_fusion.3
  47.8 0.5 convolution_bitcast_fusion.2
  48.3 0.5 convolution_bitcast_fusion.1
  48.7 0.5 convolution_bitcast_fusion
  49.2 51.7 %all-gather.3.cloned.1.call-done = bf16[8,64,32,64]{3,2,1,0:T(8,128)(2,1)} async-done(((bf16[1,64,32,64]{3,2,1,0:T(8,128)(2,1)}), bf16[8,64,32,64]{3,2,1,0:T(8,128)(2,1)}) %all-gather.3.cloned.1.call-update) | async-done | bytes 2097168 | tf_op jit(solution)/shard_map/all_gather | solution.py:21
  101.0 11.1 %while.14 = (s32[]{:T(128)}, f32[64,32,64]{2,1,0:T(8,128)S(1)}, s32[]{:T(128)}, bf16[8,64]{1,0:T(8,128)(2,1)S(1)}, bf16[8,64,32,64]{3,2,1,0:T(8,128)(2,1)}, /*index=5*/s32[]{:T(128)}, s32[]{:T(128)}) while((s32[]{:T(128)}, f32[64,32,64]{2,1,0:T(8,128)S(1)}, s32[]{:T(128)}, bf16[8,64]{1,0:T(8,128)(2,1)S(1)}, ...), condition=%wide.region_7.8_spmd.clone, body=%wide.region_6.7_spmd.clone.sunk | while | flops 655428 | bytes 1311465 | solution.py:38
  101.0 1.4 %fusion.113 = f32[64,32,64]{2,1,0:T(8,128)S(1)} fusion(f32[64,32,64]{2,1,0:T(8,128)S(1)} %get-tuple-element.203, bf16[8,64,32,64]{3,2,1,0:T(8,128)(2,1)} %get-tuple-element.213, s32[]{:T(128)} %get-tuple-element.202, f32[64]{0:T(128)S(1)} %bitcast_convert_fusion.2, pred[]{:T(512)S(6)} %compare.3, pred[]{:T(512)S(6)} %lt.22), kind=kLoop, calls=%fused_computation.1.clone.1 | loop fusion | flops 655360 | bytes 1310982 | tf_op jit(solution)/shard_map/while/body/eval_jaxpr/jit(_where)/select_n | solution.py:36
  102.4 1.4 %fusion.113 = f32[64,32,64]{2,1,0:T(8,128)S(1)} fusion(f32[64,32,64]{2,1,0:T(8,128)S(1)} %get-tuple-element.203, bf16[8,64,32,64]{3,2,1,0:T(8,128)(2,1)} %get-tuple-element.213, s32[]{:T(128)} %get-tuple-element.202, f32[64]{0:T(128)S(1)} %bitcast_convert_fusion.2, pred[]{:T(512)S(6)} %compare.3, pred[]{:T(512)S(6)} %lt.22), kind=kLoop, calls=%fused_computation.1.clone.1 | loop fusion | flops 655360 | bytes 1310982 | tf_op jit(solution)/shard_map/while/body/eval_jaxpr/jit(_where)/select_n | solution.py:36
  103.7 1.4 %fusion.113 = f32[64,32,64]{2,1,0:T(8,128)S(1)} fusion(f32[64,32,64]{2,1,0:T(8,128)S(1)} %get-tuple-element.203, bf16[8,64,32,64]{3,2,1,0:T(8,128)(2,1)} %get-tuple-element.213, s32[]{:T(128)} %get-tuple-element.202, f32[64]{0:T(128)S(1)} %bitcast_convert_fusion.2, pred[]{:T(512)S(6)} %compare.3, pred[]{:T(512)S(6)} %lt.22), kind=kLoop, calls=%fused_computation.1.clone.1 | loop fusion | flops 655360 | bytes 1310982 | tf_op jit(solution)/shard_map/while/body/eval_jaxpr/jit(_where)/select_n | solution.py:36
  105.1 1.4 %fusion.113 = f32[64,32,64]{2,1,0:T(8,128)S(1)} fusion(f32[64,32,64]{2,1,0:T(8,128)S(1)} %get-tuple-element.203, bf16[8,64,32,64]{3,2,1,0:T(8,128)(2,1)} %get-tuple-element.213, s32[]{:T(128)} %get-tuple-element.202, f32[64]{0:T(128)S(1)} %bitcast_convert_fusion.2, pred[]{:T(512)S(6)} %compare.3, pred[]{:T(512)S(6)} %lt.22), kind=kLoop, calls=%fused_computation.1.clone.1 | loop fusion | flops 655360 | bytes 1310982 | tf_op jit(solution)/shard_map/while/body/eval_jaxpr/jit(_where)/select_n | solution.py:36
  106.5 1.4 %fusion.113 = f32[64,32,64]{2,1,0:T(8,128)S(1)} fusion(f32[64,32,64]{2,1,0:T(8,128)S(1)} %get-tuple-element.203, bf16[8,64,32,64]{3,2,1,0:T(8,128)(2,1)} %get-tuple-element.213, s32[]{:T(128)} %get-tuple-element.202, f32[64]{0:T(128)S(1)} %bitcast_convert_fusion.2, pred[]{:T(512)S(6)} %compare.3, pred[]{:T(512)S(6)} %lt.22), kind=kLoop, calls=%fused_computation.1.clone.1 | loop fusion | flops 655360 | bytes 1310982 | tf_op jit(solution)/shard_map/while/body/eval_jaxpr/jit(_where)/select_n | solution.py:36
  107.9 1.4 %fusion.113 = f32[64,32,64]{2,1,0:T(8,128)S(1)} fusion(f32[64,32,64]{2,1,0:T(8,128)S(1)} %get-tuple-element.203, bf16[8,64,32,64]{3,2,1,0:T(8,128)(2,1)} %get-tuple-element.213, s32[]{:T(128)} %get-tuple-element.202, f32[64]{0:T(128)S(1)} %bitcast_convert_fusion.2, pred[]{:T(512)S(6)} %compare.3, pred[]{:T(512)S(6)} %lt.22), kind=kLoop, calls=%fused_computation.1.clone.1 | loop fusion | flops 655360 | bytes 1310982 | tf_op jit(solution)/shard_map/while/body/eval_jaxpr/jit(_where)/select_n | solution.py:36
  109.3 1.4 %fusion.113 = f32[64,32,64]{2,1,0:T(8,128)S(1)} fusion(f32[64,32,64]{2,1,0:T(8,128)S(1)} %get-tuple-element.203, bf16[8,64,32,64]{3,2,1,0:T(8,128)(2,1)} %get-tuple-element.213, s32[]{:T(128)} %get-tuple-element.202, f32[64]{0:T(128)S(1)} %bitcast_convert_fusion.2, pred[]{:T(512)S(6)} %compare.3, pred[]{:T(512)S(6)} %lt.22), kind=kLoop, calls=%fused_computation.1.clone.1 | loop fusion | flops 655360 | bytes 1310982 | tf_op jit(solution)/shard_map/while/body/eval_jaxpr/jit(_where)/select_n | solution.py:36
  110.7 1.4 %fusion.113 = f32[64,32,64]{2,1,0:T(8,128)S(1)} fusion(f32[64,32,64]{2,1,0:T(8,128)S(1)} %get-tuple-element.203, bf16[8,64,32,64]{3,2,1,0:T(8,128)(2,1)} %get-tuple-element.213, s32[]{:T(128)} %get-tuple-element.202, f32[64]{0:T(128)S(1)} %bitcast_convert_fusion.2, pred[]{:T(512)S(6)} %compare.3, pred[]{:T(512)S(6)} %lt.22), kind=kLoop, calls=%fused_computation.1.clone.1 | loop fusion | flops 655360 | bytes 1310982 | tf_op jit(solution)/shard_map/while/body/eval_jaxpr/jit(_where)/select_n | solution.py:36
  112.2 0.2 fusion.9
  112.4 0.2 fusion.10
  112.6 0.2 fusion.11
  112.8 0.2 fusion.12
  113.0 1.0 copy.21
  (30 shorter events, 0.7 us)
Async XLA Ops:
  6.5 14.7 %copy-start.2 = (bf16[2560]{0:T(1024)(128)(2,1)S(1)}, bf16[2560]{0:T(1024)(128)(2,1)}, u32[]{:S(2)}) copy-start(bf16[2560]{0:T(1024)(128)(2,1)} %param.13) | copy-start | bytes 15364
  6.5 94.4 %all-gather.3.cloned.1.call-start = ((), (), s32[]{:S(2)}) async-start(), calls=%async_computation | async-start | bytes 4718592 | tf_op jit(solution)/shard_map/all_gather | solution.py:21
  7.3 13.9 %collective-permute-start = (bf16[3,2560]{1,0:T(4,128)(2,1)S(1)}, bf16[3,2560]{1,0:T(4,128)(2,1)S(1)}, u32[]{:S(2)}, u32[]{:S(2)}) collective-permute-start(bf16[3,2560]{1,0:T(4,128)(2,1)S(1)} %slice_bitcast_fusion), channel_id=1, source_target_pairs={{0,2},{2,4},{4,6},{6,8},{8,10},{10,12},{12,14},{1,3},{3,5},{5,7},{... | collective-permute-start | bytes 46088 | tf_op jit(solution)/shard_map/ppermute | solution.py:15
  25.5 21.0 %copy-start.1 = (f32[64]{0:T(128)S(1)}, f32[64]{0:T(128)}, u32[]{:S(2)}) copy-start(f32[64]{0:T(128)} %param.15) | copy-start | bytes 772
  25.6 21.0 %copy-start = (f32[1,64,128]{2,1,0:T(8,128)S(1)}, f32[1,64,128]{2,1,0:T(8,128)}, u32[]{:S(2)}) copy-start(f32[1,64,128]{2,1,0:T(8,128)} %param.10) | copy-start | bytes 98308
Sparse Core Ops, SparseCore 0:
  27.2 73.7 all-gather.2
where the time goes:
time: 122 us; the launch traced here: 121 us
  waiting for transfers between devices  51.8 us (42%)
  other arithmetic  21.8 us (18%)
  blocking collectives  18.7 us (15%)
  between operations  14.2 us (12%)
  local copies, waits for them, and re-layouts  5.35 us (4%)
  starting transfers between devices  4.85 us (4%)
  matrix products  3.99 us (3%)
    all_gather x1, waiting for transfers between devices, carried_in(): lax.all_gather(part.astype(kind), axis)  51.7 us
    all_gather x1, blocking collectives, carried_in(): lax.all_gather(part.astype(kind), axis)  18.7 us
    select_n x8, other arithmetic, step(): return jax.tree.map(lambda a, b: jnp.where(reached, a, b), new, before)  10.9 us
    ppermute x1, starting transfers between devices, shifted(): lax.ppermute(value, axis, [(source, source + steps) for source in range(f...  4.84 us
    convert_element_type x1, other arithmetic, convolve(): return jax.nn.silu(total).astype(jnp.bfloat16)  3.08 us
  transfers between devices with their start and end apart: 2, of which 1 were waited for; matrix products, arithmetic and copies ran while one was open for 10% of the time, Pallas kernels for 0%

commit v1 on v0

--- a/solution.py
+++ b/solution.py
@@ -1,12 +1,379 @@
 import jax
 import jax.numpy as jnp
 from jax import lax
+from jax.experimental import pallas as pl
+from jax.experimental.pallas import tpu as pltpu
 from jax.sharding import PartitionSpec as P
 
 HEADS = 64
 HEAD_DIM = 32
 STATE = 64
 BC_GROUPS = 4
+HEADS_GROUP = HEADS // BC_GROUPS
+VALUES = HEADS * HEAD_DIM
+WIDE = HEADS_GROUP * HEAD_DIM
+STATE_ROWS = BC_GROUPS * STATE
+TAIL_AT = STATE_ROWS
+HEAD_AT = TAIL_AT + 16
+SCALE_AT = HEAD_AT + 16
+FIRST_ROWS = SCALE_AT + 16
+SECOND_ROWS = STATE_ROWS + 16
+LOG2E = 1.4426950408889634
+VMEM = pl.BlockSpec(memory_space=pltpu.VMEM)
+SMEM = pl.BlockSpec(memory_space=pltpu.SMEM)
+f32 = jnp.float32
+bf16 = jnp.bfloat16
+
+
+def iota(shape, dim):
+    return lax.broadcasted_iota(jnp.int32, shape, dim)
+
+
+def dot(a, b, contract=((1,), (0,)), precision=None):
+    return lax.dot_general(
+        a, b, (contract, ((), ())), preferred_element_type=f32, precision=precision
+    )
+
+
+def is_fresh(lengths_ref, position):
+    found = jnp.int32(0)
+    start = jnp.int32(0)
+    for k in range(lengths_ref.shape[1]):
+        found = jnp.where(start == position, jnp.int32(1), found)
+        start = start + lengths_ref[0, k]
+    return found
+
+
+def halves(value):
+    high = value.astype(bf16)
+    return high, (value - high.astype(f32)).astype(bf16)
+
+
+def cumulative_of(step, rate_row):
+    eye = iota((HEADS, HEADS), 0) == iota((HEADS, HEADS), 1)
+    rate = jnp.sum(jnp.where(eye, rate_row, 0.0), axis=1, keepdims=True)
+    tokens = step.shape[1]
+    upto = (iota((tokens, tokens), 0) <= iota((tokens, tokens), 1)).astype(f32)
+    return dot(-step * rate, upto, precision=lax.Precision.HIGHEST)
+
+
+def spread_matrix():
+    rows, lanes = 2 * HEADS_GROUP, WIDE
+    return (iota((rows, lanes), 0) % HEADS_GROUP == iota((rows, lanes), 1) // HEAD_DIM).astype(bf16)
+
+
+def spread(per_head, group, matrix):
+    part = per_head[group * HEADS_GROUP : (group + 1) * HEADS_GROUP]
+    return dot(jnp.concatenate(halves(part), axis=0), matrix, ((0,), (0,)))
+
+
+def half_silu(half):
+    return half + half * jnp.tanh(half)
+
+
+def to_rows(strip, first):
+    rows = iota((8, WIDE), 0)
+    top = jnp.zeros((8, WIDE), f32)
+    low = jnp.zeros((8, WIDE), f32)
+    for k in range(strip.shape[1] // WIDE):
+        chunk = strip[:, k * WIDE : (k + 1) * WIDE]
+        moved = pltpu.roll(chunk, (3 * k - first) % 8, 0)
+        for base, at in ((0, "top"), (8, "low")):
+            low_row, high_row = 3 * k - base, 3 * k + 2 - base
+            if high_row < 0 or low_row > 7:
+                continue
+            mask = (rows >= low_row) & (rows <= high_row)
+            if at == "top":
+                top = jnp.where(mask, moved, top)
+            else:
+                low = jnp.where(mask, moved, low)
+    return jnp.concatenate([top, low], axis=0)
+
+
+def state_kernel(
+    lengths_ref, x_ref, step_ref, weight_ref, bias_ref, rate_ref, conv_ref, cumulative_ref, sent_ref
+):
+    fresh = is_fresh(lengths_ref, lax.axis_index("ctx"))
+    count = x_ref.shape[1]
+    step = step_ref[0]
+    cumulative = cumulative_of(step, rate_ref[...])
+    cumulative_ref[...] = cumulative
+    last = cumulative[:, count - 1 :]
+    tail = step * jnp.exp(last - cumulative)
+    lanes = iota((HEADS, count), 1)
+    kept = jnp.where((lanes >= KERNEL_EDGE) | (fresh == 1), tail, 0.0)
+    scales = jnp.where(lanes == KERNEL_EDGE, jnp.exp(last), tail)
+    high, low = halves(scales)
+    place = iota((HEADS, 128), 1) - iota((HEADS, 128), 0)
+    picked = dot(high, (place == 0).astype(bf16), ((0,), (0,)))
+    picked = picked + dot(low, (place == HEADS).astype(bf16), ((0,), (0,)))
+    sent_ref[SCALE_AT : SCALE_AT + 16, :] = jnp.concatenate(
+        [picked[:16], jnp.zeros((16, WIDE - 128), f32)], axis=1
+    ).astype(bf16)
+    sent_ref[TAIL_AT : TAIL_AT + 16, :] = to_rows(x_ref[0, count - 16 :, :].astype(f32)[8:], 5).astype(bf16)
+    sent_ref[HEAD_AT : HEAD_AT + 16, :] = to_rows(x_ref[0, :16, :].astype(f32)[:8], 0).astype(bf16)
+
+    matrix = spread_matrix()
+    weight = weight_ref[...].astype(f32) * 0.5
+    bias = bias_ref[...].astype(f32) * 0.5
+
+    def conv_tile(j):
+        cols = slice(j * 128, (j + 1) * 128)
+        x = x_ref[0, :, cols].astype(f32)
+        padded = jnp.concatenate([jnp.zeros((8, 128), f32), x], axis=0)
+        total = bias[j : j + 1, :] + x * weight[3:4, cols]
+        for back in range(1, 4):
+            total = total + padded[8 - back : 8 - back + count] * weight[3 - back : 4 - back, cols]
+        return half_silu(total)
+
+    tiles = CONV_TILES
+    keys = []
+    for j in range(tiles - 4, tiles):
+        tile = conv_tile(j).astype(bf16)
+        conv_ref[:, j * 128 : (j + 1) * 128] = tile
+        keys.append(tile)
+    for group in range(BC_GROUPS):
+        scale = spread(kept, group, matrix)
+        parts = []
+        for i in range(WIDE // 128):
+            j = group * (WIDE // 128) + i
+            tile = conv_tile(j)
+            conv_ref[:, j * 128 : (j + 1) * 128] = tile.astype(bf16)
+            parts.append((tile * scale[:, i * 128 : (i + 1) * 128]).astype(bf16))
+        written = jnp.concatenate(parts, axis=1)
+        key = keys[group // 2][:, (group % 2) * STATE : (group % 2 + 1) * STATE]
+        local = dot(key, written, ((0,), (0,)))
+        sent_ref[group * STATE : (group + 1) * STATE, :] = local.astype(bf16)
+
+
+KERNEL_EDGE = 3
+CONV_TILES = 20
+
+
+def edge_rows(tail_block, head_block, weight, bias):
+    rows = iota((16, WIDE), 0)
+    third = rows % 3
+    chunk = rows // 3
+
+    def blocked(lines):
+        out = jnp.zeros((16, WIDE), f32)
+        for k in range(5):
+            out = jnp.where(chunk == k, lines[k], out)
+        return out
+
+    taps = [
+        blocked([weight[tap : tap + 1, k * WIDE : (k + 1) * WIDE] for k in range(5)])
+        for tap in range(4)
+    ]
+    offset = blocked(
+        [
+            jnp.concatenate([bias[4 * k + i : 4 * k + i + 1, :] for i in range(4)], axis=1)
+            for k in range(5)
+        ]
+    )
+    back1 = jnp.where(third == 0, pltpu.roll(tail_block, 14, 0), pltpu.roll(head_block, 1, 0))
+    back2 = jnp.where(third == 2, pltpu.roll(head_block, 2, 0), pltpu.roll(tail_block, 15, 0))
+    total = offset + head_block * taps[3] + back1 * taps[2] + back2 * taps[1] + tail_block * taps[0]
+    return half_silu(total)
+
+
+def unblocked(block, k):
+    return pltpu.roll(block, (16 - 3 * k) % 16, 0)[:8]
+
+
+def edge_scales(scale_rows, group):
+    lanes = iota((128, WIDE), 1) // HEAD_DIM + group * HEADS_GROUP
+    matrix = (iota((128, WIDE), 0) % HEADS == lanes).astype(bf16)
+    return dot(scale_rows, matrix)
+
+
+def edge_state(values_rows, key_rows, scale, group):
+    rows = iota((8, WIDE), 0)
+    written = jnp.where(rows < KERNEL_EDGE, values_rows.astype(bf16).astype(f32) * scale, 0.0)
+    return dot(key_rows.astype(bf16), written.astype(bf16), ((0,), (0,)))
+
+
+def edge_keys(keys_rows, group):
+    tile = keys_rows[:, (group // 2) * 128 : (group // 2 + 1) * 128]
+    return tile[:, (group % 2) * STATE : (group % 2 + 1) * STATE]
+
+
+def combine_kernel(lengths_ref, own_ref, got_ref, weight_ref, bias_ref, sent_ref, edge_ref):
+    fresh = is_fresh(lengths_ref, lax.axis_index("ctx"))
+    goes_on = (1 - fresh).astype(f32)
+    weight = weight_ref[...].astype(f32) * 0.5
+    bias = bias_ref[...].astype(f32) * 0.5
+    tail_block = got_ref[TAIL_AT : TAIL_AT + 16, :].astype(f32)
+    head_block = own_ref[HEAD_AT : HEAD_AT + 16, :].astype(f32)
+    tail_block = jnp.where(fresh == 1, 0.0, tail_block)
+    block = edge_rows(tail_block, head_block, weight, bias)
+    chunks = [unblocked(block, k) for k in range(5)]
+    for k in range(5):
+        edge_ref[:, k * WIDE : (k + 1) * WIDE] = chunks[k]
+    sent_ref[STATE_ROWS:, :] = own_ref[TAIL_AT : TAIL_AT + 16, :]
+    scales = own_ref[SCALE_AT : SCALE_AT + 16, :128]
+    for group in range(BC_GROUPS):
+        at = slice(group * STATE, (group + 1) * STATE)
+        scale = edge_scales(scales, group)[:8]
+        extra = edge_state(chunks[group], edge_keys(chunks[4], group), scale * goes_on, group)
+        decay = scale[KERNEL_EDGE : KERNEL_EDGE + 1] * goes_on
+        total = own_ref[at, :].astype(f32) + extra + decay * got_ref[at, :].astype(f32)
+        sent_ref[at, :] = total.astype(bf16)
+
+
+def diagonal_kernel(
+    skip_ref, conv_ref, edge_ref, cumulative_ref, step_ref, diagonal_ref, queries_ref, entry_ref
+):
+    count = conv_ref.shape[0]
+    cumulative = cumulative_ref[...] * LOG2E
+    across = cumulative - jnp.log2(step_ref[0])
+    down = cumulative.T
+    entry_ref[...] = jnp.concatenate(halves(jnp.exp2(cumulative)), axis=0)
+    edge_row = iota((count, 128), 0) < KERNEL_EDGE
+    causal = iota((count, 128), 0) >= iota((count, 128), 1)
+    lane_head = iota((count, 128), 1) // HEAD_DIM
+
+    def tile_of(j):
+        cols = slice(j * 128, (j + 1) * 128)
+        rows = jnp.concatenate([edge_ref[:, cols], jnp.zeros((count - 8, 128), f32)], axis=0)
+        return jnp.where(edge_row, rows, conv_ref[:, cols].astype(f32))
+
+    keys = [tile_of(16 + i).astype(bf16) for i in range(2)]
+    queries = [tile_of(18 + i).astype(bf16) for i in range(2)]
+    for i in range(2):
+        queries_ref[:, i * 128 : (i + 1) * 128] = queries[i]
+    for group in range(BC_GROUPS):
+        part = slice((group % 2) * STATE, (group % 2 + 1) * STATE)
+        scores = dot(queries[group // 2][:, part], keys[group // 2][:, part], ((1,), (1,)))
+        for i in range(4):
+            j = group * 4 + i
+            values = tile_of(j)
+            weights, parts = [], []
+            gain = jnp.zeros((1, 128), f32)
+            for k in range(4):
+                head = 4 * j + k
+                gap = down[:, head : head + 1] - across[head : head + 1, :]
+                weights.append((jnp.exp2(jnp.where(causal, gap, -1e30)) * scores).astype(bf16))
+                parts.append(jnp.where(lane_head == k, values, 0.0).astype(bf16))
+                gain = jnp.where(lane_head[:1] == k, skip_ref[0, head], gain)
+            total = dot(jnp.concatenate(weights, axis=1), jnp.concatenate(parts, axis=0))
+            diagonal_ref[:, j * 128 : (j + 1) * 128] = total + gain * values
+
+
+def finish_kernel(
+    lengths_ref, first_ref, second_ref, weight_ref, bias_ref, diagonal_ref, queries_ref, entry_ref, out_ref
+):
+    position = lax.axis_index("ctx")
+    fresh = is_fresh(lengths_ref, position)
+    before_fresh = is_fresh(lengths_ref, position - 1)
+    goes_on = (1 - before_fresh).astype(f32)
+    weight = weight_ref[...].astype(f32) * 0.5
+    bias = bias_ref[...].astype(f32) * 0.5
+    tail_block = second_ref[STATE_ROWS:, :].astype(f32)
+    head_block = first_ref[HEAD_AT : HEAD_AT + 16, :].astype(f32)
+    block = edge_rows(tail_block, head_block, weight, bias)
+    chunks = [unblocked(block, k) for k in range(5)]
+    scales = first_ref[SCALE_AT : SCALE_AT + 16, :128]
+    matrix = spread_matrix()
+    for group in range(BC_GROUPS):
+        at = slice(group * STATE, (group + 1) * STATE)
+        cols = slice(group * WIDE, (group + 1) * WIDE)
+        scale = edge_scales(scales, group)[:8] * goes_on
+        extra = edge_state(chunks[group], edge_keys(chunks[4], group), scale, group)
+        decay = scale[KERNEL_EDGE : KERNEL_EDGE + 1]
+        total = first_ref[at, :].astype(f32) + extra + decay * second_ref[at, :].astype(f32)
+        incoming = jnp.where(fresh == 1, 0.0, total).astype(bf16)
+        low = (group % 2) * STATE
+        tile = queries_ref[:, (group // 2) * 128 : (group // 2 + 1) * 128]
+        carried = dot(tile[:, low : low + STATE], incoming)
+        rows = slice(group * HEADS_GROUP, (group + 1) * HEADS_GROUP)
+        low_rows = slice(HEADS + group * HEADS_GROUP, HEADS + (group + 1) * HEADS_GROUP)
+        entry = dot(
+            jnp.concatenate([entry_ref[rows, :], entry_ref[low_rows, :]], axis=0), matrix, ((0,), (0,))
+        )
+        out_ref[0, :, cols] = (diagonal_ref[:, cols] + entry * carried).astype(bf16)
+
+
+def call(kernel, outs, specs, flops, moved, *args):
+    return pl.pallas_call(
+        kernel,
+        out_shape=outs,
+        in_specs=specs,
+        out_specs=jax.tree.map(lambda _: VMEM, outs),
+        compiler_params=pltpu.CompilerParams(vmem_limit_bytes=24 * 1024 * 1024),
+        cost_estimate=pl.CostEstimate(flops=flops, bytes_accessed=moved, transcendentals=0),
+    )(*args)
+
+
+def shard_near(pre_conv, step_size, lengths, conv_weight, conv_bias, decay_rate, skip_gain):
+    count = pre_conv.shape[1]
+    size = lax.axis_size("ctx")
+    bias = conv_bias.reshape(-1, 128)
+    rate = decay_rate.reshape(1, -1)
+    skip = skip_gain.reshape(1, -1)
+    sds = jax.ShapeDtypeStruct
+    conv, cumulative, own = call(
+        state_kernel,
+        (
+            sds(pre_conv.shape[1:], bf16),
+            sds((HEADS, count), f32),
+            sds((FIRST_ROWS, WIDE), bf16),
+        ),
+        [SMEM, VMEM, VMEM, VMEM, VMEM, VMEM],
+        60_000_000,
+        2_000_000,
+        lengths,
+        pre_conv,
+        step_size,
+        conv_weight,
+        bias,
+        rate,
+    )
+    first = lax.ppermute(own, "ctx", [(i, (i + 1) % size) for i in range(size)])
+    sent, edge = call(
+        combine_kernel,
+        (sds((SECOND_ROWS, WIDE), bf16), sds((8, pre_conv.shape[2]), f32)),
+        [SMEM, VMEM, VMEM, VMEM, VMEM],
+        1_000_000,
+        1_000_000,
+        lengths,
+        own,
+        first,
+        conv_weight,
+        bias,
+    )
+    second = lax.ppermute(sent, "ctx", [(i, i + 2) for i in range(size - 2)])
+    diagonal, queries, entry = call(
+        diagonal_kernel,
+        (
+            sds((count, VALUES), f32),
+            sds((count, BC_GROUPS * STATE), bf16),
+            sds((2 * HEADS, count), bf16),
+        ),
+        [SMEM, VMEM, VMEM, VMEM, VMEM],
+        400_000_000,
+        4_000_000,
+        skip,
+        conv,
+        edge,
+        cumulative,
+        step_size,
+    )
+    return call(
+        finish_kernel,
+        sds((1, count, VALUES), bf16),
+        [SMEM] + [VMEM] * 7,
+        100_000_000,
+        2_000_000,
+        lengths,
+        first,
+        second,
+        conv_weight,
+        bias,
+        diagonal,
+        queries,
+        entry,
+    )
 
 
 def shifted(value, axis, steps):
@@ -82,7 +449,7 @@
     return (earlier[0] * later[0], later[0][:, None, None] * earlier[1] + later[1])
 
 
-def shards(pre_conv, step_size, lengths, conv_weight, conv_bias, decay_rate, skip_gain):
+def shard_far(pre_conv, step_size, lengths, conv_weight, conv_bias, decay_rate, skip_gain):
     count_rows = pre_conv.shape[1]
     kernel_len = conv_weight.shape[0]
     heads_group = HEADS // BC_GROUPS
@@ -151,4 +518,5 @@
         P(),
     )
     out_specs = P(("groups", "lane"), "ctx", None)
+    shards = shard_near if mesh.shape["ctx"] <= 8 else shard_far
     return jax.shard_map(shards, mesh=mesh, in_specs=in_specs, out_specs=out_specs, check_vma=False)

time: 122 us -> 31 us (0.25)
  waiting for transfers between devices: 51.8 us -> 12.7 us
  other arithmetic: 21.8 us -> 0 us
  blocking collectives: 18.7 us -> 0 us
  between operations: 14.2 us -> 0.05 us
  Pallas kernels: 0 us -> 8.66 us
  matrix products: 3.99 us -> 0 us
    all_gather x1 -> x0, waiting for transfers between devices: 51.7 us -> none  [carried_in(): lax.all_gather(part.astype(kind), axis)]
    all_gather x1 -> x0, blocking collectives: 18.7 us -> none  [carried_in(): lax.all_gather(part.astype(kind), axis)]
    ppermute x1 -> x2, waiting for transfers between devices: 0.01 us -> 12.7 us  [the longest x1 10.4 us: shard_near(): first = lax.ppermute(own, 'ctx', [(i, (i + 1) % size) for i in range(size)])]
    select_n x9 -> x0, other arithmetic: 11.5 us -> none  [the longest x8 10.9 us: step(): return jax.tree.map(lambda a, b: jnp.where(reached, a, b), new, before)]
    pallas_call x0 -> x4, Pallas kernels: none -> 8.66 us  [call(): pl.pallas_call(kernel, out_shape=outs, in_specs=specs, out_specs=jax.tree...]
    dot_general x16 -> x0, matrix products: 3.99 us -> none  [the longest x4 1.88 us: group_terms(): jnp.einsum('hts,shp->thp', weights, scaled, preferred_element_type=jnp.fl...]
    unnamed x8 -> x20, local copies, waits for them, and re-layouts: 1.42 us -> 4.59 us
    convert_element_type x10 -> x0, other arithmetic: 3.14 us -> none  [the longest x1 3.08 us: convolve(): return jax.nn.silu(total).astype(jnp.bfloat16)]
  transfers between devices with their start and end apart: 2 -> 2, of which waited for: 1 -> 2; matrix products, arithmetic and copies ran while one was open for 10% -> 0% of each run, Pallas kernels for 0% -> 7%
where the time goes in v1:
time: 31 us; the launch traced here: 30.6 us
  waiting for transfers between devices  12.7 us (41%)
  Pallas kernels  8.66 us (28%)
  local copies, waits for them, and re-layouts  4.59 us (15%)
  starting transfers between devices  4.59 us (15%)
    ppermute x1, waiting for transfers between devices, shard_near(): first = lax.ppermute(own, 'ctx', [(i, (i + 1) % size) for i in range(size)])  10.4 us
    pallas_call x4, Pallas kernels, call(): pl.pallas_call(kernel, out_shape=outs, in_specs=specs, out_specs=jax.tree...  8.66 us
    unnamed x20, local copies, waits for them, and re-layouts  4.59 us
    ppermute x1, starting transfers between devices, shard_near(): first = lax.ppermute(own, 'ctx', [(i, (i + 1) % size) for i in range(size)])  2.99 us
    ppermute x1, waiting for transfers between devices, shard_near(): second = lax.ppermute(sent, 'ctx', [(i, i + 2) for i in range(size - 2)])  2.35 us
    ppermute x1, starting transfers between devices, shard_near(): second = lax.ppermute(sent, 'ctx', [(i, i + 2) for i in range(size - 2)])  1.6 us
  transfers between devices with their start and end apart: 2, of which 2 were waited for; matrix products, arithmetic and copies ran while one was open for 0% of the time, Pallas kernels for 7%

profile of v1, /device:TPU:0, one launch (start us, length us, event | category | flops | bytes accessed | tf_op | source)
XLA Modules:
  0.0 30.6 jit_solution(11079613764925612382)
XLA Ops:
  0.0 0.0 copy-start.7
  0.0 0.0 copy-start.8
  0.0 0.7 %copy-done.7 = s32[1,4]{1,0:T(1,128)S(1)} copy-done((s32[1,4]{1,0:T(1,128)S(1)}, s32[1,4]{1,0:T(1,128)}, u32[]{:S(2)}) %copy-start.7) | copy-done | bytes 40
  0.7 0.0 copy-done.8
  0.7 0.0 copy-start
  0.7 1.1 %copy-done = bf16[1,128,2560]{2,1,0:T(8,128)(2,1)S(1)} copy-done((bf16[1,128,2560]{2,1,0:T(8,128)(2,1)S(1)}, bf16[1,128,2560]{2,1,0:T(8,128)(2,1)}, u32[]{:S(2)}) %copy-start) | copy-done | bytes 655384
  1.8 0.0 copy-start.1
  1.8 0.7 %copy-done.1 = bf16[4,2560]{1,0:T(4,128)(2,1)S(1)} copy-done((bf16[4,2560]{1,0:T(4,128)(2,1)S(1)}, bf16[4,2560]{1,0:T(4,128)(2,1)}, u32[]{:S(2)}) %copy-start.1) | copy-done | bytes 20504
  2.5 0.0 copy-start.3
  2.5 0.7 %copy-done.3 = bf16[2560]{0:T(1024)(128)(2,1)S(1)} copy-done((bf16[2560]{0:T(1024)(128)(2,1)S(1)}, bf16[2560]{0:T(1024)(128)(2,1)}, u32[]{:S(2)}) %copy-start.3) | copy-done | bytes 5144
  3.2 0.0 copy-start.5
  3.2 0.8 %copy-done.5 = f32[1,64,128]{2,1,0:T(8,128)S(1)} copy-done((f32[1,64,128]{2,1,0:T(8,128)S(1)}, f32[1,64,128]{2,1,0:T(8,128)}, u32[]{:S(2)}) %copy-start.5) | copy-done | bytes 32792
  3.9 0.0 copy-start.2
  3.9 0.0 copy-start.4
  3.9 2.2 %shard_map.73 = (bf16[128,2560]{1,0:T(8,128)(2,1)S(1)}, f32[64,128]{1,0:T(8,128)S(1)}, bf16[304,512]{1,0:T(8,128)(2,1)S(1)}) custom-call(s32[1,4]{1,0:T(1,128)S(1)} %copy-done.7, bf16[1,128,2560]{2,1,0:T(8,128)(2,1)S(1)} %copy-done, f32[1,64,128]{2,1,0:T(8,128)S(1)} %copy-done.5, bf16[4,2560]{1,0:T(4,128)(2,1)S(1)} %copy-done.1, ...), custom_call_target="tpu_custom_call" | custom-call | flops 60000000 | bytes 2000000 | tf_op jit(solution)/shard_map/pallas_call | solution.py:298
  6.2 0.0 copy-start.6
  6.2 3.0 %collective-permute-start = (bf16[304,512]{1,0:T(8,128)(2,1)S(1)}, bf16[304,512]{1,0:T(8,128)(2,1)S(1)}, u32[]{:S(2)}, u32[]{:S(2)}) collective-permute-start(bf16[304,512]{1,0:T(8,128)(2,1)S(1)} %get-tuple-element.13.own_ref), channel_id=1, source_target_pairs={{0,2},{2,4},{4,6},{6,8},{8,10},{10,12},{12,14},{14,0},{1,3},{3,5},... | collective-permute-start | bytes 933896 | tf_op jit(solution)/shard_map/ppermute | solution.py:332
  9.2 10.4 %collective-permute-done.got_ref.first_ref = bf16[304,512]{1,0:T(8,128)(2,1)S(1)} collective-permute-done((bf16[304,512]{1,0:T(8,128)(2,1)S(1)}, bf16[304,512]{1,0:T(8,128)(2,1)S(1)}, u32[]{:S(2)}, u32[]{:S(2)}) %collective-permute-start) | collective-permute-done | bytes 311328 | tf_op jit(solution)/shard_map/ppermute | solution.py:332
  19.6 0.0 copy-done.2
  19.6 0.0 copy-done.4
  19.6 1.3 %shard_map.74 = (bf16[272,512]{1,0:T(8,128)(2,1)S(1)}, f32[8,2560]{1,0:T(8,128)S(1)}) custom-call(s32[1,4]{1,0:T(1,128)S(1)} %copy-done.7, bf16[304,512]{1,0:T(8,128)(2,1)S(1)} %get-tuple-element.13.own_ref, bf16[304,512]{1,0:T(8,128)(2,1)S(1)} %collective-permute-done.got_ref.first_ref, bf16[4,2560]{1,0:T(4,128)(2,1)S(1)} %copy-done.2, ...), custom_call_target="tpu_custom_call" | custom-call | flops 1000000 | bytes 1000000 | tf_op jit(solution)/shard_map/pallas_call | solution.py:298
  20.9 1.6 %collective-permute-start.1 = (bf16[272,512]{1,0:T(8,128)(2,1)S(1)}, bf16[272,512]{1,0:T(8,128)(2,1)S(1)}, u32[]{:S(2)}, u32[]{:S(2)}) collective-permute-start(bf16[272,512]{1,0:T(8,128)(2,1)S(1)} %get-tuple-element.14), channel_id=1, source_target_pairs={{0,4},{2,6},{4,8},{6,10},{8,12},{10,14},{1,5},{3,7},{5,9},{7,11},{... | collective-permute-start | bytes 835592 | tf_op jit(solution)/shard_map/ppermute | solution.py:345
  22.5 0.0 copy-start.9
  22.5 0.0 copy-done.6
  22.5 0.6 %copy-done.9 = f32[64]{0:T(128)S(1)} copy-done((f32[64]{0:T(128)S(1)}, f32[64]{0:T(128)}, u32[]{:S(2)}) %copy-start.9) | copy-done | bytes 280
  23.1 2.3 %shard_map.75 = (f32[128,2048]{1,0:T(8,128)S(1)}, bf16[128,256]{1,0:T(8,128)(2,1)S(1)}, bf16[128,128]{1,0:T(8,128)(2,1)S(1)}) custom-call(f32[1,64]{1,0:T(1,128)S(1)} %bitcast.7, bf16[128,2560]{1,0:T(8,128)(2,1)S(1)} %get-tuple-element.15.conv_ref, f32[8,2560]{1,0:T(8,128)S(1)} %get-tuple-element.16.edge_ref, ...), custom_call_target="tpu_custom_call" | custom-call | flops 400000000 | bytes 4000000 | tf_op jit(solution)/shard_map/pallas_call | solution.py:298
  25.4 2.4 %collective-permute-done.1.second_ref = bf16[272,512]{1,0:T(8,128)(2,1)S(1)} collective-permute-done((bf16[272,512]{1,0:T(8,128)(2,1)S(1)}, bf16[272,512]{1,0:T(8,128)(2,1)S(1)}, u32[]{:S(2)}, u32[]{:S(2)}) %collective-permute-start.1) | collective-permute-done | bytes 278560 | tf_op jit(solution)/shard_map/ppermute | solution.py:345
  27.8 2.9 %shard_map.76 = bf16[1,128,2048]{2,1,0:T(8,128)(2,1)} custom-call(s32[1,4]{1,0:T(1,128)S(1)} %copy-done.7, bf16[304,512]{1,0:T(8,128)(2,1)S(1)} %collective-permute-done.got_ref.first_ref, bf16[272,512]{1,0:T(8,128)(2,1)S(1)} %collective-permute-done.1.second_ref, bf16[4,2560]{1,0:T(4,128)(2,1)S(1)} %copy-done.2, bf16[20,128]{1,0:T(8,128)(2,1)S(1)} %bitcast.5, ...), custom_call_target="tpu_custom_call" | custom-call | flops 100000000 | bytes 2000000 | tf_op jit(solution)/shard_map/pallas_call | solution.py:298
Async XLA Ops:
  0.0 0.7 %copy-start.7 = (s32[1,4]{1,0:T(1,128)S(1)}, s32[1,4]{1,0:T(1,128)}, u32[]{:S(2)}) copy-start(s32[1,4]{1,0:T(1,128)} %lengths_ref.5) | copy-start | bytes 52
  0.0 0.7 %copy-start.8 = (f32[64]{0:T(128)S(1)}, f32[64]{0:T(128)}, u32[]{:S(2)}) copy-start(f32[64]{0:T(128)} %param.12) | copy-start | bytes 772
  0.7 1.1 %copy-start = (bf16[1,128,2560]{2,1,0:T(8,128)(2,1)S(1)}, bf16[1,128,2560]{2,1,0:T(8,128)(2,1)}, u32[]{:S(2)}) copy-start(bf16[1,128,2560]{2,1,0:T(8,128)(2,1)} %x_ref.1) | copy-start | bytes 1966084
  1.8 0.7 %copy-start.1 = (bf16[4,2560]{1,0:T(4,128)(2,1)S(1)}, bf16[4,2560]{1,0:T(4,128)(2,1)}, u32[]{:S(2)}) copy-start(bf16[4,2560]{1,0:T(4,128)(2,1)} %weight_ref.5) | copy-start | bytes 61444
  2.5 0.7 %copy-start.3 = (bf16[2560]{0:T(1024)(128)(2,1)S(1)}, bf16[2560]{0:T(1024)(128)(2,1)}, u32[]{:S(2)}) copy-start(bf16[2560]{0:T(1024)(128)(2,1)} %param.11) | copy-start | bytes 15364
  3.2 0.8 %copy-start.5 = (f32[1,64,128]{2,1,0:T(8,128)S(1)}, f32[1,64,128]{2,1,0:T(8,128)}, u32[]{:S(2)}) copy-start(f32[1,64,128]{2,1,0:T(8,128)} %step_ref.3) | copy-start | bytes 98308
  3.9 15.7 %copy-start.2 = (bf16[4,2560]{1,0:T(4,128)(2,1)S(1)}, bf16[4,2560]{1,0:T(4,128)(2,1)}, u32[]{:S(2)}) copy-start(bf16[4,2560]{1,0:T(4,128)(2,1)} %weight_ref.5) | copy-start | bytes 61444
  3.9 15.7 %copy-start.4 = (bf16[2560]{0:T(1024)(128)(2,1)S(1)}, bf16[2560]{0:T(1024)(128)(2,1)}, u32[]{:S(2)}) copy-start(bf16[2560]{0:T(1024)(128)(2,1)} %param.11) | copy-start | bytes 15364
  6.2 16.3 %copy-start.6 = (f32[1,64,128]{2,1,0:T(8,128)S(1)}, f32[1,64,128]{2,1,0:T(8,128)}, u32[]{:S(2)}) copy-start(f32[1,64,128]{2,1,0:T(8,128)} %step_ref.3) | copy-start | bytes 98308
  6.2 13.4 %collective-permute-start = (bf16[304,512]{1,0:T(8,128)(2,1)S(1)}, bf16[304,512]{1,0:T(8,128)(2,1)S(1)}, u32[]{:S(2)}, u32[]{:S(2)}) collective-permute-start(bf16[304,512]{1,0:T(8,128)(2,1)S(1)} %get-tuple-element.13.own_ref), channel_id=1, source_target_pairs={{0,2},{2,4},{4,6},{6,8},{8,10},{10,12},{12,14},{14,0},{1,3},{3,5},... | collective-permute-start | bytes 933896 | tf_op jit(solution)/shard_map/ppermute | solution.py:332
  20.9 6.9 %collective-permute-start.1 = (bf16[272,512]{1,0:T(8,128)(2,1)S(1)}, bf16[272,512]{1,0:T(8,128)(2,1)S(1)}, u32[]{:S(2)}, u32[]{:S(2)}) collective-permute-start(bf16[272,512]{1,0:T(8,128)(2,1)S(1)} %get-tuple-element.14), channel_id=1, source_target_pairs={{0,4},{2,6},{4,8},{6,10},{8,12},{10,14},{1,5},{3,7},{5,9},{7,11},{... | collective-permute-start | bytes 835592 | tf_op jit(solution)/shard_map/ppermute | solution.py:345
  22.5 0.7 %copy-start.9 = (f32[64]{0:T(128)S(1)}, f32[64]{0:T(128)}, u32[]{:S(2)}) copy-start(f32[64]{0:T(128)} %param.13) | copy-start | bytes 772

commit v2 on v1

--- a/solution.py
+++ b/solution.py
@@ -7,6 +7,7 @@
 
 HEADS = 64
 HEAD_DIM = 32
+EDGE = 3
 STATE = 64
 BC_GROUPS = 4
 HEADS_GROUP = HEADS // BC_GROUPS
@@ -20,6 +21,7 @@
 SECOND_ROWS = STATE_ROWS + 16
 LOG2E = 1.4426950408889634
 VMEM = pl.BlockSpec(memory_space=pltpu.VMEM)
+HBM = pl.BlockSpec(memory_space=pltpu.HBM)
 SMEM = pl.BlockSpec(memory_space=pltpu.SMEM)
 f32 = jnp.float32
 bf16 = jnp.bfloat16
@@ -76,33 +78,62 @@
     top = jnp.zeros((8, WIDE), f32)
     low = jnp.zeros((8, WIDE), f32)
     for k in range(strip.shape[1] // WIDE):
-        chunk = strip[:, k * WIDE : (k + 1) * WIDE]
-        moved = pltpu.roll(chunk, (3 * k - first) % 8, 0)
-        for base, at in ((0, "top"), (8, "low")):
-            low_row, high_row = 3 * k - base, 3 * k + 2 - base
-            if high_row < 0 or low_row > 7:
-                continue
-            mask = (rows >= low_row) & (rows <= high_row)
-            if at == "top":
-                top = jnp.where(mask, moved, top)
-            else:
-                low = jnp.where(mask, moved, low)
+        moved = pltpu.roll(strip[:, k * WIDE : (k + 1) * WIDE], (3 * k - first) % 8, 0)
+        if 3 * k < 8:
+            top = jnp.where((rows >= 3 * k) & (rows < 3 * k + 3), moved, top)
+        if 3 * k + 2 >= 8:
+            low = jnp.where((rows >= 3 * k - 8) & (rows < 3 * k - 5), moved, low)
     return jnp.concatenate([top, low], axis=0)
 
 
+def conv_rows(x, weight, bias):
+    padded = jnp.concatenate([jnp.zeros((8, x.shape[1]), f32), x], axis=0)
+    total = bias + x * weight[3:4]
+    for back in range(1, 4):
+        total = total + padded[8 - back : 8 - back + x.shape[0]] * weight[3 - back : 4 - back]
+    return half_silu(total)
+
+
 def state_kernel(
-    lengths_ref, x_ref, step_ref, weight_ref, bias_ref, rate_ref, conv_ref, cumulative_ref, sent_ref
+    lengths_hbm, x_hbm, step_hbm, weight_hbm, bias_hbm, rate_hbm,
+    conv_ref, cumulative_ref, sent_ref,
+    lengths_ref, x_ref, step_ref, weight_ref, bias_ref, rate_ref, sems,
 ):
+    order = (4, 0, 1, 2, 3)
+    small = [
+        pltpu.make_async_copy(source, target, sems.at[i])
+        for i, (source, target) in enumerate(
+            (
+                (step_hbm.at[0], step_ref),
+                (rate_hbm, rate_ref),
+                (lengths_hbm, lengths_ref),
+                (weight_hbm, weight_ref),
+                (bias_hbm, bias_ref),
+            )
+        )
+    ]
+    large = [
+        pltpu.make_async_copy(
+            x_hbm.at[0, :, pl.ds(k * WIDE, WIDE)], x_ref.at[:, pl.ds(k * WIDE, WIDE)], sems.at[5 + k]
+        )
+        for k in range(5)
+    ]
+    for copy in small:
+        copy.start()
+    for k in order:
+        large[k].start()
+    count = x_ref.shape[0]
+    for copy in small:
+        copy.wait()
     fresh = is_fresh(lengths_ref, lax.axis_index("ctx"))
-    count = x_ref.shape[1]
-    step = step_ref[0]
+    step = step_ref[...]
     cumulative = cumulative_of(step, rate_ref[...])
     cumulative_ref[...] = cumulative
     last = cumulative[:, count - 1 :]
     tail = step * jnp.exp(last - cumulative)
     lanes = iota((HEADS, count), 1)
-    kept = jnp.where((lanes >= KERNEL_EDGE) | (fresh == 1), tail, 0.0)
-    scales = jnp.where(lanes == KERNEL_EDGE, jnp.exp(last), tail)
+    kept = jnp.where((lanes >= EDGE) | (fresh == 1), tail, 0.0)
+    scales = jnp.where(lanes == EDGE, jnp.exp(last), tail)
     high, low = halves(scales)
     place = iota((HEADS, 128), 1) - iota((HEADS, 128), 0)
     picked = dot(high, (place == 0).astype(bf16), ((0,), (0,)))
@@ -110,8 +141,6 @@
     sent_ref[SCALE_AT : SCALE_AT + 16, :] = jnp.concatenate(
         [picked[:16], jnp.zeros((16, WIDE - 128), f32)], axis=1
     ).astype(bf16)
-    sent_ref[TAIL_AT : TAIL_AT + 16, :] = to_rows(x_ref[0, count - 16 :, :].astype(f32)[8:], 5).astype(bf16)
-    sent_ref[HEAD_AT : HEAD_AT + 16, :] = to_rows(x_ref[0, :16, :].astype(f32)[:8], 0).astype(bf16)
 
     matrix = spread_matrix()
     weight = weight_ref[...].astype(f32) * 0.5
@@ -119,21 +148,17 @@
 
     def conv_tile(j):
         cols = slice(j * 128, (j + 1) * 128)
-        x = x_ref[0, :, cols].astype(f32)
-        padded = jnp.concatenate([jnp.zeros((8, 128), f32), x], axis=0)
-        total = bias[j : j + 1, :] + x * weight[3:4, cols]
-        for back in range(1, 4):
-            total = total + padded[8 - back : 8 - back + count] * weight[3 - back : 4 - back, cols]
-        return half_silu(total)
-
-    tiles = CONV_TILES
+        return conv_rows(x_ref[:, cols].astype(f32), weight[:, cols], bias[j : j + 1, :])
+
     keys = []
-    for j in range(tiles - 4, tiles):
+    large[4].wait()
+    for j in (16, 17):
         tile = conv_tile(j).astype(bf16)
         conv_ref[:, j * 128 : (j + 1) * 128] = tile
         keys.append(tile)
     for group in range(BC_GROUPS):
         scale = spread(kept, group, matrix)
+        large[group].wait()
         parts = []
         for i in range(WIDE // 128):
             j = group * (WIDE // 128) + i
@@ -144,13 +169,48 @@
         key = keys[group // 2][:, (group % 2) * STATE : (group % 2 + 1) * STATE]
         local = dot(key, written, ((0,), (0,)))
         sent_ref[group * STATE : (group + 1) * STATE, :] = local.astype(bf16)
-
-
-KERNEL_EDGE = 3
-CONV_TILES = 20
-
-
-def edge_rows(tail_block, head_block, weight, bias):
+    sent_ref[TAIL_AT : TAIL_AT + 16, :] = to_rows(x_ref[count - 16 :, :].astype(f32)[8:], 5).astype(bf16)
+    sent_ref[HEAD_AT : HEAD_AT + 16, :] = to_rows(x_ref[:16, :].astype(f32)[:8], 0).astype(bf16)
+
+
+def known_part(head_block, table_ref):
+    return (
+        table_ref[0]
+        + head_block * table_ref[1]
+        + pltpu.roll(head_block, 1, 0) * table_ref[2]
+        + pltpu.roll(head_block, 2, 0) * table_ref[3]
+    )
+
+
+def edge_rows(tail_block, known, table_ref):
+    block = half_silu(
+        known
+        + tail_block * table_ref[4]
+        + pltpu.roll(tail_block, 15, 0) * table_ref[5]
+        + pltpu.roll(tail_block, 14, 0) * table_ref[6]
+    )
+    return [pltpu.roll(block, (16 - 3 * k) % 16, 0)[:8] for k in range(5)]
+
+
+def edge_scales(scale_rows):
+    lanes = iota((128, VALUES), 1) // HEAD_DIM
+    matrix = (iota((128, VALUES), 0) % HEADS == lanes).astype(bf16)
+    return dot(scale_rows, matrix)[:8]
+
+
+def prepare_kernel(
+    lengths_ref, x_hbm, own_ref, weight_ref, bias_ref, cumulative_ref, step_ref, skip_ref,
+    queries_ref, table_ref, known_ref, scale_ref, across_ref, down_ref, entry_ref, gain_ref, x_ref, sem,
+):
+    count = x_ref.shape[0]
+    first = VALUES + BC_GROUPS * STATE
+    copy = pltpu.make_async_copy(x_hbm.at[0, :, pl.ds(first, BC_GROUPS * STATE)], x_ref, sem)
+    copy.start()
+    position = lax.axis_index("ctx")
+    goes_on = (1 - is_fresh(lengths_ref, position)).astype(f32)
+    went_on = (1 - is_fresh(lengths_ref, position - 1)).astype(f32)
+    weight = weight_ref[...].astype(f32) * 0.5
+    bias = bias_ref[...].astype(f32) * 0.5
     rows = iota((16, WIDE), 0)
     third = rows % 3
     chunk = rows // 3
@@ -165,81 +225,85 @@
         blocked([weight[tap : tap + 1, k * WIDE : (k + 1) * WIDE] for k in range(5)])
         for tap in range(4)
     ]
-    offset = blocked(
+    table_ref[0] = blocked(
         [
             jnp.concatenate([bias[4 * k + i : 4 * k + i + 1, :] for i in range(4)], axis=1)
             for k in range(5)
         ]
     )
-    back1 = jnp.where(third == 0, pltpu.roll(tail_block, 14, 0), pltpu.roll(head_block, 1, 0))
-    back2 = jnp.where(third == 2, pltpu.roll(head_block, 2, 0), pltpu.roll(tail_block, 15, 0))
-    total = offset + head_block * taps[3] + back1 * taps[2] + back2 * taps[1] + tail_block * taps[0]
-    return half_silu(total)
-
-
-def unblocked(block, k):
-    return pltpu.roll(block, (16 - 3 * k) % 16, 0)[:8]
-
-
-def edge_scales(scale_rows, group):
-    lanes = iota((128, WIDE), 1) // HEAD_DIM + group * HEADS_GROUP
-    matrix = (iota((128, WIDE), 0) % HEADS == lanes).astype(bf16)
-    return dot(scale_rows, matrix)
-
-
-def edge_state(values_rows, key_rows, scale, group):
+    table_ref[1] = taps[3]
+    table_ref[2] = jnp.where(third == 0, 0.0, taps[2])
+    table_ref[3] = jnp.where(third == 2, taps[1], 0.0)
+    table_ref[4] = taps[0]
+    table_ref[5] = jnp.where(third == 2, 0.0, taps[1])
+    table_ref[6] = jnp.where(third == 0, taps[2], 0.0)
+    known_ref[:16, :] = known_part(own_ref[HEAD_AT : HEAD_AT + 16, :].astype(f32), table_ref)
+    known_ref[16:, :] = jnp.where(iota((8, WIDE), 0) == 0, goes_on, goes_on * went_on)
+    scale_ref[...] = edge_scales(own_ref[SCALE_AT : SCALE_AT + 16, :128]) * goes_on
+    cumulative = cumulative_ref[...] * LOG2E
+    across_ref[...] = cumulative - jnp.log2(step_ref[0])
+    down_ref[...] = cumulative.T
+    matrix = spread_matrix()
+    entry = jnp.exp2(cumulative)
+    for group in range(BC_GROUPS):
+        entry_ref[:, group * WIDE : (group + 1) * WIDE] = spread(entry, group, matrix)
+    gain = jnp.concatenate(halves(skip_ref[...] + jnp.zeros((16, HEADS), f32)), axis=1)
+    gain_ref[...] = edge_scales(gain)
+    copy.wait()
+    for i in range(2):
+        cols = slice(first + i * 128, first + (i + 1) * 128)
+        j = first // 128 + i
+        tile = conv_rows(
+            x_ref[:, i * 128 : (i + 1) * 128].astype(f32), weight[:, cols], bias[j : j + 1, :]
+        )
+        queries_ref[:, i * 128 : (i + 1) * 128] = tile.astype(bf16)
+
+
+def edge_state(values_rows, keys_rows, scale, group):
     rows = iota((8, WIDE), 0)
-    written = jnp.where(rows < KERNEL_EDGE, values_rows.astype(bf16).astype(f32) * scale, 0.0)
-    return dot(key_rows.astype(bf16), written.astype(bf16), ((0,), (0,)))
-
-
-def edge_keys(keys_rows, group):
-    tile = keys_rows[:, (group // 2) * 128 : (group // 2 + 1) * 128]
-    return tile[:, (group % 2) * STATE : (group % 2 + 1) * STATE]
-
-
-def combine_kernel(lengths_ref, own_ref, got_ref, weight_ref, bias_ref, sent_ref, edge_ref):
-    fresh = is_fresh(lengths_ref, lax.axis_index("ctx"))
-    goes_on = (1 - fresh).astype(f32)
-    weight = weight_ref[...].astype(f32) * 0.5
-    bias = bias_ref[...].astype(f32) * 0.5
-    tail_block = got_ref[TAIL_AT : TAIL_AT + 16, :].astype(f32)
-    head_block = own_ref[HEAD_AT : HEAD_AT + 16, :].astype(f32)
-    tail_block = jnp.where(fresh == 1, 0.0, tail_block)
-    block = edge_rows(tail_block, head_block, weight, bias)
-    chunks = [unblocked(block, k) for k in range(5)]
+    written = jnp.where(rows < EDGE, values_rows * scale, 0.0)
+    tile = keys_rows[:, (group // 2) * 128 : (group // 2 + 1) * 128].astype(bf16)
+    return dot(tile[:, (group % 2) * STATE : (group % 2 + 1) * STATE], written.astype(bf16), ((0,), (0,)))
+
+
+def combine_kernel(own_ref, got_ref, table_ref, known_ref, scale_ref, sent_ref, edge_ref):
+    tail_block = got_ref[TAIL_AT : TAIL_AT + 16, :].astype(f32) * known_ref[16:17, :]
+    chunks = edge_rows(tail_block, known_ref[:16, :], table_ref)
     for k in range(5):
         edge_ref[:, k * WIDE : (k + 1) * WIDE] = chunks[k]
     sent_ref[STATE_ROWS:, :] = own_ref[TAIL_AT : TAIL_AT + 16, :]
-    scales = own_ref[SCALE_AT : SCALE_AT + 16, :128]
     for group in range(BC_GROUPS):
         at = slice(group * STATE, (group + 1) * STATE)
-        scale = edge_scales(scales, group)[:8]
-        extra = edge_state(chunks[group], edge_keys(chunks[4], group), scale * goes_on, group)
-        decay = scale[KERNEL_EDGE : KERNEL_EDGE + 1] * goes_on
-        total = own_ref[at, :].astype(f32) + extra + decay * got_ref[at, :].astype(f32)
+        scale = scale_ref[:, group * WIDE : (group + 1) * WIDE]
+        extra = edge_state(chunks[group], chunks[4], scale, group)
+        total = own_ref[at, :].astype(f32) + extra + scale[EDGE : EDGE + 1] * got_ref[at, :].astype(f32)
         sent_ref[at, :] = total.astype(bf16)
 
 
 def diagonal_kernel(
-    skip_ref, conv_ref, edge_ref, cumulative_ref, step_ref, diagonal_ref, queries_ref, entry_ref
+    conv_ref, raw_queries_ref, edge_ref, across_ref, down_ref, gain_ref, got_ref, table_ref, gates_ref,
+    diagonal_ref, queries_ref, known_ref, scale_ref,
 ):
+    known_ref[:16, :] = known_part(got_ref[HEAD_AT : HEAD_AT + 16, :].astype(f32), table_ref)
+    known_ref[16:, :] = gates_ref[16:, :]
+    both = gates_ref[17:18, :1]
+    scale_ref[...] = edge_scales(got_ref[SCALE_AT : SCALE_AT + 16, :128]) * both
+
     count = conv_ref.shape[0]
-    cumulative = cumulative_ref[...] * LOG2E
-    across = cumulative - jnp.log2(step_ref[0])
-    down = cumulative.T
-    entry_ref[...] = jnp.concatenate(halves(jnp.exp2(cumulative)), axis=0)
-    edge_row = iota((count, 128), 0) < KERNEL_EDGE
+    edge_row = iota((count, 128), 0) < EDGE
     causal = iota((count, 128), 0) >= iota((count, 128), 1)
     lane_head = iota((count, 128), 1) // HEAD_DIM
 
-    def tile_of(j):
-        cols = slice(j * 128, (j + 1) * 128)
-        rows = jnp.concatenate([edge_ref[:, cols], jnp.zeros((count - 8, 128), f32)], axis=0)
-        return jnp.where(edge_row, rows, conv_ref[:, cols].astype(f32))
-
-    keys = [tile_of(16 + i).astype(bf16) for i in range(2)]
-    queries = [tile_of(18 + i).astype(bf16) for i in range(2)]
+    def patched(tile, j):
+        rows = jnp.concatenate(
+            [edge_ref[:, j * 128 : (j + 1) * 128], jnp.zeros((count - 8, 128), f32)], axis=0
+        )
+        return jnp.where(edge_row, rows, tile.astype(f32))
+
+    keys = [patched(conv_ref[:, (16 + i) * 128 : (17 + i) * 128], 16 + i).astype(bf16) for i in range(2)]
+    queries = [
+        patched(raw_queries_ref[:, i * 128 : (i + 1) * 128], 18 + i).astype(bf16) for i in range(2)
+    ]
     for i in range(2):
         queries_ref[:, i * 128 : (i + 1) * 128] = queries[i]
     for group in range(BC_GROUPS):
@@ -247,132 +311,142 @@
         scores = dot(queries[group // 2][:, part], keys[group // 2][:, part], ((1,), (1,)))
         for i in range(4):
             j = group * 4 + i
-            values = tile_of(j)
+            cols = slice(j * 128, (j + 1) * 128)
+            values = patched(conv_ref[:, cols], j)
             weights, parts = [], []
-            gain = jnp.zeros((1, 128), f32)
             for k in range(4):
-                head = 4 * j + k
-                gap = down[:, head : head + 1] - across[head : head + 1, :]
+                at = 4 * j + k
+                gap = down_ref[:, at : at + 1] - across_ref[at : at + 1, :]
                 weights.append((jnp.exp2(jnp.where(causal, gap, -1e30)) * scores).astype(bf16))
                 parts.append(jnp.where(lane_head == k, values, 0.0).astype(bf16))
-                gain = jnp.where(lane_head[:1] == k, skip_ref[0, head], gain)
             total = dot(jnp.concatenate(weights, axis=1), jnp.concatenate(parts, axis=0))
-            diagonal_ref[:, j * 128 : (j + 1) * 128] = total + gain * values
+            diagonal_ref[:, cols] = total + gain_ref[:1, cols] * values
 
 
 def finish_kernel(
-    lengths_ref, first_ref, second_ref, weight_ref, bias_ref, diagonal_ref, queries_ref, entry_ref, out_ref
+    first_ref, second_ref, table_ref, known_ref, scale_ref, diagonal_ref, queries_ref, entry_ref, out_hbm, out_ref, sems
 ):
-    position = lax.axis_index("ctx")
-    fresh = is_fresh(lengths_ref, position)
-    before_fresh = is_fresh(lengths_ref, position - 1)
-    goes_on = (1 - before_fresh).astype(f32)
-    weight = weight_ref[...].astype(f32) * 0.5
-    bias = bias_ref[...].astype(f32) * 0.5
     tail_block = second_ref[STATE_ROWS:, :].astype(f32)
-    head_block = first_ref[HEAD_AT : HEAD_AT + 16, :].astype(f32)
-    block = edge_rows(tail_block, head_block, weight, bias)
-    chunks = [unblocked(block, k) for k in range(5)]
-    scales = first_ref[SCALE_AT : SCALE_AT + 16, :128]
-    matrix = spread_matrix()
+    chunks = edge_rows(tail_block, known_ref[:16, :], table_ref)
+    kept = known_ref[16:17, :]
+    copies = []
     for group in range(BC_GROUPS):
         at = slice(group * STATE, (group + 1) * STATE)
         cols = slice(group * WIDE, (group + 1) * WIDE)
-        scale = edge_scales(scales, group)[:8] * goes_on
-        extra = edge_state(chunks[group], edge_keys(chunks[4], group), scale, group)
-        decay = scale[KERNEL_EDGE : KERNEL_EDGE + 1]
-        total = first_ref[at, :].astype(f32) + extra + decay * second_ref[at, :].astype(f32)
-        incoming = jnp.where(fresh == 1, 0.0, total).astype(bf16)
+        scale = scale_ref[:, cols]
+        extra = edge_state(chunks[group], chunks[4], scale, group)
+        total = first_ref[at, :].astype(f32) * kept + extra
+        total = total + scale[EDGE : EDGE + 1] * second_ref[at, :].astype(f32)
         low = (group % 2) * STATE
         tile = queries_ref[:, (group // 2) * 128 : (group // 2 + 1) * 128]
-        carried = dot(tile[:, low : low + STATE], incoming)
-        rows = slice(group * HEADS_GROUP, (group + 1) * HEADS_GROUP)
-        low_rows = slice(HEADS + group * HEADS_GROUP, HEADS + (group + 1) * HEADS_GROUP)
-        entry = dot(
-            jnp.concatenate([entry_ref[rows, :], entry_ref[low_rows, :]], axis=0), matrix, ((0,), (0,))
-        )
-        out_ref[0, :, cols] = (diagonal_ref[:, cols] + entry * carried).astype(bf16)
-
-
-def call(kernel, outs, specs, flops, moved, *args):
+        carried = dot(tile[:, low : low + STATE], total.astype(bf16))
+        out_ref[:, cols] = (diagonal_ref[:, cols] + entry_ref[:, cols] * carried).astype(bf16)
+        copy = pltpu.make_async_copy(
+            out_ref.at[:, pl.ds(group * WIDE, WIDE)],
+            out_hbm.at[0, :, pl.ds(group * WIDE, WIDE)],
+            sems.at[group],
+        )
+        copy.start()
+        copies.append(copy)
+    for copy in copies:
+        copy.wait()
+
+
+def call(kernel, outs, in_specs, cost, args, out_specs=None, scratch=()):
     return pl.pallas_call(
         kernel,
         out_shape=outs,
-        in_specs=specs,
-        out_specs=jax.tree.map(lambda _: VMEM, outs),
+        in_specs=in_specs,
+        out_specs=out_specs or jax.tree.map(lambda _: VMEM, outs),
+        scratch_shapes=scratch,
         compiler_params=pltpu.CompilerParams(vmem_limit_bytes=24 * 1024 * 1024),
-        cost_estimate=pl.CostEstimate(flops=flops, bytes_accessed=moved, transcendentals=0),
+        cost_estimate=pl.CostEstimate(flops=cost[0], bytes_accessed=cost[1], transcendentals=0),
     )(*args)
 
 
 def shard_near(pre_conv, step_size, lengths, conv_weight, conv_bias, decay_rate, skip_gain):
-    count = pre_conv.shape[1]
+    count, channels = pre_conv.shape[1:]
     size = lax.axis_size("ctx")
-    bias = conv_bias.reshape(-1, 128)
-    rate = decay_rate.reshape(1, -1)
-    skip = skip_gain.reshape(1, -1)
+    lengths, pre_conv, step_size, weight, bias, rate, skip = (
+        pltpu.with_memory_space_constraint(array, pltpu.HBM)
+        for array in (
+            lengths,
+            pre_conv,
+            step_size,
+            conv_weight,
+            conv_bias.reshape(-1, 128),
+            decay_rate.reshape(1, -1),
+            skip_gain.reshape(1, -1),
+        )
+    )
     sds = jax.ShapeDtypeStruct
+    grouped = BC_GROUPS * STATE
     conv, cumulative, own = call(
         state_kernel,
         (
-            sds(pre_conv.shape[1:], bf16),
+            sds((count, channels - grouped), bf16),
             sds((HEADS, count), f32),
             sds((FIRST_ROWS, WIDE), bf16),
         ),
-        [SMEM, VMEM, VMEM, VMEM, VMEM, VMEM],
-        60_000_000,
-        2_000_000,
-        lengths,
-        pre_conv,
-        step_size,
-        conv_weight,
-        bias,
-        rate,
+        [HBM] * 6,
+        (60_000_000, 2_000_000),
+        (lengths, pre_conv, step_size, weight, bias, rate),
+        scratch=(
+            pltpu.SMEM(lengths.shape, jnp.int32),
+            pltpu.VMEM((count, channels), bf16),
+            pltpu.VMEM((HEADS, count), f32),
+            pltpu.VMEM(weight.shape, bf16),
+            pltpu.VMEM(bias.shape, bf16),
+            pltpu.VMEM(rate.shape, f32),
+            pltpu.SemaphoreType.DMA((10,)),
+        ),
     )
     first = lax.ppermute(own, "ctx", [(i, (i + 1) % size) for i in range(size)])
+    raw_queries, table, gates, scale, across, down, entry, gain = call(
+        prepare_kernel,
+        (
+            sds((count, grouped), bf16),
+            sds((7, 16, WIDE), f32),
+            sds((24, WIDE), f32),
+            sds((8, VALUES), f32),
+            sds((HEADS, count), f32),
+            sds((count, HEADS), f32),
+            sds((count, VALUES), f32),
+            sds((8, VALUES), f32),
+        ),
+        [SMEM, HBM] + [VMEM] * 6,
+        (10_000_000, 1_000_000),
+        (lengths, pre_conv, own, weight, bias, cumulative, step_size, skip),
+        scratch=(pltpu.VMEM((count, grouped), bf16), pltpu.SemaphoreType.DMA(())),
+    )
     sent, edge = call(
         combine_kernel,
-        (sds((SECOND_ROWS, WIDE), bf16), sds((8, pre_conv.shape[2]), f32)),
-        [SMEM, VMEM, VMEM, VMEM, VMEM],
-        1_000_000,
-        1_000_000,
-        lengths,
-        own,
-        first,
-        conv_weight,
-        bias,
+        (sds((SECOND_ROWS, WIDE), bf16), sds((8, channels), f32)),
+        [VMEM] * 5,
+        (1_000_000, 1_000_000),
+        (own, first, table, gates, scale),
     )
     second = lax.ppermute(sent, "ctx", [(i, i + 2) for i in range(size - 2)])
-    diagonal, queries, entry = call(
+    diagonal, queries, known, scale = call(
         diagonal_kernel,
         (
             sds((count, VALUES), f32),
-            sds((count, BC_GROUPS * STATE), bf16),
-            sds((2 * HEADS, count), bf16),
+            sds((count, grouped), bf16),
+            sds((24, WIDE), f32),
+            sds((8, VALUES), f32),
         ),
-        [SMEM, VMEM, VMEM, VMEM, VMEM],
-        400_000_000,
-        4_000_000,
-        skip,
-        conv,
-        edge,
-        cumulative,
-        step_size,
+        [VMEM] * 9,
+        (400_000_000, 4_000_000),
+        (conv, raw_queries, edge, across, down, gain, first, table, gates),
     )
     return call(
         finish_kernel,
         sds((1, count, VALUES), bf16),
-        [SMEM] + [VMEM] * 7,
-        100_000_000,
-        2_000_000,
-        lengths,
-        first,
-        second,
-        conv_weight,
-        bias,
-        diagonal,
-        queries,
-        entry,
+        [VMEM] * 8,
+        (100_000_000, 2_000_000),
+        (first, second, table, known, scale, diagonal, queries, entry),
+        out_specs=HBM,
+        scratch=(pltpu.VMEM((count, VALUES), bf16), pltpu.SemaphoreType.DMA((BC_GROUPS,))),
     )
 
 

time: 31 us -> 25.7 us (0.83)
  local copies, waits for them, and re-layouts: 4.59 us -> 0 us
  waiting for transfers between devices: 12.7 us -> 12.2 us
    unnamed x20 -> x0, local copies, waits for them, and re-layouts: 4.59 us -> none
    ppermute x1, waiting for transfers between devices: 10.4 us -> 8.5 us  [shard_near(): first = lax.ppermute(own, 'ctx', [(i, (i + 1) % size) for i in range(size)])]
    ppermute x1, waiting for transfers between devices: 2.35 us -> 3.67 us  [shard_near(): second = lax.ppermute(sent, 'ctx', [(i, i + 2) for i in range(size - 2)])]
    pallas_call x4 -> x5, Pallas kernels: 8.66 us -> 8.66 us  [call(): pl.pallas_call(kernel, out_shape=outs, in_specs=in_specs, out_specs=out_s...]
  transfers between devices with their start and end apart: 2 -> 2, of which waited for: 2 -> 2; matrix products, arithmetic and copies ran while one was open for 0% -> 0% of each run, Pallas kernels for 7% -> 14%
where the time goes in v2:
time: 25.7 us; the launch traced here: 25.5 us
  waiting for transfers between devices  12.2 us (47%)
  Pallas kernels  8.66 us (34%)
  starting transfers between devices  4.59 us (18%)
    pallas_call x5, Pallas kernels, call(): pl.pallas_call(kernel, out_shape=outs, in_specs=in_specs, out_specs=out_s...  8.66 us
    ppermute x1, waiting for transfers between devices, shard_near(): first = lax.ppermute(own, 'ctx', [(i, (i + 1) % size) for i in range(size)])  8.5 us
    ppermute x1, waiting for transfers between devices, shard_near(): second = lax.ppermute(sent, 'ctx', [(i, i + 2) for i in range(size - 2)])  3.67 us
    ppermute x1, starting transfers between devices, shard_near(): first = lax.ppermute(own, 'ctx', [(i, (i + 1) % size) for i in range(size)])  2.99 us
    ppermute x1, starting transfers between devices, shard_near(): second = lax.ppermute(sent, 'ctx', [(i, i + 2) for i in range(size - 2)])  1.6 us
  transfers between devices with their start and end apart: 2, of which 2 were waited for; matrix products, arithmetic and copies ran while one was open for 0% of the time, Pallas kernels for 14%

profile of v2, /device:TPU:0, one launch (start us, length us, event | category | flops | bytes accessed | tf_op | source)
XLA Modules:
  0.0 25.5 jit_solution(14146783545980907251)
XLA Ops:
  0.0 3.2 %shard_map.73 = (bf16[128,2304]{1,0:T(8,128)(2,1)S(1)}, f32[64,128]{1,0:T(8,128)S(1)}, bf16[304,512]{1,0:T(8,128)(2,1)S(1)}) custom-call(s32[1,4]{1,0:T(1,128)} %lengths_ref.1, bf16[1,128,2560]{2,1,0:T(8,128)(2,1)} %x_hbm.3, f32[1,64,128]{2,1,0:T(8,128)} %step_ref.1, bf16[4,2560]{1,0:T(4,128)(2,1)} %weight_ref.1, bf16[20,128]{1,0:T(8,128)(2,1)} %bitcast.3, ...), custom_call_target="tpu_custom_call" | custom-call | flops 60000000 | bytes 2000000 | tf_op jit(solution)/shard_map/pallas_call | solution.py:356
  3.2 3.0 %collective-permute-start = (bf16[304,512]{1,0:T(8,128)(2,1)S(1)}, bf16[304,512]{1,0:T(8,128)(2,1)S(1)}, u32[]{:S(2)}, u32[]{:S(2)}) collective-permute-start(bf16[304,512]{1,0:T(8,128)(2,1)S(1)} %get-tuple-element.22.own_ref), channel_id=1, source_target_pairs={{0,2},{2,4},{4,6},{6,8},{8,10},{10,12},{12,14},{14,0},{1,3},{3,5},... | collective-permute-start | bytes 933896 | tf_op jit(solution)/shard_map/ppermute | solution.py:404
  6.2 1.9 %shard_map.74 = (bf16[128,256]{1,0:T(8,128)(2,1)S(1)}, f32[7,16,512]{2,1,0:T(8,128)S(1)}, f32[24,512]{1,0:T(8,128)S(1)}, f32[8,2048]{1,0:T(8,128)S(1)}, f32[64,1...) custom-call(s32[1,4]{1,0:T(1,128)} %lengths_ref.1, ...), custom_call_target="tpu_custom_call" | custom-call | flops 10000000 | bytes 1000000 | tf_op jit(solution)/shard_map/pallas_call | solution.py:356
  8.1 8.5 %collective-permute-done.got_ref.first_ref = bf16[304,512]{1,0:T(8,128)(2,1)S(1)} collective-permute-done((bf16[304,512]{1,0:T(8,128)(2,1)S(1)}, bf16[304,512]{1,0:T(8,128)(2,1)S(1)}, u32[]{:S(2)}, u32[]{:S(2)}) %collective-permute-start) | collective-permute-done | bytes 311328 | tf_op jit(solution)/shard_map/ppermute | solution.py:404
  16.6 0.3 %shard_map.75 = (bf16[272,512]{1,0:T(8,128)(2,1)S(1)}, f32[8,2560]{1,0:T(8,128)S(1)}) custom-call(bf16[304,512]{1,0:T(8,128)(2,1)S(1)} %get-tuple-element.22.own_ref, bf16[304,512]{1,0:T(8,128)(2,1)S(1)} %collective-permute-done.got_ref.first_ref, f32[7,16,512]{2,1,0:T(8,128)S(1)} %get-tuple-element.24.table_ref, ...), custom_call_target="tpu_custom_call" | custom-call | flops 1000000 | bytes 1000000 | tf_op jit(solution)/shard_map/pallas_call | solution.py:356
  16.9 1.6 %collective-permute-start.1 = (bf16[272,512]{1,0:T(8,128)(2,1)S(1)}, bf16[272,512]{1,0:T(8,128)(2,1)S(1)}, u32[]{:S(2)}, u32[]{:S(2)}) collective-permute-start(bf16[272,512]{1,0:T(8,128)(2,1)S(1)} %get-tuple-element.27), channel_id=1, source_target_pairs={{0,4},{2,6},{4,8},{6,10},{8,12},{10,14},{1,5},{3,7},{5,9},{7,11},{... | collective-permute-start | bytes 835592 | tf_op jit(solution)/shard_map/ppermute | solution.py:429
  18.6 1.6 %shard_map.76 = (f32[128,2048]{1,0:T(8,128)S(1)}, bf16[128,256]{1,0:T(8,128)(2,1)S(1)}, f32[24,512]{1,0:T(8,128)S(1)}, f32[8,2048]{1,0:T(8,128)S(1)}) custom-call(bf16[128,2304]{1,0:T(8,128)(2,1)S(1)} %get-tuple-element.28.conv_ref, bf16[128,256]{1,0:T(8,128)(2,1)S(1)} %get-tuple-element.29.raw_queries_ref, f32[8,2560]{1,0:T(8,128)S(1)} %get-tuple-element.30.edge_ref, ...), custom_call_target="tpu_custom_call" | custom-call | flops 400000000 | bytes 4000000 | tf_op jit(solution)/shard_map/pallas_call | solution.py:356
  20.2 3.7 %collective-permute-done.1.second_ref = bf16[272,512]{1,0:T(8,128)(2,1)S(1)} collective-permute-done((bf16[272,512]{1,0:T(8,128)(2,1)S(1)}, bf16[272,512]{1,0:T(8,128)(2,1)S(1)}, u32[]{:S(2)}, u32[]{:S(2)}) %collective-permute-start.1) | collective-permute-done | bytes 278560 | tf_op jit(solution)/shard_map/ppermute | solution.py:429
  23.9 1.6 %shard_map.77 = bf16[1,128,2048]{2,1,0:T(8,128)(2,1)} custom-call(bf16[304,512]{1,0:T(8,128)(2,1)S(1)} %collective-permute-done.got_ref.first_ref, bf16[272,512]{1,0:T(8,128)(2,1)S(1)} %collective-permute-done.1.second_ref, f32[7,16,512]{2,1,0:T(8,128)S(1)} %get-tuple-element.24.table_ref, f32[24,512]{1,0:T(8,128)S(1)} %get-tuple-element.34.known_ref, ...), custom_call_target="tpu_custom_call" | custom-call | flops 100000000 | bytes 2000000 | tf_op jit(solution)/shard_map/pallas_call | solution.py:356
Async XLA Ops:
  3.2 13.4 %collective-permute-start = (bf16[304,512]{1,0:T(8,128)(2,1)S(1)}, bf16[304,512]{1,0:T(8,128)(2,1)S(1)}, u32[]{:S(2)}, u32[]{:S(2)}) collective-permute-start(bf16[304,512]{1,0:T(8,128)(2,1)S(1)} %get-tuple-element.22.own_ref), channel_id=1, source_target_pairs={{0,2},{2,4},{4,6},{6,8},{8,10},{10,12},{12,14},{14,0},{1,3},{3,5},... | collective-permute-start | bytes 933896 | tf_op jit(solution)/shard_map/ppermute | solution.py:404
  16.9 6.9 %collective-permute-start.1 = (bf16[272,512]{1,0:T(8,128)(2,1)S(1)}, bf16[272,512]{1,0:T(8,128)(2,1)S(1)}, u32[]{:S(2)}, u32[]{:S(2)}) collective-permute-start(bf16[272,512]{1,0:T(8,128)(2,1)S(1)} %get-tuple-element.27), channel_id=1, source_target_pairs={{0,4},{2,6},{4,8},{6,10},{8,12},{10,14},{1,5},{3,7},{5,9},{7,11},{... | collective-permute-start | bytes 835592 | tf_op jit(solution)/shard_map/ppermute | solution.py:429

commit v3 on v2

v3 whole, which is shorter than its diff:
```python
import jax
import jax.numpy as jnp
from jax import lax
from jax.experimental import pallas as pl
from jax.experimental.pallas import tpu as pltpu
from jax.sharding import PartitionSpec as P

HEADS = 64
HEAD_DIM = 32
EDGE = 3
STATE = 64
BC_GROUPS = 4
HEADS_GROUP = HEADS // BC_GROUPS
VALUES = HEADS * HEAD_DIM
WIDE = HEADS_GROUP * HEAD_DIM
GROUPED = BC_GROUPS * STATE
CHUNKS = 2
PADS = 4
PER_CHUNK = BC_GROUPS // CHUNKS
HALF = PER_CHUNK * WIDE
ROWS = PER_CHUNK * STATE
TAIL_AT = ROWS
HEAD_AT = ROWS
SENT = ROWS + 16
LOG2E = 1.4426950408889634
VMEM = pl.BlockSpec(memory_space=pltpu.VMEM)
HBM = pl.BlockSpec(memory_space=pltpu.HBM)
f32 = jnp.float32
bf16 = jnp.bfloat16


def iota(shape, dim):
    return lax.broadcasted_iota(jnp.int32, shape, dim)


def dot(a, b, contract=((1,), (0,))):
    return lax.dot_general(a, b, (contract, ((), ())), preferred_element_type=f32)


def is_fresh(lengths_ref, position):
    found = jnp.int32(0)
    start = jnp.int32(0)
    for k in range(lengths_ref.shape[1]):
        found = jnp.where(start == position, jnp.int32(1), found)
        start = start + lengths_ref[0, k]
    return found


def halves(value):
    high = value.astype(bf16)
    return high, (value - high.astype(f32)).astype(bf16)


def cumulative_of(step, rate_row):
    eye = iota((HEADS, HEADS), 0) == iota((HEADS, HEADS), 1)
    rate = jnp.sum(jnp.where(eye, rate_row, 0.0), axis=1, keepdims=True)
    tokens = step.shape[1]
    upto = iota((tokens, tokens), 0) <= iota((tokens, tokens), 1)
    upto = upto.astype(bf16)
    rest = -step * rate
    total = jnp.zeros_like(rest)
    for _ in range(3):
        part = rest.astype(bf16)
        rest = rest - part.astype(f32)
        total = total + dot(part, upto)
    return total


def spread_matrix():
    rows, lanes = 2 * HEADS_GROUP, WIDE
    return (iota((rows, lanes), 0) % HEADS_GROUP == iota((rows, lanes), 1) // HEAD_DIM).astype(bf16)


def spread(per_head, group, matrix):
    part = per_head[group * HEADS_GROUP : (group + 1) * HEADS_GROUP]
    return dot(jnp.concatenate(halves(part), axis=0), matrix, ((0,), (0,)))


def half_silu(half):
    return half + half * jnp.tanh(half)


def to_rows(strip, first):
    rows = iota((8, WIDE), 0)
    top = jnp.zeros((8, WIDE), f32)
    low = jnp.zeros((8, WIDE), f32)
    for k in range(strip.shape[1] // WIDE):
        moved = pltpu.roll(strip[:, k * WIDE : (k + 1) * WIDE], (3 * k - first) % 8, 0)
        if 3 * k < 8:
            top = jnp.where((rows >= 3 * k) & (rows < 3 * k + 3), moved, top)
        if 3 * k + 2 >= 8:
            low = jnp.where((rows >= 3 * k - 8) & (rows < 3 * k - 5), moved, low)
    return jnp.concatenate([top, low], axis=0)


def conv_rows(x, weight, bias, pad_ref):
    count = x.shape[0]
    pad_ref[8 : 8 + count, :] = x
    total = bias + x * weight[3:4]
    for back in range(1, 4):
        total = total + pad_ref[8 - back : 8 - back + count, :] * weight[3 - back : 4 - back]
    return half_silu(total)


def clear(pads_ref):
    for slot in range(PADS):
        pads_ref[slot, :8, :] = jnp.zeros((8, 128), f32)


def half_taps(weight_ref, bias_ref):
    return weight_ref[...].astype(f32) * 0.5, bias_ref[...].astype(f32) * 0.5


def chunk_states(chunk, x_of, key_x, weight, bias, kept, conv_ref, key_ref, sent_ref, pads_ref, wait):
    matrix = spread_matrix()
    lanes = 128
    j = VALUES // lanes + chunk
    clear(pads_ref)
    key = conv_rows(key_x(), weight[:, j * lanes : (j + 1) * lanes], bias[j : j + 1], pads_ref.at[0]).astype(bf16)
    key_ref[...] = key
    for index in range(PER_CHUNK):
        group = chunk * PER_CHUNK + index
        scale = spread(kept, group, matrix)
        wait(index)
        parts = []
        for i in range(WIDE // lanes):
            local = index * WIDE + i * lanes
            j = (chunk * HALF + local) // lanes
            tile = conv_rows(
                x_of(local), weight[:, j * lanes : (j + 1) * lanes], bias[j : j + 1], pads_ref.at[(j + 1) % PADS]
            )
            conv_ref[:, local : local + lanes] = tile.astype(bf16)
            parts.append((tile * scale[:, i * lanes : (i + 1) * lanes]).astype(bf16))
        state = dot(
            key[:, index * STATE : (index + 1) * STATE], jnp.concatenate(parts, axis=1), ((0,), (0,))
        )
        sent_ref[index * STATE : (index + 1) * STATE, :] = state.astype(bf16)


def first_kernel(
    lengths_hbm, x_hbm, step_hbm, weight_hbm, bias_hbm, rate_hbm, skip_hbm,
    conv_ref, key_ref, cumulative_ref, kept_ref, sent_ref, later_ref, query_x_ref, weight_ref, bias_ref, step_ref,
    skip_ref, gates_ref, head_ref,
    lengths_ref, x_ref, key_x_ref, edges_ref, rate_ref, pads_ref, sems,
):
    count = x_ref.shape[0]
    keys_at = VALUES
    pairs = [
        (step_hbm.at[0], step_ref),
        (rate_hbm, rate_ref),
        (lengths_hbm, lengths_ref),
        (weight_hbm, weight_ref),
        (bias_hbm, bias_ref),
        (x_hbm.at[0, :, pl.ds(keys_at, 128)], key_x_ref),
        (x_hbm.at[0, :, pl.ds(0, WIDE)], x_ref.at[:, pl.ds(0, WIDE)]),
        (x_hbm.at[0, :, pl.ds(WIDE, WIDE)], x_ref.at[:, pl.ds(WIDE, WIDE)]),
        (x_hbm.at[0, pl.ds(0, 16), :], edges_ref.at[pl.ds(0, 16), :]),
        (x_hbm.at[0, pl.ds(count - 16, 16), :], edges_ref.at[pl.ds(16, 16), :]),
        (x_hbm.at[0, :, pl.ds(HALF, HALF)], later_ref.at[:, pl.ds(0, HALF)]),
        (x_hbm.at[0, :, pl.ds(keys_at + 128, 128)], later_ref.at[:, pl.ds(HALF, 128)]),
        (x_hbm.at[0, :, pl.ds(keys_at + GROUPED, GROUPED)], query_x_ref),
        (skip_hbm, skip_ref),
    ]
    copies = [pltpu.make_async_copy(a, b, sems.at[i]) for i, (a, b) in enumerate(pairs)]
    for copy in copies:
        copy.start()
    for copy in copies[:7]:
        copy.wait()
    position = lax.axis_index("ctx")
    fresh = is_fresh(lengths_ref, position)
    goes_on = (1 - fresh).astype(f32)
    both = goes_on * (1 - is_fresh(lengths_ref, position - 1)).astype(f32)
    third = jnp.where(position == 2, 1.0, 0.0).astype(f32)
    rows = iota((8, WIDE), 0)
    gates_ref[...] = jnp.where(rows == 0, goes_on, jnp.where(rows == 1, both, third))
    step = step_ref[...]
    cumulative = cumulative_of(step, rate_ref[...])
    cumulative_ref[...] = cumulative
    last = cumulative[:, count - 1 :]
    tail = step * jnp.exp(last - cumulative)
    lanes = iota((HEADS, count), 1)
    kept = jnp.where((lanes >= EDGE) | (fresh == 1), tail, 0.0)
    kept_ref[...] = kept
    weight, bias = half_taps(weight_ref, bias_ref)
    chunk_states(
        0,
        lambda at: x_ref[:, at : at + 128].astype(f32),
        lambda: key_x_ref[...].astype(f32),
        weight, bias, kept, conv_ref, key_ref, sent_ref, pads_ref,
        lambda index: copies[7].wait() if index else None,
    )
    scales = jnp.where(lanes == EDGE, jnp.exp(last), tail)
    high, low = halves(scales)
    place = iota((HEADS, 128), 1) - iota((HEADS, 128), 0)
    picked = dot(high, (place == 0).astype(bf16), ((0,), (0,)))
    picked = picked + dot(low, (place == HEADS).astype(bf16), ((0,), (0,)))
    line = jnp.concatenate([picked[k : k + 1] for k in range(4)], axis=1)
    copies[8].wait()
    copies[9].wait()
    tail_rows = to_rows(edges_ref[16:, :].astype(f32)[8:], 5)
    tail_rows = jnp.where(iota((16, WIDE), 0) == 15, line, tail_rows)
    sent_ref[TAIL_AT : TAIL_AT + 16, :] = tail_rows.astype(bf16)
    head_ref[...] = edges_ref[:16, :]
    for copy in copies[10:]:
        copy.wait()


def later_kernel(
    x_ref, head_ref, weight_ref, bias_ref, kept_ref, before_ref, conv_ref, key_ref, sent_ref, early_ref, pads_ref
):
    weight, bias = half_taps(weight_ref, bias_ref)
    chunk_states(
        1,
        lambda at: x_ref[:, at : at + 128].astype(f32),
        lambda: x_ref[:, HALF : HALF + 128].astype(f32),
        weight, bias, kept_ref[...], conv_ref, key_ref, sent_ref, pads_ref,
        lambda index: None,
    )
    sent_ref[HEAD_AT : HEAD_AT + 16, :] = to_rows(head_ref[...].astype(f32)[:8], 0).astype(bf16)
    early_ref[:ROWS, :] = before_ref[:ROWS, :]
    early_ref[ROWS : 2 * ROWS, :] = sent_ref[:ROWS, :]
    early_ref[2 * ROWS :, :] = before_ref[TAIL_AT : TAIL_AT + 16, :]


def known_part(head_block, table_ref):
    return (
        table_ref[0]
        + head_block * table_ref[1]
        + pltpu.roll(head_block, 1, 0) * table_ref[2]
        + pltpu.roll(head_block, 2, 0) * table_ref[3]
    )


def edge_rows(tail_block, known, table_ref):
    block = half_silu(
        known
        + tail_block * table_ref[4]
        + pltpu.roll(tail_block, 15, 0) * table_ref[5]
        + pltpu.roll(tail_block, 14, 0) * table_ref[6]
    )
    return [pltpu.roll(block, (16 - 3 * k) % 16, 0)[:8] for k in range(5)]


def head_lanes(rows):
    lanes = iota((128, VALUES), 1) // HEAD_DIM
    matrix = (iota((128, VALUES), 0) % HEADS == lanes).astype(bf16)
    return dot(rows, matrix)[:8]


def edge_scales(tail_rows):
    line = tail_rows[15:16].astype(f32)
    rows = [line[:, k * 128 : (k + 1) * 128] for k in range(4)]
    return head_lanes(jnp.concatenate(rows + [jnp.zeros((12, 128), f32)], axis=0).astype(bf16))


def prepare_kernel(
    own_ref, later_ref, query_x_ref, weight_ref, bias_ref, cumulative_ref, step_ref, skip_ref, gates_ref,
    queries_ref, table_ref, known_ref, scale_ref, decay_ref, entry_ref, gain_ref, pads_ref,
):
    clear(pads_ref)
    weight, bias = half_taps(weight_ref, bias_ref)
    rows = iota((16, WIDE), 0)
    third = rows % 3
    chunk = rows // 3

    def blocked(lines):
        out = jnp.zeros((16, WIDE), f32)
        for k in range(5):
            out = jnp.where(chunk == k, lines[k], out)
        return out

    taps = [
        blocked([weight[tap : tap + 1, k * WIDE : (k + 1) * WIDE] for k in range(5)])
        for tap in range(4)
    ]
    table_ref[0] = blocked(
        [
            jnp.concatenate([bias[4 * k + i : 4 * k + i + 1, :] for i in range(4)], axis=1)
            for k in range(5)
        ]
    )
    table_ref[1] = taps[3]
    table_ref[2] = jnp.where(third == 0, 0.0, taps[2])
    table_ref[3] = jnp.where(third == 2, taps[1], 0.0)
    table_ref[4] = taps[0]
    table_ref[5] = jnp.where(third == 2, 0.0, taps[1])
    table_ref[6] = jnp.where(third == 0, taps[2], 0.0)
    known_ref[...] = known_part(later_ref[HEAD_AT : HEAD_AT + 16, :].astype(f32), table_ref)
    scale_ref[...] = edge_scales(own_ref[TAIL_AT : TAIL_AT + 16, :]) * gates_ref[:1, :1]
    cumulative = cumulative_ref[...] * LOG2E
    across = cumulative - jnp.log2(step_ref[...])
    down = cumulative.T
    count = down.shape[0]
    causal = iota((count, count), 0) >= iota((count, count), 1)
    for at in range(HEADS):
        gap = down[:, at : at + 1] - across[at : at + 1, :]
        decay_ref[at] = jnp.exp2(jnp.where(causal, gap, -1e30))
    matrix = spread_matrix()
    entry = jnp.exp2(cumulative)
    for group in range(BC_GROUPS):
        entry_ref[:, group * WIDE : (group + 1) * WIDE] = spread(entry, group, matrix)
    gain_ref[...] = head_lanes(
        jnp.concatenate(halves(skip_ref[...] + jnp.zeros((16, HEADS), f32)), axis=1)
    )
    first = VALUES + GROUPED
    for i in range(2):
        cols = slice(first + i * 128, first + (i + 1) * 128)
        j = first // 128 + i
        tile = conv_rows(
            query_x_ref[:, i * 128 : (i + 1) * 128].astype(f32), weight[:, cols], bias[j : j + 1, :], pads_ref.at[i]
        )
        queries_ref[:, i * 128 : (i + 1) * 128] = tile.astype(bf16)


def edge_state(values_rows, keys_rows, scale, group):
    rows = iota((8, WIDE), 0)
    written = jnp.where(rows < EDGE, values_rows * scale, 0.0)
    tile = keys_rows[:, (group // 2) * 128 : (group // 2 + 1) * 128].astype(bf16)
    return dot(tile[:, (group % 2) * STATE : (group % 2 + 1) * STATE], written.astype(bf16), ((0,), (0,)))


def combine_chunk(chunk, own_ref, got_ref, scale_ref, sent_ref, edge_of):
    keys = edge_of(BC_GROUPS)
    for index in range(PER_CHUNK):
        group = chunk * PER_CHUNK + index
        at = slice(index * STATE, (index + 1) * STATE)
        scale = scale_ref[:, group * WIDE : (group + 1) * WIDE]
        extra = edge_state(edge_of(group), keys, scale, group)
        total = own_ref[at, :].astype(f32) + extra + scale[EDGE : EDGE + 1] * got_ref[at, :].astype(f32)
        sent_ref[at, :] = total.astype(bf16)


def combine_first_kernel(own_ref, got_ref, table_ref, known_ref, gates_ref, scale_ref, sent_ref, edge_ref):
    tail_block = got_ref[TAIL_AT : TAIL_AT + 16, :].astype(f32) * gates_ref[:1, :]
    chunks = edge_rows(tail_block, known_ref[...], table_ref)
    combine_chunk(0, own_ref, got_ref, scale_ref, sent_ref, lambda k: chunks[k])
    sent_ref[ROWS:, :] = own_ref[TAIL_AT : TAIL_AT + 16, :]
    for k in range(5):
        edge_ref[:, k * WIDE : (k + 1) * WIDE] = chunks[k]


def combine_later_kernel(own_ref, got_ref, scale_ref, edge_ref, sent_ref):
    combine_chunk(
        1, own_ref, got_ref, scale_ref, sent_ref, lambda k: edge_ref[:, k * WIDE : (k + 1) * WIDE]
    )


def diagonal_kernel(
    conv0_ref, conv1_ref, key0_ref, key1_ref, raw_queries_ref, edge_ref, decay_ref, gain_ref,
    got_ref, later_ref, table_ref, gates_ref,
    diagonal_ref, queries_ref, known_ref, scale_ref,
):
    known_ref[...] = known_part(later_ref[HEAD_AT : HEAD_AT + 16, :].astype(f32), table_ref)
    scale_ref[...] = edge_scales(got_ref[TAIL_AT : TAIL_AT + 16, :]) * gates_ref[1:2, :1]
    count = conv0_ref.shape[0]
    edge_row = iota((count, 128), 0) < EDGE
    lane_head = iota((count, 128), 1) // HEAD_DIM

    def patched(tile, j):
        rows = jnp.concatenate(
            [edge_ref[:, j * 128 : (j + 1) * 128], jnp.zeros((count - 8, 128), f32)], axis=0
        )
        return jnp.where(edge_row, rows, tile.astype(f32))

    keys = [patched(ref[...], 16 + i).astype(bf16) for i, ref in enumerate((key0_ref, key1_ref))]
    queries = [
        patched(raw_queries_ref[:, i * 128 : (i + 1) * 128], 18 + i).astype(bf16) for i in range(2)
    ]
    for i in range(2):
        queries_ref[:, i * 128 : (i + 1) * 128] = queries[i]
    for group in range(BC_GROUPS):
        part = slice((group % 2) * STATE, (group % 2 + 1) * STATE)
        scores = dot(queries[group // 2][:, part], keys[group // 2][:, part], ((1,), (1,)))
        conv_ref = (conv0_ref, conv1_ref)[group // PER_CHUNK]
        for i in range(4):
            j = group * 4 + i
            cols = slice(j * 128, (j + 1) * 128)
            at = (j * 128) % HALF
            values = patched(conv_ref[:, at : at + 128], j)
            weights, parts = [], []
            for k in range(4):
                at = 4 * j + k
                weights.append((decay_ref[at] * scores).astype(bf16))
                parts.append(jnp.where(lane_head == k, values, 0.0).astype(bf16))
            total = dot(jnp.concatenate(weights, axis=1), jnp.concatenate(parts, axis=0))
            diagonal_ref[:, cols] = total + gain_ref[:1, cols] * values


def group_out(group, total, diagonal_ref, queries_ref, entry_ref):
    cols = slice(group * WIDE, (group + 1) * WIDE)
    low = (group % 2) * STATE
    tile = queries_ref[:, (group // 2) * 128 : (group // 2 + 1) * 128]
    carried = dot(tile[:, low : low + STATE], total.astype(bf16))
    return (diagonal_ref[:, cols] + entry_ref[:, cols] * carried).astype(bf16)


def finish_first_kernel(
    first0_ref, first1_ref, second_ref, early_ref, table_ref, known_ref, gates_ref, scale_ref, diagonal_ref,
    queries_ref, entry_ref,
    out_ref, base_ref,
):
    third = gates_ref[2:3, :] > 0.5
    kept = gates_ref[:1, :]

    def second_of(at, early_at, rows):
        a = second_ref[at : at + rows, :].astype(f32)
        return jnp.where(third, early_ref[early_at : early_at + rows, :].astype(f32), a)

    chunks = edge_rows(second_of(ROWS, 2 * ROWS, 16), known_ref[...], table_ref)
    for group in range(BC_GROUPS):
        chunk, index = divmod(group, PER_CHUNK)
        at = slice(index * STATE, (index + 1) * STATE)
        scale = scale_ref[:, group * WIDE : (group + 1) * WIDE]
        first = (first0_ref, first1_ref)[chunk][at, :].astype(f32)
        total = first * kept + edge_state(chunks[group], chunks[BC_GROUPS], scale, group)
        if chunk == 0:
            total = total + scale[EDGE : EDGE + 1] * second_of(index * STATE, index * STATE, STATE)
            out_ref[:, group * WIDE : (group + 1) * WIDE] = group_out(
                group, total, diagonal_ref, queries_ref, entry_ref
            )
        else:
            base_ref[at, :] = total


def finish_later_kernel(
    second_ref, early_ref, base_ref, gates_ref, scale_ref, diagonal_ref, queries_ref, entry_ref, before_ref,
    out_hbm, out_ref, sems,
):
    third = gates_ref[2:3, :] > 0.5
    copies = [
        pltpu.make_async_copy(before_ref, out_hbm.at[0, :, pl.ds(0, HALF)], sems.at[PER_CHUNK])
    ]
    copies[0].start()
    for index in range(PER_CHUNK):
        group = PER_CHUNK + index
        at = slice(index * STATE, (index + 1) * STATE)
        early = early_ref[ROWS + index * STATE : ROWS + (index + 1) * STATE, :].astype(f32)
        second = jnp.where(third, early, second_ref[at, :].astype(f32))
        decay = scale_ref[EDGE : EDGE + 1, group * WIDE : (group + 1) * WIDE]
        total = base_ref[at, :] + decay * second
        here = pl.ds(index * WIDE, WIDE)
        out_ref[:, here] = group_out(group, total, diagonal_ref, queries_ref, entry_ref)
        copy = pltpu.make_async_copy(
            out_ref.at[:, here], out_hbm.at[0, :, pl.ds(group * WIDE, WIDE)], sems.at[index]
        )
        copy.start()
        copies.append(copy)
    for copy in copies:
        copy.wait()


def call(kernel, outs, in_specs, cost, args, out_specs=None, scratch=()):
    return pl.pallas_call(
        kernel,
        out_shape=outs,
        in_specs=in_specs,
        out_specs=out_specs or jax.tree.map(lambda _: VMEM, outs),
        scratch_shapes=scratch,
        compiler_params=pltpu.CompilerParams(vmem_limit_bytes=24 * 1024 * 1024),
        cost_estimate=pl.CostEstimate(flops=cost[0], bytes_accessed=cost[1], transcendentals=0),
    )(*args)


def permuted(array, edges):
    size, lanes = lax.axis_size("ctx"), lax.axis_size("lane")
    table = []
    for source in range(size):
        for lane in range(lanes):
            if source in edges:
                target = edges[source] * lanes + lane
            else:
                target = source * lanes + (lane + 1) % lanes
            table.append((source * lanes + lane, target))
    return lax.ppermute(array, ("ctx", "lane"), table)


def shard_near(pre_conv, step_size, lengths, conv_weight, conv_bias, decay_rate, skip_gain):
    count, channels = pre_conv.shape[1:]
    size = lax.axis_size("ctx")
    ring = [(i, (i + 1) % size) for i in range(size)]
    onward = {i: i + 2 for i in range(1, size - 2)}
    onward[size - 2] = 2
    onward[size - 1] = 1
    arguments = tuple(
        pltpu.with_memory_space_constraint(array, pltpu.HBM)
        for array in (
            lengths,
            pre_conv,
            step_size,
            conv_weight,
            conv_bias.reshape(-1, 128),
            decay_rate.reshape(1, -1),
            skip_gain.reshape(1, -1),
        )
    )
    sds = jax.ShapeDtypeStruct
    pads = pltpu.VMEM((PADS, count + 8, 128), f32)
    conv0, key0, cumulative, kept, own0, later_x, query_x, weight, bias, step, skip, gates, head = call(
        first_kernel,
        (
            sds((count, HALF), bf16),
            sds((count, 128), bf16),
            sds((HEADS, count), f32),
            sds((HEADS, count), f32),
            sds((SENT, WIDE), bf16),
            sds((count, HALF + 128), bf16),
            sds((count, GROUPED), bf16),
            sds(conv_weight.shape, bf16),
            sds((channels // 128, 128), bf16),
            sds((HEADS, count), f32),
            sds((1, HEADS), f32),
            sds((8, WIDE), f32),
            sds((16, channels), bf16),
        ),
        [HBM] * 7,
        (40_000_000, 2_000_000),
        arguments,
        scratch=(
            pltpu.SMEM(lengths.shape, jnp.int32),
            pltpu.VMEM((count, HALF), bf16),
            pltpu.VMEM((count, 128), bf16),
            pltpu.VMEM((32, channels), bf16),
            pltpu.VMEM((1, HEADS), f32),
            pads,
            pltpu.SemaphoreType.DMA((14,)),
        ),
    )
    first0 = lax.ppermute(own0, "ctx", ring)
    conv1, key1, own1, early = call(
        later_kernel,
        (
            sds((count, HALF), bf16),
            sds((count, 128), bf16),
            sds((SENT, WIDE), bf16),
            sds((2 * ROWS + 16, WIDE), bf16),
        ),
        [VMEM] * 6,
        (40_000_000, 2_000_000),
        (later_x, head, weight, bias, kept, own0),
        scratch=(pads,),
    )
    first1 = lax.ppermute(own1, "ctx", ring)
    early = permuted(early, {0: 2, 2: 0})
    raw_queries, table, known, scale, decay, entry, gain = call(
        prepare_kernel,
        (
            sds((count, GROUPED), bf16),
            sds((7, 16, WIDE), f32),
            sds((16, WIDE), f32),
            sds((8, VALUES), f32),
            sds((HEADS, count, count), f32),
            sds((count, VALUES), f32),
            sds((8, VALUES), f32),
        ),
        [VMEM] * 9,
        (100_000_000, 1_000_000),
        (own0, own1, query_x, weight, bias, cumulative, step, skip, gates),
        scratch=(pads,),
    )
    sent0, edge = call(
        combine_first_kernel,
        (sds((ROWS + 16, WIDE), bf16), sds((8, channels), f32)),
        [VMEM] * 6,
        (1_000_000, 1_000_000),
        (own0, first0, table, known, gates, scale),
    )
    second0 = permuted(sent0, onward)
    sent1 = call(
        combine_later_kernel,
        sds((ROWS, WIDE), bf16),
        [VMEM] * 4,
        (1_000_000, 1_000_000),
        (own1, first1, scale, edge),
    )
    second1 = permuted(sent1, onward)
    diagonal, queries, known, scale = call(
        diagonal_kernel,
        (
            sds((count, VALUES), f32),
            sds((count, GROUPED), bf16),
            sds((16, WIDE), f32),
            sds((8, VALUES), f32),
        ),
        [VMEM] * 12,
        (400_000_000, 4_000_000),
        (conv0, conv1, key0, key1, raw_queries, edge, decay, gain, first0, first1, table, gates),
    )
    out0, base = call(
        finish_first_kernel,
        (sds((count, HALF), bf16), sds((ROWS, WIDE), f32)),
        [VMEM] * 11,
        (50_000_000, 2_000_000),
        (first0, first1, second0, early, table, known, gates, scale, diagonal, queries, entry),
    )
    return call(
        finish_later_kernel,
        sds((1, count, VALUES), bf16),
        [VMEM] * 9,
        (50_000_000, 2_000_000),
        (second1, early, base, gates, scale, diagonal, queries, entry, out0),
        out_specs=HBM,
        scratch=(pltpu.VMEM((count, HALF), bf16), pltpu.SemaphoreType.DMA((PER_CHUNK + 1,))),
    )


def shifted(value, axis, steps):
    count = lax.axis_size(axis)
    first, last = (max(0, -steps), min(count, count - steps))
    return lax.ppermute(value, axis, [(source, source + steps) for source in range(first, last)])


def carried_in(array, axis, combine, identity):
    length, index = (lax.axis_size(axis), lax.axis_index(axis))
    everything = jax.tree.map(
        lambda part, kind: lax.all_gather(part.astype(kind), axis),
        array,
        (jnp.bfloat16, jnp.bfloat16),
    )
    start = jax.tree.map(
        lambda part, zero: jnp.broadcast_to(jnp.asarray(zero, part.dtype), part.shape),
        array,
        identity,
    )

    def step(k, before):
        reached = k < index
        new = combine(
            before, jax.tree.map(lambda part, own: part[k].astype(own.dtype), everything, array)
        )
        return jax.tree.map(lambda a, b: jnp.where(reached, a, b), new, before)

    return lax.fori_loop(0, length, step, start)


def convolve(padded, conv_weight, conv_bias, count_rows):
    total = conv_bias.astype(jnp.float32)[None, :]
    for offset in range(conv_weight.shape[0]):
        total = (
            total
            + padded[offset : offset + count_rows].astype(jnp.float32)
            * conv_weight[offset].astype(jnp.float32)[None, :]
        )
    return jax.nn.silu(total).astype(jnp.bfloat16)


def group_terms(values, keys_in, queries, decay_rate, step_rows):
    heads_group = step_rows.shape[0]
    count_rows = step_rows.shape[1]
    values = values.reshape(count_rows, heads_group, -1)
    cumulative = jnp.cumsum(-step_rows * decay_rate[:, None], axis=1)
    scores = jnp.einsum("tn,sn->ts", queries, keys_in, preferred_element_type=jnp.float32)
    later = lax.broadcasted_iota(jnp.int32, (count_rows, count_rows), 0)
    earlier = lax.broadcasted_iota(jnp.int32, (count_rows, count_rows), 1)
    spread = jnp.where(
        (later >= earlier)[None], cumulative[:, :, None] - cumulative[:, None, :], -1e30
    )
    weights = (jnp.exp(spread) * scores[None]).astype(jnp.bfloat16)
    scaled = (values * step_rows.T[:, :, None]).astype(jnp.bfloat16)
    diagonal_part = jnp.einsum("hts,shp->thp", weights, scaled, preferred_element_type=jnp.float32)
    tail_weight = jnp.exp(cumulative[:, -1:] - cumulative)
    written = (values * (step_rows * tail_weight).T[:, :, None]).astype(jnp.bfloat16)
    local_state = jnp.einsum("tn,thp->hpn", keys_in, written, preferred_element_type=jnp.float32)
    return (diagonal_part, local_state, jnp.exp(cumulative[:, -1]), jnp.exp(cumulative), values)


def finish_group(diagonal_part, entry_decay, queries, incoming, values, skip_gain):
    incoming_rounded = incoming.astype(jnp.bfloat16)
    carried_part = jnp.einsum(
        "tn,hpn->thp", queries, incoming_rounded, preferred_element_type=jnp.float32
    )
    carried_part = carried_part * entry_decay.T[:, :, None]
    return diagonal_part + carried_part + skip_gain[None, :, None] * values.astype(jnp.float32)


def combine(earlier, later):
    return (earlier[0] * later[0], later[0][:, None, None] * earlier[1] + later[1])


def shard_far(pre_conv, step_size, lengths, conv_weight, conv_bias, decay_rate, skip_gain):
    count_rows = pre_conv.shape[1]
    kernel_len = conv_weight.shape[0]
    heads_group = HEADS // BC_GROUPS
    position = lax.axis_index("ctx")
    sizes_row = lengths[0]
    starts = jnp.cumsum(sizes_row) - sizes_row
    fresh = jnp.any(starts == position)
    retain = jnp.where(fresh, 0.0, 1.0).astype(jnp.float32)
    own_rows = pre_conv[0]
    previous = shifted(own_rows[count_rows - kernel_len + 1 :], "ctx", 1)
    previous = jnp.where(fresh, jnp.zeros_like(previous), previous)
    convolved = convolve(
        jnp.concatenate([previous, own_rows], axis=0), conv_weight, conv_bias, count_rows
    )
    values = convolved[:, : HEADS * HEAD_DIM]
    keys_all = convolved[:, HEADS * HEAD_DIM : HEADS * HEAD_DIM + BC_GROUPS * STATE]
    queries_all = convolved[:, HEADS * HEAD_DIM + BC_GROUPS * STATE :]
    step_rows = step_size[0]
    results = []
    pieces = []
    for bc_group in range(BC_GROUPS):
        low = bc_group * heads_group
        high = low + heads_group
        pieces.append(
            group_terms(
                values[:, low * HEAD_DIM : high * HEAD_DIM],
                keys_all[:, bc_group * STATE : (bc_group + 1) * STATE],
                queries_all[:, bc_group * STATE : (bc_group + 1) * STATE],
                decay_rate[low:high],
                step_rows[low:high],
            )
        )
    decays = jnp.concatenate([piece[2] for piece in pieces], axis=0) * retain
    states = jnp.concatenate([piece[1] for piece in pieces], axis=0)
    identity = (jnp.ones_like(decays), jnp.zeros_like(states))
    totals = carried_in((decays, states), "ctx", combine, identity)
    incoming = totals[1] * retain
    for bc_group in range(BC_GROUPS):
        low = bc_group * heads_group
        high = low + heads_group
        piece = pieces[bc_group]
        results.append(
            finish_group(
                piece[0],
                piece[3],
                queries_all[:, bc_group * STATE : (bc_group + 1) * STATE],
                incoming[low:high],
                piece[4],
                skip_gain[low:high],
            )
        )
    output = (
        jnp.concatenate(results, axis=1).reshape(count_rows, HEADS * HEAD_DIM).astype(jnp.bfloat16)
    )
    return output[None]


def solution(mesh):
    in_specs = (
        P(("groups", "lane"), "ctx", None),
        P(("groups", "lane"), None, "ctx"),
        P(("groups", "lane"), None),
        P(),
        P(),
        P(),
        P(),
    )
    out_specs = P(("groups", "lane"), "ctx", None)
    shards = shard_near if mesh.shape["ctx"] <= 8 else shard_far
    return jax.shard_map(shards, mesh=mesh, in_specs=in_specs, out_specs=out_specs, check_vma=False)
```

time: 25.7 us -> 20.1 us (0.78)
  waiting for transfers between devices: 12.2 us -> 7.2 us
  Pallas kernels: 8.66 us -> 7.77 us
    ppermute x2 -> x5, waiting for transfers between devices: 12.2 us -> 7.2 us  [the longest x1 4.14 us: shard_near(): first1 = lax.ppermute(own1, 'ctx', ring)]
    pallas_call x5 -> x8, Pallas kernels: 8.66 us -> 7.77 us  [call(): pl.pallas_call(kernel, out_shape=outs, in_specs=in_specs, out_specs=out_s...]
    ppermute x2 -> x5, starting transfers between devices: 4.59 us -> 4.78 us  [the longest x1 2.99 us: shard_near(): first0 = lax.ppermute(own0, 'ctx', ring)]
  transfers between devices with their start and end apart: 2 -> 5, of which waited for: 2 -> 2; matrix products, arithmetic and copies ran while one was open for 0% -> 0% of each run, Pallas kernels for 14% -> 23%
where the time goes in v3:
time: 20.1 us; the launch traced here: 19.8 us
  Pallas kernels  7.77 us (39%)
  waiting for transfers between devices  7.2 us (36%)
  starting transfers between devices  4.78 us (24%)
    pallas_call x8, Pallas kernels, call(): pl.pallas_call(kernel, out_shape=outs, in_specs=in_specs, out_specs=out_s...  7.77 us
    ppermute x1, waiting for transfers between devices, shard_near(): first1 = lax.ppermute(own1, 'ctx', ring)  4.14 us
    ppermute x1, waiting for transfers between devices, shard_near(): first0 = lax.ppermute(own0, 'ctx', ring)  3.06 us
    ppermute x1, starting transfers between devices, shard_near(): first0 = lax.ppermute(own0, 'ctx', ring)  2.99 us
    ppermute x3, starting transfers between devices, permuted(): return lax.ppermute(array, ('ctx', 'lane'), table)  1.76 us
  transfers between devices with their start and end apart: 5, of which 2 were waited for; matrix products, arithmetic and copies ran while one was open for 0% of the time, Pallas kernels for 23%

profile of v3, /device:TPU:0, one launch (start us, length us, event | category | flops | bytes accessed | tf_op | source)
XLA Modules:
  0.0 19.8 jit_solution(10546224898732058962)
XLA Ops:
  0.0 2.2 %shard_map.73 = (bf16[128,1024]{1,0:T(8,128)(2,1)S(1)}, bf16[128,128]{1,0:T(8,128)(2,1)S(1)}, f32[64,128]{1,0:T(8,128)S(1)}, f32[64,128]{1,0:T(8,128)S(1)}, bf16...) custom-call(s32[1,4]{1,0:T(1,128)} %lengths_hbm.1, ...), custom_call_target="tpu_custom_call" | custom-call | flops 40000000 | bytes 2000000 | tf_op jit(solution)/shard_map/pallas_call | solution.py:453
  2.3 3.0 %collective-permute-start.1 = (bf16[144,512]{1,0:T(8,128)(2,1)S(1)}, bf16[144,512]{1,0:T(8,128)(2,1)S(1)}, u32[]{:S(2)}, u32[]{:S(2)}) collective-permute-start(bf16[144,512]{1,0:T(8,128)(2,1)S(1)} %get-tuple-element.42.before_ref.own_ref), channel_id=1, source_target_pairs={{0,2},{2,4},{4,6},{6,8},{8,10},{10,12},{12,14},{14,0},{1,3},{3,5},... | collective-permute-start | bytes 442376 | tf_op jit(solution)/shard_map/ppermute | solution.py:528
  5.2 0.6 %shard_map.74 = (bf16[128,1024]{1,0:T(8,128)(2,1)S(1)}, bf16[128,128]{1,0:T(8,128)(2,1)S(1)}, bf16[144,512]{1,0:T(8,128)(2,1)S(1)}, bf16[272,512]{1,0:T(8,128)(2,1)S(1)}) custom-call(bf16[128,1152]{1,0:T(8,128)(2,1)S(1)} %get-tuple-element.37.x_ref, bf16[16,2560]{1,0:T(8,128)(2,1)S(1)} %get-tuple-element.38.head_ref, ...), custom_call_target="tpu_custom_call" | custom-call | flops 40000000 | bytes 2000000 | tf_op jit(solution)/shard_map/pallas_call | solution.py:453
  5.9 1.6 %collective-permute-start.3 = (bf16[272,512]{1,0:T(8,128)(2,1)S(1)}, bf16[272,512]{1,0:T(8,128)(2,1)S(1)}, u32[]{:S(2)}, u32[]{:S(2)}) collective-permute-start(bf16[272,512]{1,0:T(8,128)(2,1)S(1)} %get-tuple-element.53), channel_id=1, source_target_pairs={{0,4},{1,5},{2,3},{3,2},{4,0},{5,1},{6,7},{7,6},{8,9},{9,8},{10,11... | collective-permute-start | bytes 835592 | tf_op jit(solution)/shard_map/ppermute | solution.py:474
  7.5 0.0 collective-permute-start
  7.6 1.5 %shard_map.75 = (bf16[128,256]{1,0:T(8,128)(2,1)S(1)}, f32[7,16,512]{2,1,0:T(8,128)S(1)}, f32[16,512]{1,0:T(8,128)S(1)}, f32[8,2048]{1,0:T(8,128)S(1)}, f32[64,1...) custom-call(bf16[144,512]{1,0:T(8,128)(2,1)S(1)} %get-tuple-element.42.before_ref.own_ref, ...), custom_call_target="tpu_custom_call" | custom-call | flops 100000000 | bytes 1000000 | tf_op jit(solution)/shard_map/pallas_call | solution.py:453
  9.1 3.1 %collective-permute-done.1.got_ref.first0_ref = bf16[144,512]{1,0:T(8,128)(2,1)S(1)} collective-permute-done((bf16[144,512]{1,0:T(8,128)(2,1)S(1)}, bf16[144,512]{1,0:T(8,128)(2,1)S(1)}, u32[]{:S(2)}, u32[]{:S(2)}) %collective-permute-start.1) | collective-permute-done | bytes 147488 | tf_op jit(solution)/shard_map/ppermute | solution.py:528
  12.1 0.3 %shard_map.76 = (bf16[144,512]{1,0:T(8,128)(2,1)S(1)}, f32[8,2560]{1,0:T(8,128)S(1)}) custom-call(bf16[144,512]{1,0:T(8,128)(2,1)S(1)} %get-tuple-element.42.before_ref.own_ref, bf16[144,512]{1,0:T(8,128)(2,1)S(1)} %collective-permute-done.1.got_ref.first0_ref, f32[7,16,512]{2,1,0:T(8,128)S(1)} %get-tuple-element.50.table_ref, ...), custom_call_target="tpu_custom_call" | custom-call | flops 1000000 | bytes 1000000 | tf_op jit(solution)/shard_map/pallas_call | solution.py:453
  12.4 0.1 collective-permute-start.4
  12.5 4.1 %collective-permute-done.got_ref.later_ref.first1_ref = bf16[144,512]{1,0:T(8,128)(2,1)S(1)} collective-permute-done((bf16[144,512]{1,0:T(8,128)(2,1)S(1)}, bf16[144,512]{1,0:T(8,128)(2,1)S(1)}, u32[]{:S(2)}, u32[]{:S(2)}) %collective-permute-start) | collective-permute-done | bytes 147488 | tf_op jit(solution)/shard_map/ppermute | solution.py:542
  16.6 0.3 %shard_map.77 = bf16[128,512]{1,0:T(8,128)(2,1)S(1)} custom-call(bf16[144,512]{1,0:T(8,128)(2,1)S(1)} %get-tuple-element.43.later_ref.own_ref, bf16[144,512]{1,0:T(8,128)(2,1)S(1)} %collective-permute-done.got_ref.later_ref.first1_ref, f32[8,2048]{1,0:T(8,128)S(1)} %get-tuple-element.49.scale_ref, f32[8,2560]{1,0:T(8,128)S(1)} %get-tuple-element.52.edge_ref), custom_call_target="tpu_custom_call" | custom-call | flops 1000000 | bytes 1000000 | tf_op jit(solution)/shard_map/pallas_call | solution.py:453
  16.9 0.1 collective-permute-start.2
  16.9 1.4 %shard_map.78 = (f32[128,2048]{1,0:T(8,128)S(1)}, bf16[128,256]{1,0:T(8,128)(2,1)S(1)}, f32[16,512]{1,0:T(8,128)S(1)}, f32[8,2048]{1,0:T(8,128)S(1)}) custom-call(bf16[128,1024]{1,0:T(8,128)(2,1)S(1)} %get-tuple-element.55.conv0_ref, bf16[128,1024]{1,0:T(8,128)(2,1)S(1)} %get-tuple-element.56.conv1_ref, bf16[128,128]{1,0:T(8,128)(2,1)S(1)} %get-tuple-element.57.key0_ref, ...), custom_call_target="tpu_custom_call" | custom-call | flops 400000000 | bytes 4000000 | tf_op jit(solution)/shard_map/pallas_call | solution.py:453
  18.3 0.0 collective-permute-done.3.early_ref
  18.3 0.0 collective-permute-done.4.second_ref
  18.3 0.6 %shard_map.79 = (bf16[128,1024]{1,0:T(8,128)(2,1)S(1)}, f32[128,512]{1,0:T(8,128)S(1)}) custom-call(bf16[144,512]{1,0:T(8,128)(2,1)S(1)} %collective-permute-done.1.got_ref.first0_ref, bf16[144,512]{1,0:T(8,128)(2,1)S(1)} %collective-permute-done.got_ref.later_ref.first1_ref, bf16[144,512]{1,0:T(8,128)(2,1)S(1)} %collective-permute-done.4.second_ref, ...), custom_call_target="tpu_custom_call" | custom-call | flops 50000000 | bytes 2000000 | tf_op jit(solution)/shard_map/pallas_call | solution.py:453
  18.9 0.0 collective-permute-done.2.second_ref
  18.9 0.9 %shard_map.80 = bf16[1,128,2048]{2,1,0:T(8,128)(2,1)} custom-call(bf16[128,512]{1,0:T(8,128)(2,1)S(1)} %collective-permute-done.2.second_ref, bf16[272,512]{1,0:T(8,128)(2,1)S(1)} %collective-permute-done.3.early_ref, f32[128,512]{1,0:T(8,128)S(1)} %get-tuple-element.67.base_ref, f32[8,512]{1,0:T(8,128)S(1)} %get-tuple-element.48.gates_ref, ...), custom_call_target="tpu_custom_call" | custom-call | flops 50000000 | bytes 2000000 | tf_op jit(solution)/shard_map/pallas_call | solution.py:453
Async XLA Ops:
  2.3 9.9 %collective-permute-start.1 = (bf16[144,512]{1,0:T(8,128)(2,1)S(1)}, bf16[144,512]{1,0:T(8,128)(2,1)S(1)}, u32[]{:S(2)}, u32[]{:S(2)}) collective-permute-start(bf16[144,512]{1,0:T(8,128)(2,1)S(1)} %get-tuple-element.42.before_ref.own_ref), channel_id=1, source_target_pairs={{0,2},{2,4},{4,6},{6,8},{8,10},{10,12},{12,14},{14,0},{1,3},{3,5},... | collective-permute-start | bytes 442376 | tf_op jit(solution)/shard_map/ppermute | solution.py:528
  5.9 12.4 %collective-permute-start.3 = (bf16[272,512]{1,0:T(8,128)(2,1)S(1)}, bf16[272,512]{1,0:T(8,128)(2,1)S(1)}, u32[]{:S(2)}, u32[]{:S(2)}) collective-permute-start(bf16[272,512]{1,0:T(8,128)(2,1)S(1)} %get-tuple-element.53), channel_id=1, source_target_pairs={{0,4},{1,5},{2,3},{3,2},{4,0},{5,1},{6,7},{7,6},{8,9},{9,8},{10,11... | collective-permute-start | bytes 835592 | tf_op jit(solution)/shard_map/ppermute | solution.py:474
  7.5 9.1 %collective-permute-start = (bf16[144,512]{1,0:T(8,128)(2,1)S(1)}, bf16[144,512]{1,0:T(8,128)(2,1)S(1)}, u32[]{:S(2)}, u32[]{:S(2)}) collective-permute-start(bf16[144,512]{1,0:T(8,128)(2,1)S(1)} %get-tuple-element.43.later_ref.own_ref), channel_id=1, source_target_pairs={{0,2},{2,4},{4,6},{6,8},{8,10},{10,12},{12,14},{14,0},{1,3},{3,5},... | collective-permute-start | bytes 442376 | tf_op jit(solution)/shard_map/ppermute | solution.py:542
  12.4 5.9 %collective-permute-start.4 = (bf16[144,512]{1,0:T(8,128)(2,1)S(1)}, bf16[144,512]{1,0:T(8,128)(2,1)S(1)}, u32[]{:S(2)}, u32[]{:S(2)}) collective-permute-start(bf16[144,512]{1,0:T(8,128)(2,1)S(1)} %get-tuple-element.54), channel_id=1, source_target_pairs={{0,1},{1,0},{2,6},{3,7},{4,8},{5,9},{6,10},{7,11},{8,12},{9,13},{1... | collective-permute-start | bytes 442376 | tf_op jit(solution)/shard_map/ppermute | solution.py:474
  16.9 2.0 %collective-permute-start.2 = (bf16[128,512]{1,0:T(8,128)(2,1)S(1)}, bf16[128,512]{1,0:T(8,128)(2,1)S(1)}, u32[]{:S(2)}, u32[]{:S(2)}) collective-permute-start(bf16[128,512]{1,0:T(8,128)(2,1)S(1)} %shard_map.77), channel_id=1, source_target_pairs={{0,1},{1,0},{2,6},{3,7},{4,8},{5,9},{6,10},{7,11},{8,12},{9,13},{1... | collective-permute-start | bytes 393224 | tf_op jit(solution)/shard_map/ppermute | solution.py:474

commit v4 on v3

--- a/solution.py
+++ b/solution.py
@@ -16,6 +16,7 @@
 GROUPED = BC_GROUPS * STATE
 CHUNKS = 2
 PADS = 4
+ORDER = (0, 1, 2, 5, 3, 4, 6)
 PER_CHUNK = BC_GROUPS // CHUNKS
 HALF = PER_CHUNK * WIDE
 ROWS = PER_CHUNK * STATE
@@ -111,26 +112,25 @@
     return weight_ref[...].astype(f32) * 0.5, bias_ref[...].astype(f32) * 0.5
 
 
-def chunk_states(chunk, x_of, key_x, weight, bias, kept, conv_ref, key_ref, sent_ref, pads_ref, wait):
+def chunk_states(chunk, x_ref, weight, bias, kept, conv_ref, key_ref, sent_ref, pads_ref):
     matrix = spread_matrix()
-    lanes = 128
-    j = VALUES // lanes + chunk
     clear(pads_ref)
-    key = conv_rows(key_x(), weight[:, j * lanes : (j + 1) * lanes], bias[j : j + 1], pads_ref.at[0]).astype(bf16)
+
+    def conv_tile(j):
+        cols = slice(j * 128, (j + 1) * 128)
+        return conv_rows(x_ref[:, cols].astype(f32), weight[:, cols], bias[j : j + 1], pads_ref.at[j % PADS])
+
+    key = conv_tile(VALUES // 128 + chunk).astype(bf16)
     key_ref[...] = key
     for index in range(PER_CHUNK):
         group = chunk * PER_CHUNK + index
         scale = spread(kept, group, matrix)
-        wait(index)
         parts = []
-        for i in range(WIDE // lanes):
-            local = index * WIDE + i * lanes
-            j = (chunk * HALF + local) // lanes
-            tile = conv_rows(
-                x_of(local), weight[:, j * lanes : (j + 1) * lanes], bias[j : j + 1], pads_ref.at[(j + 1) % PADS]
-            )
-            conv_ref[:, local : local + lanes] = tile.astype(bf16)
-            parts.append((tile * scale[:, i * lanes : (i + 1) * lanes]).astype(bf16))
+        for i in range(WIDE // 128):
+            local = index * WIDE + i * 128
+            tile = conv_tile((chunk * HALF + local) // 128)
+            conv_ref[:, local : local + 128] = tile.astype(bf16)
+            parts.append((tile * scale[:, i * 128 : (i + 1) * 128]).astype(bf16))
         state = dot(
             key[:, index * STATE : (index + 1) * STATE], jnp.concatenate(parts, axis=1), ((0,), (0,))
         )
@@ -139,32 +139,23 @@
 
 def first_kernel(
     lengths_hbm, x_hbm, step_hbm, weight_hbm, bias_hbm, rate_hbm, skip_hbm,
-    conv_ref, key_ref, cumulative_ref, kept_ref, sent_ref, later_ref, query_x_ref, weight_ref, bias_ref, step_ref,
-    skip_ref, gates_ref, head_ref,
-    lengths_ref, x_ref, key_x_ref, edges_ref, rate_ref, pads_ref, sems,
+    conv_ref, key_ref, cumulative_ref, kept_ref, sent_ref, x_ref, weight_ref, bias_ref, step_ref, skip_ref, gates_ref,
+    lengths_ref, rate_ref, pads_ref, sems,
 ):
     count = x_ref.shape[0]
-    keys_at = VALUES
     pairs = [
         (step_hbm.at[0], step_ref),
         (rate_hbm, rate_ref),
         (lengths_hbm, lengths_ref),
         (weight_hbm, weight_ref),
         (bias_hbm, bias_ref),
-        (x_hbm.at[0, :, pl.ds(keys_at, 128)], key_x_ref),
-        (x_hbm.at[0, :, pl.ds(0, WIDE)], x_ref.at[:, pl.ds(0, WIDE)]),
-        (x_hbm.at[0, :, pl.ds(WIDE, WIDE)], x_ref.at[:, pl.ds(WIDE, WIDE)]),
-        (x_hbm.at[0, pl.ds(0, 16), :], edges_ref.at[pl.ds(0, 16), :]),
-        (x_hbm.at[0, pl.ds(count - 16, 16), :], edges_ref.at[pl.ds(16, 16), :]),
-        (x_hbm.at[0, :, pl.ds(HALF, HALF)], later_ref.at[:, pl.ds(0, HALF)]),
-        (x_hbm.at[0, :, pl.ds(keys_at + 128, 128)], later_ref.at[:, pl.ds(HALF, 128)]),
-        (x_hbm.at[0, :, pl.ds(keys_at + GROUPED, GROUPED)], query_x_ref),
+        (x_hbm.at[0], x_ref),
         (skip_hbm, skip_ref),
     ]
     copies = [pltpu.make_async_copy(a, b, sems.at[i]) for i, (a, b) in enumerate(pairs)]
-    for copy in copies:
-        copy.start()
-    for copy in copies[:7]:
+    for i in ORDER:
+        copies[i].start()
+    for copy in copies[:3]:
         copy.wait()
     position = lax.axis_index("ctx")
     fresh = is_fresh(lengths_ref, position)
@@ -181,13 +172,12 @@
     lanes = iota((HEADS, count), 1)
     kept = jnp.where((lanes >= EDGE) | (fresh == 1), tail, 0.0)
     kept_ref[...] = kept
+    for copy in copies[3:6]:
+        copy.wait()
     weight, bias = half_taps(weight_ref, bias_ref)
     chunk_states(
         0,
-        lambda at: x_ref[:, at : at + 128].astype(f32),
-        lambda: key_x_ref[...].astype(f32),
-        weight, bias, kept, conv_ref, key_ref, sent_ref, pads_ref,
-        lambda index: copies[7].wait() if index else None,
+        x_ref, weight, bias, kept, conv_ref, key_ref, sent_ref, pads_ref,
     )
     scales = jnp.where(lanes == EDGE, jnp.exp(last), tail)
     high, low = halves(scales)
@@ -195,28 +185,21 @@
     picked = dot(high, (place == 0).astype(bf16), ((0,), (0,)))
     picked = picked + dot(low, (place == HEADS).astype(bf16), ((0,), (0,)))
     line = jnp.concatenate([picked[k : k + 1] for k in range(4)], axis=1)
-    copies[8].wait()
-    copies[9].wait()
-    tail_rows = to_rows(edges_ref[16:, :].astype(f32)[8:], 5)
+    tail_rows = to_rows(x_ref[count - 16 :, :].astype(f32)[8:], 5)
     tail_rows = jnp.where(iota((16, WIDE), 0) == 15, line, tail_rows)
     sent_ref[TAIL_AT : TAIL_AT + 16, :] = tail_rows.astype(bf16)
-    head_ref[...] = edges_ref[:16, :]
-    for copy in copies[10:]:
-        copy.wait()
+    copies[6].wait()
 
 
 def later_kernel(
-    x_ref, head_ref, weight_ref, bias_ref, kept_ref, before_ref, conv_ref, key_ref, sent_ref, early_ref, pads_ref
+    x_ref, weight_ref, bias_ref, kept_ref, before_ref, conv_ref, key_ref, sent_ref, early_ref, pads_ref
 ):
     weight, bias = half_taps(weight_ref, bias_ref)
     chunk_states(
         1,
-        lambda at: x_ref[:, at : at + 128].astype(f32),
-        lambda: x_ref[:, HALF : HALF + 128].astype(f32),
-        weight, bias, kept_ref[...], conv_ref, key_ref, sent_ref, pads_ref,
-        lambda index: None,
-    )
-    sent_ref[HEAD_AT : HEAD_AT + 16, :] = to_rows(head_ref[...].astype(f32)[:8], 0).astype(bf16)
+        x_ref, weight, bias, kept_ref[...], conv_ref, key_ref, sent_ref, pads_ref,
+    )
+    sent_ref[HEAD_AT : HEAD_AT + 16, :] = to_rows(x_ref[:16, :].astype(f32)[:8], 0).astype(bf16)
     early_ref[:ROWS, :] = before_ref[:ROWS, :]
     early_ref[ROWS : 2 * ROWS, :] = sent_ref[:ROWS, :]
     early_ref[2 * ROWS :, :] = before_ref[TAIL_AT : TAIL_AT + 16, :]
@@ -254,7 +237,7 @@
 
 
 def prepare_kernel(
-    own_ref, later_ref, query_x_ref, weight_ref, bias_ref, cumulative_ref, step_ref, skip_ref, gates_ref,
+    own_ref, later_ref, x_ref, weight_ref, bias_ref, cumulative_ref, step_ref, skip_ref, gates_ref,
     queries_ref, table_ref, known_ref, scale_ref, decay_ref, entry_ref, gain_ref, pads_ref,
 ):
     clear(pads_ref)
@@ -307,7 +290,7 @@
         cols = slice(first + i * 128, first + (i + 1) * 128)
         j = first // 128 + i
         tile = conv_rows(
-            query_x_ref[:, i * 128 : (i + 1) * 128].astype(f32), weight[:, cols], bias[j : j + 1, :], pads_ref.at[i]
+            x_ref[:, cols].astype(f32), weight[:, cols], bias[j : j + 1, :], pads_ref.at[i]
         )
         queries_ref[:, i * 128 : (i + 1) * 128] = tile.astype(bf16)
 
@@ -495,7 +478,7 @@
     )
     sds = jax.ShapeDtypeStruct
     pads = pltpu.VMEM((PADS, count + 8, 128), f32)
-    conv0, key0, cumulative, kept, own0, later_x, query_x, weight, bias, step, skip, gates, head = call(
+    conv0, key0, cumulative, kept, own0, x, weight, bias, step, skip, gates = call(
         first_kernel,
         (
             sds((count, HALF), bf16),
@@ -503,26 +486,21 @@
             sds((HEADS, count), f32),
             sds((HEADS, count), f32),
             sds((SENT, WIDE), bf16),
-            sds((count, HALF + 128), bf16),
-            sds((count, GROUPED), bf16),
+            sds((count, channels), bf16),
             sds(conv_weight.shape, bf16),
             sds((channels // 128, 128), bf16),
             sds((HEADS, count), f32),
             sds((1, HEADS), f32),
             sds((8, WIDE), f32),
-            sds((16, channels), bf16),
         ),
         [HBM] * 7,
         (40_000_000, 2_000_000),
         arguments,
         scratch=(
             pltpu.SMEM(lengths.shape, jnp.int32),
-            pltpu.VMEM((count, HALF), bf16),
-            pltpu.VMEM((count, 128), bf16),
-            pltpu.VMEM((32, channels), bf16),
             pltpu.VMEM((1, HEADS), f32),
             pads,
-            pltpu.SemaphoreType.DMA((14,)),
+            pltpu.SemaphoreType.DMA((7,)),
         ),
     )
     first0 = lax.ppermute(own0, "ctx", ring)
@@ -534,9 +512,9 @@
             sds((SENT, WIDE), bf16),
             sds((2 * ROWS + 16, WIDE), bf16),
         ),
-        [VMEM] * 6,
+        [VMEM] * 5,
         (40_000_000, 2_000_000),
-        (later_x, head, weight, bias, kept, own0),
+        (x, weight, bias, kept, own0),
         scratch=(pads,),
     )
     first1 = lax.ppermute(own1, "ctx", ring)
@@ -554,7 +532,7 @@
         ),
         [VMEM] * 9,
         (100_000_000, 1_000_000),
-        (own0, own1, query_x, weight, bias, cumulative, step, skip, gates),
+        (own0, own1, x, weight, bias, cumulative, step, skip, gates),
         scratch=(pads,),
     )
     sent0, edge = call(

time: 20.1 us -> 19.7 us (0.980)
  Pallas kernels: 7.77 us -> 7.35 us
    pallas_call x8, Pallas kernels: 7.77 us -> 7.35 us  [call(): pl.pallas_call(kernel, out_shape=outs, in_specs=in_specs, out_specs=out_s...]
  transfers between devices with their start and end apart: 5 -> 5, of which waited for: 2 -> 2; matrix products, arithmetic and copies ran while one was open for 0% -> 0% of each run, Pallas kernels for 23% -> 24%
where the time goes in v4:
time: 19.7 us; the launch traced here: 19.4 us
  Pallas kernels  7.35 us (37%)
  waiting for transfers between devices  7.19 us (36%)
  starting transfers between devices  4.78 us (24%)
    pallas_call x8, Pallas kernels, call(): pl.pallas_call(kernel, out_shape=outs, in_specs=in_specs, out_specs=out_s...  7.35 us
    ppermute x1, waiting for transfers between devices, shard_near(): first1 = lax.ppermute(own1, 'ctx', ring)  4.13 us
    ppermute x1, waiting for transfers between devices, shard_near(): first0 = lax.ppermute(own0, 'ctx', ring)  3.05 us
    ppermute x1, starting transfers between devices, shard_near(): first0 = lax.ppermute(own0, 'ctx', ring)  2.99 us
    ppermute x3, starting transfers between devices, permuted(): return lax.ppermute(array, ('ctx', 'lane'), table)  1.75 us
  transfers between devices with their start and end apart: 5, of which 2 were waited for; matrix products, arithmetic and copies ran while one was open for 0% of the time, Pallas kernels for 24%

profile of v4, /device:TPU:0, one launch (start us, length us, event | category | flops | bytes accessed | tf_op | source)
XLA Modules:
  0.0 19.4 jit_solution(9646927452705670972)
XLA Ops:
  0.0 1.8 %shard_map.73 = (bf16[128,1024]{1,0:T(8,128)(2,1)S(1)}, bf16[128,128]{1,0:T(8,128)(2,1)S(1)}, f32[64,128]{1,0:T(8,128)S(1)}, f32[64,128]{1,0:T(8,128)S(1)}, bf16...) custom-call(s32[1,4]{1,0:T(1,128)} %lengths_hbm.1, ...), custom_call_target="tpu_custom_call" | custom-call | flops 40000000 | bytes 2000000 | tf_op jit(solution)/shard_map/pallas_call | solution.py:436
  1.8 3.0 %collective-permute-start.1 = (bf16[144,512]{1,0:T(8,128)(2,1)S(1)}, bf16[144,512]{1,0:T(8,128)(2,1)S(1)}, u32[]{:S(2)}, u32[]{:S(2)}) collective-permute-start(bf16[144,512]{1,0:T(8,128)(2,1)S(1)} %get-tuple-element.39.before_ref.own_ref), channel_id=1, source_target_pairs={{0,2},{2,4},{4,6},{6,8},{8,10},{10,12},{12,14},{14,0},{1,3},{3,5},... | collective-permute-start | bytes 442376 | tf_op jit(solution)/shard_map/ppermute | solution.py:506
  4.8 0.6 %shard_map.74 = (bf16[128,1024]{1,0:T(8,128)(2,1)S(1)}, bf16[128,128]{1,0:T(8,128)(2,1)S(1)}, bf16[144,512]{1,0:T(8,128)(2,1)S(1)}, bf16[272,512]{1,0:T(8,128)(2,1)S(1)}) custom-call(bf16[128,2560]{1,0:T(8,128)(2,1)S(1)} %get-tuple-element.35.x_ref, bf16[4,2560]{1,0:T(4,128)(2,1)S(1)} %get-tuple-element.36.weight_ref, ...), custom_call_target="tpu_custom_call" | custom-call | flops 40000000 | bytes 2000000 | tf_op jit(solution)/shard_map/pallas_call | solution.py:436
  5.4 1.6 %collective-permute-start.3 = (bf16[272,512]{1,0:T(8,128)(2,1)S(1)}, bf16[272,512]{1,0:T(8,128)(2,1)S(1)}, u32[]{:S(2)}, u32[]{:S(2)}) collective-permute-start(bf16[272,512]{1,0:T(8,128)(2,1)S(1)} %get-tuple-element.49), channel_id=1, source_target_pairs={{0,4},{1,5},{2,3},{3,2},{4,0},{5,1},{6,7},{7,6},{8,9},{9,8},{10,11... | collective-permute-start | bytes 835592 | tf_op jit(solution)/shard_map/ppermute | solution.py:457
  7.1 0.0 collective-permute-start
  7.1 1.5 %shard_map.75 = (bf16[128,256]{1,0:T(8,128)(2,1)S(1)}, f32[7,16,512]{2,1,0:T(8,128)S(1)}, f32[16,512]{1,0:T(8,128)S(1)}, f32[8,2048]{1,0:T(8,128)S(1)}, f32[64,1...) custom-call(bf16[144,512]{1,0:T(8,128)(2,1)S(1)} %get-tuple-element.39.before_ref.own_ref, ...), custom_call_target="tpu_custom_call" | custom-call | flops 100000000 | bytes 1000000 | tf_op jit(solution)/shard_map/pallas_call | solution.py:436
  8.6 3.1 %collective-permute-done.1.got_ref.first0_ref = bf16[144,512]{1,0:T(8,128)(2,1)S(1)} collective-permute-done((bf16[144,512]{1,0:T(8,128)(2,1)S(1)}, bf16[144,512]{1,0:T(8,128)(2,1)S(1)}, u32[]{:S(2)}, u32[]{:S(2)}) %collective-permute-start.1) | collective-permute-done | bytes 147488 | tf_op jit(solution)/shard_map/ppermute | solution.py:506
  11.7 0.3 %shard_map.76 = (bf16[144,512]{1,0:T(8,128)(2,1)S(1)}, f32[8,2560]{1,0:T(8,128)S(1)}) custom-call(bf16[144,512]{1,0:T(8,128)(2,1)S(1)} %get-tuple-element.39.before_ref.own_ref, bf16[144,512]{1,0:T(8,128)(2,1)S(1)} %collective-permute-done.1.got_ref.first0_ref, f32[7,16,512]{2,1,0:T(8,128)S(1)} %get-tuple-element.46.table_ref, ...), custom_call_target="tpu_custom_call" | custom-call | flops 1000000 | bytes 1000000 | tf_op jit(solution)/shard_map/pallas_call | solution.py:436
  12.0 0.1 collective-permute-start.4
  12.0 4.1 %collective-permute-done.got_ref.later_ref.first1_ref = bf16[144,512]{1,0:T(8,128)(2,1)S(1)} collective-permute-done((bf16[144,512]{1,0:T(8,128)(2,1)S(1)}, bf16[144,512]{1,0:T(8,128)(2,1)S(1)}, u32[]{:S(2)}, u32[]{:S(2)}) %collective-permute-start) | collective-permute-done | bytes 147488 | tf_op jit(solution)/shard_map/ppermute | solution.py:520
  16.2 0.3 %shard_map.77 = bf16[128,512]{1,0:T(8,128)(2,1)S(1)} custom-call(bf16[144,512]{1,0:T(8,128)(2,1)S(1)} %get-tuple-element.40.later_ref.own_ref, bf16[144,512]{1,0:T(8,128)(2,1)S(1)} %collective-permute-done.got_ref.later_ref.first1_ref, f32[8,2048]{1,0:T(8,128)S(1)} %get-tuple-element.45.scale_ref, f32[8,2560]{1,0:T(8,128)S(1)} %get-tuple-element.48.edge_ref), custom_call_target="tpu_custom_call" | custom-call | flops 1000000 | bytes 1000000 | tf_op jit(solution)/shard_map/pallas_call | solution.py:436
  16.4 0.1 collective-permute-start.2
  16.5 1.4 %shard_map.78 = (f32[128,2048]{1,0:T(8,128)S(1)}, bf16[128,256]{1,0:T(8,128)(2,1)S(1)}, f32[16,512]{1,0:T(8,128)S(1)}, f32[8,2048]{1,0:T(8,128)S(1)}) custom-call(bf16[128,1024]{1,0:T(8,128)(2,1)S(1)} %get-tuple-element.51.conv0_ref, bf16[128,1024]{1,0:T(8,128)(2,1)S(1)} %get-tuple-element.52.conv1_ref, bf16[128,128]{1,0:T(8,128)(2,1)S(1)} %get-tuple-element.53.key0_ref, ...), custom_call_target="tpu_custom_call" | custom-call | flops 400000000 | bytes 4000000 | tf_op jit(solution)/shard_map/pallas_call | solution.py:436
  17.9 0.0 collective-permute-done.3.early_ref
  17.9 0.0 collective-permute-done.4.second_ref
  17.9 0.6 %shard_map.79 = (bf16[128,1024]{1,0:T(8,128)(2,1)S(1)}, f32[128,512]{1,0:T(8,128)S(1)}) custom-call(bf16[144,512]{1,0:T(8,128)(2,1)S(1)} %collective-permute-done.1.got_ref.first0_ref, bf16[144,512]{1,0:T(8,128)(2,1)S(1)} %collective-permute-done.got_ref.later_ref.first1_ref, bf16[144,512]{1,0:T(8,128)(2,1)S(1)} %collective-permute-done.4.second_ref, ...), custom_call_target="tpu_custom_call" | custom-call | flops 50000000 | bytes 2000000 | tf_op jit(solution)/shard_map/pallas_call | solution.py:436
  18.5 0.0 collective-permute-done.2.second_ref
  18.5 0.9 %shard_map.80 = bf16[1,128,2048]{2,1,0:T(8,128)(2,1)} custom-call(bf16[128,512]{1,0:T(8,128)(2,1)S(1)} %collective-permute-done.2.second_ref, bf16[272,512]{1,0:T(8,128)(2,1)S(1)} %collective-permute-done.3.early_ref, f32[128,512]{1,0:T(8,128)S(1)} %get-tuple-element.63.base_ref, f32[8,512]{1,0:T(8,128)S(1)} %get-tuple-element.44.gates_ref, ...), custom_call_target="tpu_custom_call" | custom-call | flops 50000000 | bytes 2000000 | tf_op jit(solution)/shard_map/pallas_call | solution.py:436
Async XLA Ops:
  1.8 9.9 %collective-permute-start.1 = (bf16[144,512]{1,0:T(8,128)(2,1)S(1)}, bf16[144,512]{1,0:T(8,128)(2,1)S(1)}, u32[]{:S(2)}, u32[]{:S(2)}) collective-permute-start(bf16[144,512]{1,0:T(8,128)(2,1)S(1)} %get-tuple-element.39.before_ref.own_ref), channel_id=1, source_target_pairs={{0,2},{2,4},{4,6},{6,8},{8,10},{10,12},{12,14},{14,0},{1,3},{3,5},... | collective-permute-start | bytes 442376 | tf_op jit(solution)/shard_map/ppermute | solution.py:506
  5.4 12.4 %collective-permute-start.3 = (bf16[272,512]{1,0:T(8,128)(2,1)S(1)}, bf16[272,512]{1,0:T(8,128)(2,1)S(1)}, u32[]{:S(2)}, u32[]{:S(2)}) collective-permute-start(bf16[272,512]{1,0:T(8,128)(2,1)S(1)} %get-tuple-element.49), channel_id=1, source_target_pairs={{0,4},{1,5},{2,3},{3,2},{4,0},{5,1},{6,7},{7,6},{8,9},{9,8},{10,11... | collective-permute-start | bytes 835592 | tf_op jit(solution)/shard_map/ppermute | solution.py:457
  7.1 9.1 %collective-permute-start = (bf16[144,512]{1,0:T(8,128)(2,1)S(1)}, bf16[144,512]{1,0:T(8,128)(2,1)S(1)}, u32[]{:S(2)}, u32[]{:S(2)}) collective-permute-start(bf16[144,512]{1,0:T(8,128)(2,1)S(1)} %get-tuple-element.40.later_ref.own_ref), channel_id=1, source_target_pairs={{0,2},{2,4},{4,6},{6,8},{8,10},{10,12},{12,14},{14,0},{1,3},{3,5},... | collective-permute-start | bytes 442376 | tf_op jit(solution)/shard_map/ppermute | solution.py:520
  12.0 5.9 %collective-permute-start.4 = (bf16[144,512]{1,0:T(8,128)(2,1)S(1)}, bf16[144,512]{1,0:T(8,128)(2,1)S(1)}, u32[]{:S(2)}, u32[]{:S(2)}) collective-permute-start(bf16[144,512]{1,0:T(8,128)(2,1)S(1)} %get-tuple-element.50), channel_id=1, source_target_pairs={{0,1},{1,0},{2,6},{3,7},{4,8},{5,9},{6,10},{7,11},{8,12},{9,13},{1... | collective-permute-start | bytes 442376 | tf_op jit(solution)/shard_map/ppermute | solution.py:457
  16.4 2.1 %collective-permute-start.2 = (bf16[128,512]{1,0:T(8,128)(2,1)S(1)}, bf16[128,512]{1,0:T(8,128)(2,1)S(1)}, u32[]{:S(2)}, u32[]{:S(2)}) collective-permute-start(bf16[128,512]{1,0:T(8,128)(2,1)S(1)} %shard_map.77), channel_id=1, source_target_pairs={{0,1},{1,0},{2,6},{3,7},{4,8},{5,9},{6,10},{7,11},{8,12},{9,13},{1... | collective-permute-start | bytes 393224 | tf_op jit(solution)/shard_map/ppermute | solution.py:457

commit v5 on v4

--- a/solution.py
+++ b/solution.py
@@ -137,9 +137,18 @@
         sent_ref[index * STATE : (index + 1) * STATE, :] = state.astype(bf16)
 
 
+def kept_weights(step, cumulative, goes_on):
+    count = step.shape[1]
+    last = cumulative[:, count - 1 :]
+    tail = step * jnp.exp(last - cumulative)
+    lanes = iota((HEADS, count), 1)
+    kept = jnp.where((lanes >= EDGE) | (goes_on < 0.5), tail, 0.0)
+    return kept, jnp.where(lanes == EDGE, jnp.exp(last), tail)
+
+
 def first_kernel(
     lengths_hbm, x_hbm, step_hbm, weight_hbm, bias_hbm, rate_hbm, skip_hbm,
-    conv_ref, key_ref, cumulative_ref, kept_ref, sent_ref, x_ref, weight_ref, bias_ref, step_ref, skip_ref, gates_ref,
+    conv_ref, key_ref, cumulative_ref, sent_ref, x_ref, weight_ref, bias_ref, step_ref, skip_ref, gates_ref,
     lengths_ref, rate_ref, pads_ref, sems,
 ):
     count = x_ref.shape[0]
@@ -167,11 +176,7 @@
     step = step_ref[...]
     cumulative = cumulative_of(step, rate_ref[...])
     cumulative_ref[...] = cumulative
-    last = cumulative[:, count - 1 :]
-    tail = step * jnp.exp(last - cumulative)
-    lanes = iota((HEADS, count), 1)
-    kept = jnp.where((lanes >= EDGE) | (fresh == 1), tail, 0.0)
-    kept_ref[...] = kept
+    kept = kept_weights(step, cumulative, goes_on)[0]
     for copy in copies[3:6]:
         copy.wait()
     weight, bias = half_taps(weight_ref, bias_ref)
@@ -179,27 +184,26 @@
         0,
         x_ref, weight, bias, kept, conv_ref, key_ref, sent_ref, pads_ref,
     )
-    scales = jnp.where(lanes == EDGE, jnp.exp(last), tail)
+    tail_rows = to_rows(x_ref[count - 16 :, :].astype(f32)[8:], 5)
+    sent_ref[TAIL_AT : TAIL_AT + 16, :] = tail_rows.astype(bf16)
+    copies[6].wait()
+
+
+def later_kernel(
+    x_ref, weight_ref, bias_ref, step_ref, cumulative_ref, gates_ref, before_ref,
+    conv_ref, key_ref, sent_ref, early_ref, pads_ref,
+):
+    weight, bias = half_taps(weight_ref, bias_ref)
+    kept, scales = kept_weights(step_ref[...], cumulative_ref[...], gates_ref[:1, :1])
+    chunk_states(1, x_ref, weight, bias, kept, conv_ref, key_ref, sent_ref, pads_ref)
     high, low = halves(scales)
     place = iota((HEADS, 128), 1) - iota((HEADS, 128), 0)
     picked = dot(high, (place == 0).astype(bf16), ((0,), (0,)))
     picked = picked + dot(low, (place == HEADS).astype(bf16), ((0,), (0,)))
     line = jnp.concatenate([picked[k : k + 1] for k in range(4)], axis=1)
-    tail_rows = to_rows(x_ref[count - 16 :, :].astype(f32)[8:], 5)
-    tail_rows = jnp.where(iota((16, WIDE), 0) == 15, line, tail_rows)
-    sent_ref[TAIL_AT : TAIL_AT + 16, :] = tail_rows.astype(bf16)
-    copies[6].wait()
-
-
-def later_kernel(
-    x_ref, weight_ref, bias_ref, kept_ref, before_ref, conv_ref, key_ref, sent_ref, early_ref, pads_ref
-):
-    weight, bias = half_taps(weight_ref, bias_ref)
-    chunk_states(
-        1,
-        x_ref, weight, bias, kept_ref[...], conv_ref, key_ref, sent_ref, pads_ref,
-    )
-    sent_ref[HEAD_AT : HEAD_AT + 16, :] = to_rows(x_ref[:16, :].astype(f32)[:8], 0).astype(bf16)
+    head_rows = to_rows(x_ref[:16, :].astype(f32)[:8], 0)
+    head_rows = jnp.where(iota((16, WIDE), 0) == 15, line, head_rows)
+    sent_ref[HEAD_AT : HEAD_AT + 16, :] = head_rows.astype(bf16)
     early_ref[:ROWS, :] = before_ref[:ROWS, :]
     early_ref[ROWS : 2 * ROWS, :] = sent_ref[:ROWS, :]
     early_ref[2 * ROWS :, :] = before_ref[TAIL_AT : TAIL_AT + 16, :]
@@ -230,14 +234,14 @@
     return dot(rows, matrix)[:8]
 
 
-def edge_scales(tail_rows):
-    line = tail_rows[15:16].astype(f32)
+def edge_scales(head_rows):
+    line = head_rows[15:16].astype(f32)
     rows = [line[:, k * 128 : (k + 1) * 128] for k in range(4)]
     return head_lanes(jnp.concatenate(rows + [jnp.zeros((12, 128), f32)], axis=0).astype(bf16))
 
 
 def prepare_kernel(
-    own_ref, later_ref, x_ref, weight_ref, bias_ref, cumulative_ref, step_ref, skip_ref, gates_ref,
+    later_ref, x_ref, weight_ref, bias_ref, cumulative_ref, step_ref, skip_ref, gates_ref,
     queries_ref, table_ref, known_ref, scale_ref, decay_ref, entry_ref, gain_ref, pads_ref,
 ):
     clear(pads_ref)
@@ -269,7 +273,7 @@
     table_ref[5] = jnp.where(third == 2, 0.0, taps[1])
     table_ref[6] = jnp.where(third == 0, taps[2], 0.0)
     known_ref[...] = known_part(later_ref[HEAD_AT : HEAD_AT + 16, :].astype(f32), table_ref)
-    scale_ref[...] = edge_scales(own_ref[TAIL_AT : TAIL_AT + 16, :]) * gates_ref[:1, :1]
+    scale_ref[...] = edge_scales(later_ref[HEAD_AT : HEAD_AT + 16, :]) * gates_ref[:1, :1]
     cumulative = cumulative_ref[...] * LOG2E
     across = cumulative - jnp.log2(step_ref[...])
     down = cumulative.T
@@ -302,40 +306,38 @@
     return dot(tile[:, (group % 2) * STATE : (group % 2 + 1) * STATE], written.astype(bf16), ((0,), (0,)))
 
 
-def combine_chunk(chunk, own_ref, got_ref, scale_ref, sent_ref, edge_of):
-    keys = edge_of(BC_GROUPS)
+def combine_chunk(own_ref, got_ref, decays, extras, sent_ref):
     for index in range(PER_CHUNK):
-        group = chunk * PER_CHUNK + index
         at = slice(index * STATE, (index + 1) * STATE)
-        scale = scale_ref[:, group * WIDE : (group + 1) * WIDE]
-        extra = edge_state(edge_of(group), keys, scale, group)
-        total = own_ref[at, :].astype(f32) + extra + scale[EDGE : EDGE + 1] * got_ref[at, :].astype(f32)
+        total = own_ref[at, :].astype(f32) + extras[index] + decays[index] * got_ref[at, :].astype(f32)
         sent_ref[at, :] = total.astype(bf16)
+
+
+def group_cols(group):
+    return slice(group * WIDE, (group + 1) * WIDE)
 
 
 def combine_first_kernel(own_ref, got_ref, table_ref, known_ref, gates_ref, scale_ref, sent_ref, edge_ref):
     tail_block = got_ref[TAIL_AT : TAIL_AT + 16, :].astype(f32) * gates_ref[:1, :]
     chunks = edge_rows(tail_block, known_ref[...], table_ref)
-    combine_chunk(0, own_ref, got_ref, scale_ref, sent_ref, lambda k: chunks[k])
+    scales = [scale_ref[:, group_cols(group)] for group in range(PER_CHUNK)]
+    extras = [edge_state(chunks[g], chunks[BC_GROUPS], scales[g], g) for g in range(PER_CHUNK)]
+    decays = [scale[EDGE : EDGE + 1] for scale in scales]
+    combine_chunk(own_ref, got_ref, decays, extras, sent_ref)
     sent_ref[ROWS:, :] = own_ref[TAIL_AT : TAIL_AT + 16, :]
     for k in range(5):
         edge_ref[:, k * WIDE : (k + 1) * WIDE] = chunks[k]
 
 
-def combine_later_kernel(own_ref, got_ref, scale_ref, edge_ref, sent_ref):
-    combine_chunk(
-        1, own_ref, got_ref, scale_ref, sent_ref, lambda k: edge_ref[:, k * WIDE : (k + 1) * WIDE]
-    )
-
-
-def diagonal_kernel(
-    conv0_ref, conv1_ref, key0_ref, key1_ref, raw_queries_ref, edge_ref, decay_ref, gain_ref,
-    got_ref, later_ref, table_ref, gates_ref,
-    diagonal_ref, queries_ref, known_ref, scale_ref,
-):
-    known_ref[...] = known_part(later_ref[HEAD_AT : HEAD_AT + 16, :].astype(f32), table_ref)
-    scale_ref[...] = edge_scales(got_ref[TAIL_AT : TAIL_AT + 16, :]) * gates_ref[1:2, :1]
-    count = conv0_ref.shape[0]
+def combine_later_kernel(own_ref, got_ref, scale_ref, extra_ref, sent_ref):
+    groups = range(PER_CHUNK, BC_GROUPS)
+    decays = [scale_ref[EDGE : EDGE + 1, group_cols(group)] for group in groups]
+    extras = [extra_ref[index * STATE : (index + 1) * STATE, :] for index in range(PER_CHUNK)]
+    combine_chunk(own_ref, got_ref, decays, extras, sent_ref)
+
+
+def diagonal_chunk(chunk, conv_ref, key_ref, raw_queries_ref, edge_ref, decay_ref, gain_ref, diagonal_ref, queries_ref):
+    count = conv_ref.shape[0]
     edge_row = iota((count, 128), 0) < EDGE
     lane_head = iota((count, 128), 1) // HEAD_DIM
 
@@ -345,42 +347,60 @@
         )
         return jnp.where(edge_row, rows, tile.astype(f32))
 
-    keys = [patched(ref[...], 16 + i).astype(bf16) for i, ref in enumerate((key0_ref, key1_ref))]
-    queries = [
-        patched(raw_queries_ref[:, i * 128 : (i + 1) * 128], 18 + i).astype(bf16) for i in range(2)
-    ]
-    for i in range(2):
-        queries_ref[:, i * 128 : (i + 1) * 128] = queries[i]
-    for group in range(BC_GROUPS):
-        part = slice((group % 2) * STATE, (group % 2 + 1) * STATE)
-        scores = dot(queries[group // 2][:, part], keys[group // 2][:, part], ((1,), (1,)))
-        conv_ref = (conv0_ref, conv1_ref)[group // PER_CHUNK]
-        for i in range(4):
-            j = group * 4 + i
-            cols = slice(j * 128, (j + 1) * 128)
-            at = (j * 128) % HALF
+    keys = patched(key_ref[...], VALUES // 128 + chunk).astype(bf16)
+    j = (VALUES + GROUPED) // 128 + chunk
+    queries = patched(raw_queries_ref[:, chunk * 128 : (chunk + 1) * 128], j).astype(bf16)
+    queries_ref[...] = queries
+    for index in range(PER_CHUNK):
+        part = slice(index * STATE, (index + 1) * STATE)
+        scores = dot(queries[:, part], keys[:, part], ((1,), (1,)))
+        for i in range(WIDE // 128):
+            at = index * WIDE + i * 128
+            j = (chunk * HALF + at) // 128
             values = patched(conv_ref[:, at : at + 128], j)
             weights, parts = [], []
             for k in range(4):
-                at = 4 * j + k
-                weights.append((decay_ref[at] * scores).astype(bf16))
+                weights.append((decay_ref[4 * j + k] * scores).astype(bf16))
                 parts.append(jnp.where(lane_head == k, values, 0.0).astype(bf16))
             total = dot(jnp.concatenate(weights, axis=1), jnp.concatenate(parts, axis=0))
-            diagonal_ref[:, cols] = total + gain_ref[:1, cols] * values
+            diagonal_ref[:, at : at + 128] = total + gain_ref[:1, j * 128 : (j + 1) * 128] * values
+
+
+def diagonal_first_kernel(
+    conv_ref, key_ref, raw_queries_ref, edge_ref, decay_ref, gain_ref, own_scale_ref,
+    diagonal_ref, queries_ref, extra_ref,
+):
+    keys = edge_ref[:, BC_GROUPS * WIDE :]
+    for index in range(PER_CHUNK):
+        group = PER_CHUNK + index
+        cols = group_cols(group)
+        extra_ref[index * STATE : (index + 1) * STATE, :] = edge_state(
+            edge_ref[:, cols], keys, own_scale_ref[:, cols], group
+        )
+    diagonal_chunk(0, conv_ref, key_ref, raw_queries_ref, edge_ref, decay_ref, gain_ref, diagonal_ref, queries_ref)
+
+
+def diagonal_later_kernel(
+    conv_ref, key_ref, raw_queries_ref, edge_ref, decay_ref, gain_ref, later_ref, table_ref, gates_ref,
+    diagonal_ref, queries_ref, known_ref, scale_ref,
+):
+    head_rows = later_ref[HEAD_AT : HEAD_AT + 16, :]
+    known_ref[...] = known_part(head_rows.astype(f32), table_ref)
+    scale_ref[...] = edge_scales(head_rows) * gates_ref[1:2, :1]
+    diagonal_chunk(1, conv_ref, key_ref, raw_queries_ref, edge_ref, decay_ref, gain_ref, diagonal_ref, queries_ref)
 
 
 def group_out(group, total, diagonal_ref, queries_ref, entry_ref):
-    cols = slice(group * WIDE, (group + 1) * WIDE)
-    low = (group % 2) * STATE
-    tile = queries_ref[:, (group // 2) * 128 : (group // 2 + 1) * 128]
-    carried = dot(tile[:, low : low + STATE], total.astype(bf16))
-    return (diagonal_ref[:, cols] + entry_ref[:, cols] * carried).astype(bf16)
+    index = group % PER_CHUNK
+    here = slice(index * WIDE, (index + 1) * WIDE)
+    carried = dot(queries_ref[:, index * STATE : (index + 1) * STATE], total.astype(bf16))
+    return (diagonal_ref[:, here] + entry_ref[:, group_cols(group)] * carried).astype(bf16)
 
 
 def finish_first_kernel(
     first0_ref, first1_ref, second_ref, early_ref, table_ref, known_ref, gates_ref, scale_ref, diagonal_ref,
     queries_ref, entry_ref,
-    out_ref, base_ref,
+    out_ref, base_ref, decay_ref,
 ):
     third = gates_ref[2:3, :] > 0.5
     kept = gates_ref[:1, :]
@@ -393,23 +413,22 @@
     for group in range(BC_GROUPS):
         chunk, index = divmod(group, PER_CHUNK)
         at = slice(index * STATE, (index + 1) * STATE)
-        scale = scale_ref[:, group * WIDE : (group + 1) * WIDE]
+        scale = scale_ref[:, group_cols(group)]
+        decay = scale[EDGE : EDGE + 1]
         first = (first0_ref, first1_ref)[chunk][at, :].astype(f32)
         total = first * kept + edge_state(chunks[group], chunks[BC_GROUPS], scale, group)
         if chunk == 0:
-            total = total + scale[EDGE : EDGE + 1] * second_of(index * STATE, index * STATE, STATE)
-            out_ref[:, group * WIDE : (group + 1) * WIDE] = group_out(
-                group, total, diagonal_ref, queries_ref, entry_ref
-            )
+            total = total + decay * second_of(index * STATE, index * STATE, STATE)
+            out_ref[:, group_cols(group)] = group_out(group, total, diagonal_ref, queries_ref, entry_ref)
         else:
-            base_ref[at, :] = total
+            early = early_ref[ROWS + index * STATE : ROWS + (index + 1) * STATE, :].astype(f32)
+            base_ref[at, :] = jnp.where(third, total + decay * early, total)
+            decay_ref[index * 8 : (index + 1) * 8, :] = jnp.where(third, 0.0, decay) + jnp.zeros((8, WIDE), f32)
 
 
 def finish_later_kernel(
-    second_ref, early_ref, base_ref, gates_ref, scale_ref, diagonal_ref, queries_ref, entry_ref, before_ref,
-    out_hbm, out_ref, sems,
+    second_ref, base_ref, decay_ref, diagonal_ref, queries_ref, entry_ref, before_ref, out_hbm, out_ref, sems
 ):
-    third = gates_ref[2:3, :] > 0.5
     copies = [
         pltpu.make_async_copy(before_ref, out_hbm.at[0, :, pl.ds(0, HALF)], sems.at[PER_CHUNK])
     ]
@@ -417,10 +436,8 @@
     for index in range(PER_CHUNK):
         group = PER_CHUNK + index
         at = slice(index * STATE, (index + 1) * STATE)
-        early = early_ref[ROWS + index * STATE : ROWS + (index + 1) * STATE, :].astype(f32)
-        second = jnp.where(third, early, second_ref[at, :].astype(f32))
-        decay = scale_ref[EDGE : EDGE + 1, group * WIDE : (group + 1) * WIDE]
-        total = base_ref[at, :] + decay * second
+        decay = decay_ref[index * 8 : index * 8 + 1, :]
+        total = base_ref[at, :] + decay * second_ref[at, :].astype(f32)
         here = pl.ds(index * WIDE, WIDE)
         out_ref[:, here] = group_out(group, total, diagonal_ref, queries_ref, entry_ref)
         copy = pltpu.make_async_copy(
@@ -478,12 +495,11 @@
     )
     sds = jax.ShapeDtypeStruct
     pads = pltpu.VMEM((PADS, count + 8, 128), f32)
-    conv0, key0, cumulative, kept, own0, x, weight, bias, step, skip, gates = call(
+    conv0, key0, cumulative, own0, x, weight, bias, step, skip, gates = call(
         first_kernel,
         (
             sds((count, HALF), bf16),
             sds((count, 128), bf16),
-            sds((HEADS, count), f32),
             sds((HEADS, count), f32),
             sds((SENT, WIDE), bf16),
             sds((count, channels), bf16),
@@ -512,9 +528,9 @@
             sds((SENT, WIDE), bf16),
             sds((2 * ROWS + 16, WIDE), bf16),
         ),
-        [VMEM] * 5,
+        [VMEM] * 7,
         (40_000_000, 2_000_000),
-        (x, weight, bias, kept, own0),
+        (x, weight, bias, step, cumulative, gates, own0),
         scratch=(pads,),
     )
     first1 = lax.ppermute(own1, "ctx", ring)
@@ -530,9 +546,9 @@
             sds((count, VALUES), f32),
             sds((8, VALUES), f32),
         ),
-        [VMEM] * 9,
+        [VMEM] * 8,
         (100_000_000, 1_000_000),
-        (own0, own1, x, weight, bias, cumulative, step, skip, gates),
+        (own1, x, weight, bias, cumulative, step, skip, gates),
         scratch=(pads,),
     )
     sent0, edge = call(
@@ -543,39 +559,42 @@
         (own0, first0, table, known, gates, scale),
     )
     second0 = permuted(sent0, onward)
+    diagonal_outs = (sds((count, HALF), f32), sds((count, 128), bf16))
+    diagonal0, queries0, extra = call(
+        diagonal_first_kernel,
+        diagonal_outs + (sds((ROWS, WIDE), f32),),
+        [VMEM] * 7,
+        (200_000_000, 2_000_000),
+        (conv0, key0, raw_queries, edge, decay, gain, scale),
+    )
     sent1 = call(
         combine_later_kernel,
         sds((ROWS, WIDE), bf16),
         [VMEM] * 4,
         (1_000_000, 1_000_000),
-        (own1, first1, scale, edge),
+        (own1, first1, scale, extra),
     )
     second1 = permuted(sent1, onward)
-    diagonal, queries, known, scale = call(
-        diagonal_kernel,
-        (
-            sds((count, VALUES), f32),
-            sds((count, GROUPED), bf16),
-            sds((16, WIDE), f32),
-            sds((8, VALUES), f32),
-        ),
-        [VMEM] * 12,
-        (400_000_000, 4_000_000),
-        (conv0, conv1, key0, key1, raw_queries, edge, decay, gain, first0, first1, table, gates),
-    )
-    out0, base = call(
+    diagonal1, queries1, known, scale = call(
+        diagonal_later_kernel,
+        diagonal_outs + (sds((16, WIDE), f32), sds((8, VALUES), f32)),
+        [VMEM] * 9,
+        (200_000_000, 2_000_000),
+        (conv1, key1, raw_queries, edge, decay, gain, first1, table, gates),
+    )
+    out0, base, decay = call(
         finish_first_kernel,
-        (sds((count, HALF), bf16), sds((ROWS, WIDE), f32)),
+        (sds((count, HALF), bf16), sds((ROWS, WIDE), f32), sds((8 * PER_CHUNK, WIDE), f32)),
         [VMEM] * 11,
         (50_000_000, 2_000_000),
-        (first0, first1, second0, early, table, known, gates, scale, diagonal, queries, entry),
+        (first0, first1, second0, early, table, known, gates, scale, diagonal0, queries0, entry),
     )
     return call(
         finish_later_kernel,
         sds((1, count, VALUES), bf16),
-        [VMEM] * 9,
+        [VMEM] * 7,
         (50_000_000, 2_000_000),
-        (second1, early, base, gates, scale, diagonal, queries, entry, out0),
+        (second1, base, decay, diagonal1, queries1, entry, out0),
         out_specs=HBM,
         scratch=(pltpu.VMEM((count, HALF), bf16), pltpu.SemaphoreType.DMA((PER_CHUNK + 1,))),
     )

time: 19.7 us -> 19.7 us (level)
  the two profiles are of different devices: /device:TPU:0 before, /device:TPU:2 now
where the time goes in v5:
time: 19.7 us; the launch traced here: 19.5 us
  Pallas kernels  7.5 us (38%)
  starting transfers between devices  6.79 us (34%)
  waiting for transfers between devices  5.15 us (26%)
    pallas_call x9, Pallas kernels, call(): pl.pallas_call(kernel, out_shape=outs, in_specs=in_specs, out_specs=out_s...  7.5 us
    ppermute x3, waiting for transfers between devices, permuted(): return lax.ppermute(array, ('ctx', 'lane'), table)  4.87 us
    ppermute x3, starting transfers between devices, permuted(): return lax.ppermute(array, ('ctx', 'lane'), table)  3.26 us
    ppermute x1, starting transfers between devices, shard_near(): first1 = lax.ppermute(own1, 'ctx', ring)  1.92 us
    ppermute x1, starting transfers between devices, shard_near(): first0 = lax.ppermute(own0, 'ctx', ring)  1.6 us
  transfers between devices with their start and end apart: 5, of which 3 were waited for; matrix products, arithmetic and copies ran while one was open for 0% of the time, Pallas kernels for 24%

profile of v5, /device:TPU:2, one launch (start us, length us, event | category | flops | bytes accessed | tf_op | source)
XLA Modules:
  0.0 19.5 jit_solution(4846205290403787416)
XLA Ops:
  0.0 1.8 %shard_map.73 = (bf16[128,1024]{1,0:T(8,128)(2,1)S(1)}, bf16[128,128]{1,0:T(8,128)(2,1)S(1)}, f32[64,128]{1,0:T(8,128)S(1)}, bf16[144,512]{1,0:T(8,128)(2,1)S(1)...) custom-call(s32[1,4]{1,0:T(1,128)} %lengths_hbm.1, ...), custom_call_target="tpu_custom_call" | custom-call | flops 40000000 | bytes 2000000 | tf_op jit(solution)/shard_map/pallas_call | solution.py:453
  1.9 1.6 %collective-permute-start.1 = (bf16[144,512]{1,0:T(8,128)(2,1)S(1)}, bf16[144,512]{1,0:T(8,128)(2,1)S(1)}, u32[]{:S(2)}, u32[]{:S(2)}) collective-permute-start(bf16[144,512]{1,0:T(8,128)(2,1)S(1)} %get-tuple-element.44.before_ref.own_ref), channel_id=1, source_target_pairs={{0,2},{2,4},{4,6},{6,8},{8,10},{10,12},{12,14},{14,0},{1,3},{3,5},... | collective-permute-start | bytes 442376 | tf_op jit(solution)/shard_map/ppermute | solution.py:522
  3.5 0.7 %shard_map.74 = (bf16[128,1024]{1,0:T(8,128)(2,1)S(1)}, bf16[128,128]{1,0:T(8,128)(2,1)S(1)}, bf16[144,512]{1,0:T(8,128)(2,1)S(1)}, bf16[272,512]{1,0:T(8,128)(2,1)S(1)}) custom-call(bf16[128,2560]{1,0:T(8,128)(2,1)S(1)} %get-tuple-element.38.x_ref, bf16[4,2560]{1,0:T(4,128)(2,1)S(1)} %get-tuple-element.39.weight_ref, ...), custom_call_target="tpu_custom_call" | custom-call | flops 40000000 | bytes 2000000 | tf_op jit(solution)/shard_map/pallas_call | solution.py:453
  4.1 0.1 collective-permute-start.4
  4.2 1.9 %collective-permute-start = (bf16[144,512]{1,0:T(8,128)(2,1)S(1)}, bf16[144,512]{1,0:T(8,128)(2,1)S(1)}, u32[]{:S(2)}, u32[]{:S(2)}) collective-permute-start(bf16[144,512]{1,0:T(8,128)(2,1)S(1)} %get-tuple-element.45.later_ref.own_ref), channel_id=1, source_target_pairs={{0,2},{2,4},{4,6},{6,8},{8,10},{10,12},{12,14},{14,0},{1,3},{3,5},... | collective-permute-start | bytes 442376 | tf_op jit(solution)/shard_map/ppermute | solution.py:536
  6.1 1.5 %shard_map.75 = (bf16[128,256]{1,0:T(8,128)(2,1)S(1)}, f32[7,16,512]{2,1,0:T(8,128)S(1)}, f32[16,512]{1,0:T(8,128)S(1)}, f32[8,2048]{1,0:T(8,128)S(1)}, f32[64,1...) custom-call(bf16[144,512]{1,0:T(8,128)(2,1)S(1)} %get-tuple-element.45.later_ref.own_ref, ...), custom_call_target="tpu_custom_call" | custom-call | flops 100000000 | bytes 1000000 | tf_op jit(solution)/shard_map/pallas_call | solution.py:453
  7.7 0.0 collective-permute-done.1.got_ref.first0_ref
  7.7 0.3 %shard_map.76 = (bf16[144,512]{1,0:T(8,128)(2,1)S(1)}, f32[8,2560]{1,0:T(8,128)S(1)}) custom-call(bf16[144,512]{1,0:T(8,128)(2,1)S(1)} %get-tuple-element.44.before_ref.own_ref, bf16[144,512]{1,0:T(8,128)(2,1)S(1)} %collective-permute-done.1.got_ref.first0_ref, f32[7,16,512]{2,1,0:T(8,128)S(1)} %get-tuple-element.51.table_ref, ...), custom_call_target="tpu_custom_call" | custom-call | flops 1000000 | bytes 1000000 | tf_op jit(solution)/shard_map/pallas_call | solution.py:453
  7.9 1.6 %collective-permute-start.3 = (bf16[144,512]{1,0:T(8,128)(2,1)S(1)}, bf16[144,512]{1,0:T(8,128)(2,1)S(1)}, u32[]{:S(2)}, u32[]{:S(2)}) collective-permute-start(bf16[144,512]{1,0:T(8,128)(2,1)S(1)} %get-tuple-element.57), channel_id=1, source_target_pairs={{0,1},{1,0},{2,6},{3,7},{4,8},{5,9},{6,10},{7,11},{8,12},{9,13},{1... | collective-permute-start | bytes 442376 | tf_op jit(solution)/shard_map/ppermute | solution.py:474
  9.5 0.9 %shard_map.77 = (f32[128,1024]{1,0:T(8,128)S(1)}, bf16[128,128]{1,0:T(8,128)(2,1)S(1)}, f32[128,512]{1,0:T(8,128)S(1)}) custom-call(bf16[128,1024]{1,0:T(8,128)(2,1)S(1)} %get-tuple-element.48.conv_ref, bf16[128,128]{1,0:T(8,128)(2,1)S(1)} %get-tuple-element.49.key_ref, bf16[128,256]{1,0:T(8,128)(2,1)S(1)} %get-tuple-element.50.raw_queries_ref, ...), custom_call_target="tpu_custom_call" | custom-call | flops 200000000 | bytes 2000000 | tf_op jit(solution)/shard_map/pallas_call | solution.py:453
  10.4 0.3 %collective-permute-done.got_ref.later_ref.first1_ref = bf16[144,512]{1,0:T(8,128)(2,1)S(1)} collective-permute-done((bf16[144,512]{1,0:T(8,128)(2,1)S(1)}, bf16[144,512]{1,0:T(8,128)(2,1)S(1)}, u32[]{:S(2)}, u32[]{:S(2)}) %collective-permute-start) | collective-permute-done | bytes 147488 | tf_op jit(solution)/shard_map/ppermute | solution.py:536
  10.7 0.1 shard_map.78
  10.7 1.6 %collective-permute-start.2 = (bf16[128,512]{1,0:T(8,128)(2,1)S(1)}, bf16[128,512]{1,0:T(8,128)(2,1)S(1)}, u32[]{:S(2)}, u32[]{:S(2)}) collective-permute-start(bf16[128,512]{1,0:T(8,128)(2,1)S(1)} %shard_map.78), channel_id=1, source_target_pairs={{0,1},{1,0},{2,6},{3,7},{4,8},{5,9},{6,10},{7,11},{8,12},{9,13},{1... | collective-permute-start | bytes 393224 | tf_op jit(solution)/shard_map/ppermute | solution.py:474
  12.3 0.8 %shard_map.79 = (f32[128,1024]{1,0:T(8,128)S(1)}, bf16[128,128]{1,0:T(8,128)(2,1)S(1)}, f32[16,512]{1,0:T(8,128)S(1)}, f32[8,2048]{1,0:T(8,128)S(1)}) custom-call(bf16[128,1024]{1,0:T(8,128)(2,1)S(1)} %get-tuple-element.59.conv_ref, bf16[128,128]{1,0:T(8,128)(2,1)S(1)} %get-tuple-element.60.key_ref, bf16[128,256]{1,0:T(8,128)(2,1)S(1)} %get-tuple-element.50.raw_queries_ref, ...), custom_call_target="tpu_custom_call" | custom-call | flops 200000000 | bytes 2000000 | tf_op jit(solution)/shard_map/pallas_call | solution.py:453
  13.1 0.0 collective-permute-done.4.early_ref
  13.1 3.6 %collective-permute-done.3.second_ref = bf16[144,512]{1,0:T(8,128)(2,1)S(1)} collective-permute-done((bf16[144,512]{1,0:T(8,128)(2,1)S(1)}, bf16[144,512]{1,0:T(8,128)(2,1)S(1)}, u32[]{:S(2)}, u32[]{:S(2)}) %collective-permute-start.3) | collective-permute-done | bytes 147488 | tf_op jit(solution)/shard_map/ppermute | solution.py:474
  16.7 0.6 %shard_map.80 = (bf16[128,1024]{1,0:T(8,128)(2,1)S(1)}, f32[128,512]{1,0:T(8,128)S(1)}, f32[16,512]{1,0:T(8,128)S(1)}) custom-call(bf16[144,512]{1,0:T(8,128)(2,1)S(1)} %collective-permute-done.1.got_ref.first0_ref, bf16[144,512]{1,0:T(8,128)(2,1)S(1)} %collective-permute-done.got_ref.later_ref.first1_ref, ...), custom_call_target="tpu_custom_call" | custom-call | flops 50000000 | bytes 2000000 | tf_op jit(solution)/shard_map/pallas_call | solution.py:453
  17.3 1.3 %collective-permute-done.2.second_ref = bf16[128,512]{1,0:T(8,128)(2,1)S(1)} collective-permute-done((bf16[128,512]{1,0:T(8,128)(2,1)S(1)}, bf16[128,512]{1,0:T(8,128)(2,1)S(1)}, u32[]{:S(2)}, u32[]{:S(2)}) %collective-permute-start.2) | collective-permute-done | bytes 131104 | tf_op jit(solution)/shard_map/ppermute | solution.py:474
  18.6 0.9 %shard_map.81 = bf16[1,128,2048]{2,1,0:T(8,128)(2,1)} custom-call(bf16[128,512]{1,0:T(8,128)(2,1)S(1)} %collective-permute-done.2.second_ref, f32[128,512]{1,0:T(8,128)S(1)} %get-tuple-element.66.base_ref, f32[16,512]{1,0:T(8,128)S(1)} %get-tuple-element.67.decay_ref, f32[128,1024]{1,0:T(8,128)S(1)} %get-tuple-element.68.diagonal_ref, ...), custom_call_target="tpu_custom_call" | custom-call | flops 50000000 | bytes 2000000 | tf_op jit(solution)/shard_map/pallas_call | solution.py:453
Async XLA Ops:
  1.9 5.8 %collective-permute-start.1 = (bf16[144,512]{1,0:T(8,128)(2,1)S(1)}, bf16[144,512]{1,0:T(8,128)(2,1)S(1)}, u32[]{:S(2)}, u32[]{:S(2)}) collective-permute-start(bf16[144,512]{1,0:T(8,128)(2,1)S(1)} %get-tuple-element.44.before_ref.own_ref), channel_id=1, source_target_pairs={{0,2},{2,4},{4,6},{6,8},{8,10},{10,12},{12,14},{14,0},{1,3},{3,5},... | collective-permute-start | bytes 442376 | tf_op jit(solution)/shard_map/ppermute | solution.py:522
  4.1 9.0 %collective-permute-start.4 = (bf16[272,512]{1,0:T(8,128)(2,1)S(1)}, bf16[272,512]{1,0:T(8,128)(2,1)S(1)}, u32[]{:S(2)}, u32[]{:S(2)}) collective-permute-start(bf16[272,512]{1,0:T(8,128)(2,1)S(1)} %get-tuple-element.58), channel_id=1, source_target_pairs={{0,4},{1,5},{2,3},{3,2},{4,0},{5,1},{6,7},{7,6},{8,9},{9,8},{10,11... | collective-permute-start | bytes 835592 | tf_op jit(solution)/shard_map/ppermute | solution.py:474
  4.2 6.4 %collective-permute-start = (bf16[144,512]{1,0:T(8,128)(2,1)S(1)}, bf16[144,512]{1,0:T(8,128)(2,1)S(1)}, u32[]{:S(2)}, u32[]{:S(2)}) collective-permute-start(bf16[144,512]{1,0:T(8,128)(2,1)S(1)} %get-tuple-element.45.later_ref.own_ref), channel_id=1, source_target_pairs={{0,2},{2,4},{4,6},{6,8},{8,10},{10,12},{12,14},{14,0},{1,3},{3,5},... | collective-permute-start | bytes 442376 | tf_op jit(solution)/shard_map/ppermute | solution.py:536
  7.9 8.8 %collective-permute-start.3 = (bf16[144,512]{1,0:T(8,128)(2,1)S(1)}, bf16[144,512]{1,0:T(8,128)(2,1)S(1)}, u32[]{:S(2)}, u32[]{:S(2)}) collective-permute-start(bf16[144,512]{1,0:T(8,128)(2,1)S(1)} %get-tuple-element.57), channel_id=1, source_target_pairs={{0,1},{1,0},{2,6},{3,7},{4,8},{5,9},{6,10},{7,11},{8,12},{9,13},{1... | collective-permute-start | bytes 442376 | tf_op jit(solution)/shard_map/ppermute | solution.py:474
  10.7 7.9 %collective-permute-start.2 = (bf16[128,512]{1,0:T(8,128)(2,1)S(1)}, bf16[128,512]{1,0:T(8,128)(2,1)S(1)}, u32[]{:S(2)}, u32[]{:S(2)}) collective-permute-start(bf16[128,512]{1,0:T(8,128)(2,1)S(1)} %shard_map.78), channel_id=1, source_target_pairs={{0,1},{1,0},{2,6},{3,7},{4,8},{5,9},{6,10},{7,11},{8,12},{9,13},{1... | collective-permute-start | bytes 393224 | tf_op jit(solution)/shard_map/ppermute | solution.py:474

commit v6 on v5

--- a/solution.py
+++ b/solution.py
@@ -23,6 +23,7 @@
 TAIL_AT = ROWS
 HEAD_AT = ROWS
 SENT = ROWS + 16
+LAST_LOW = 2
 LOG2E = 1.4426950408889634
 VMEM = pl.BlockSpec(memory_space=pltpu.VMEM)
 HBM = pl.BlockSpec(memory_space=pltpu.HBM)
@@ -381,14 +382,25 @@
 
 
 def diagonal_later_kernel(
-    conv_ref, key_ref, raw_queries_ref, edge_ref, decay_ref, gain_ref, later_ref, table_ref, gates_ref,
-    diagonal_ref, queries_ref, known_ref, scale_ref,
+    conv_ref, key_ref, raw_queries_ref, edge_ref, decay_ref, gain_ref, later_ref, table_ref, gates_ref, before_ref,
+    diagonal_ref, queries_ref, known_ref, scale_ref, out_hbm, out_ref, sems,
 ):
     head_rows = later_ref[HEAD_AT : HEAD_AT + 16, :]
     known_ref[...] = known_part(head_rows.astype(f32), table_ref)
     scale_ref[...] = edge_scales(head_rows) * gates_ref[1:2, :1]
     diagonal_chunk(1, conv_ref, key_ref, raw_queries_ref, edge_ref, decay_ref, gain_ref, diagonal_ref, queries_ref)
 
+    @pl.when(lax.axis_index("ctx") == 0)
+    def _():
+        copies = []
+        for chunk, ref in enumerate((before_ref, diagonal_ref)):
+            here = pl.ds(chunk * HALF, HALF)
+            out_ref[:, here] = ref[...].astype(bf16)
+            copies.append(pltpu.make_async_copy(out_ref.at[:, here], out_hbm.at[0, :, here], sems.at[chunk]))
+            copies[-1].start()
+        for copy in copies:
+            copy.wait()
+
 
 def group_out(group, total, diagonal_ref, queries_ref, entry_ref):
     index = group % PER_CHUNK
@@ -399,63 +411,86 @@
 
 def finish_first_kernel(
     first0_ref, first1_ref, second_ref, early_ref, table_ref, known_ref, gates_ref, scale_ref, diagonal_ref,
-    queries_ref, entry_ref,
-    out_ref, base_ref, decay_ref,
+    queries_ref, later_diagonal_ref, later_queries_ref, entry_ref, done_hbm,
+    out_hbm, out_ref, base_ref, decay_ref, later_ref, sems,
 ):
-    third = gates_ref[2:3, :] > 0.5
-    kept = gates_ref[:1, :]
-
-    def second_of(at, early_at, rows):
-        a = second_ref[at : at + rows, :].astype(f32)
-        return jnp.where(third, early_ref[early_at : early_at + rows, :].astype(f32), a)
-
-    chunks = edge_rows(second_of(ROWS, 2 * ROWS, 16), known_ref[...], table_ref)
-    for group in range(BC_GROUPS):
-        chunk, index = divmod(group, PER_CHUNK)
-        at = slice(index * STATE, (index + 1) * STATE)
-        scale = scale_ref[:, group_cols(group)]
-        decay = scale[EDGE : EDGE + 1]
-        first = (first0_ref, first1_ref)[chunk][at, :].astype(f32)
-        total = first * kept + edge_state(chunks[group], chunks[BC_GROUPS], scale, group)
-        if chunk == 0:
-            total = total + decay * second_of(index * STATE, index * STATE, STATE)
-            out_ref[:, group_cols(group)] = group_out(group, total, diagonal_ref, queries_ref, entry_ref)
-        else:
-            early = early_ref[ROWS + index * STATE : ROWS + (index + 1) * STATE, :].astype(f32)
-            base_ref[at, :] = jnp.where(third, total + decay * early, total)
-            decay_ref[index * 8 : (index + 1) * 8, :] = jnp.where(third, 0.0, decay) + jnp.zeros((8, WIDE), f32)
+    position = lax.axis_index("ctx")
+
+    @pl.when(position > 0)
+    def _():
+        third = gates_ref[2:3, :] > 0.5
+        kept = gates_ref[:1, :]
+
+        def second_of(at, early_at, rows):
+            a = second_ref[at : at + rows, :].astype(f32)
+            return jnp.where(third, early_ref[early_at : early_at + rows, :].astype(f32), a)
+
+        chunks = edge_rows(second_of(ROWS, 2 * ROWS, 16), known_ref[...], table_ref)
+        for group in range(BC_GROUPS):
+            chunk, index = divmod(group, PER_CHUNK)
+            at = slice(index * STATE, (index + 1) * STATE)
+            scale = scale_ref[:, group_cols(group)]
+            decay = scale[EDGE : EDGE + 1]
+            first = (first0_ref, first1_ref)[chunk][at, :].astype(f32)
+            total = first * kept + edge_state(chunks[group], chunks[BC_GROUPS], scale, group)
+            if chunk == 0:
+                total = total + decay * second_of(index * STATE, index * STATE, STATE)
+                out_ref[:, group_cols(group)] = group_out(group, total, diagonal_ref, queries_ref, entry_ref)
+            else:
+                early = early_ref[ROWS + index * STATE : ROWS + (index + 1) * STATE, :].astype(f32)
+                base_ref[at, :] = jnp.where(third, total + decay * early, total)
+                decay_ref[index * 8 : (index + 1) * 8, :] = jnp.where(third, 0.0, decay) + jnp.zeros((8, WIDE), f32)
+
+    @pl.when((position > 0) & (position <= LAST_LOW))
+    def _():
+        copies = [
+            pltpu.make_async_copy(out_ref, out_hbm.at[0, :, pl.ds(0, HALF)], sems.at[0]),
+            pltpu.make_async_copy(later_ref, out_hbm.at[0, :, pl.ds(HALF, HALF)], sems.at[1]),
+        ]
+        copies[0].start()
+        for index in range(PER_CHUNK):
+            at = slice(index * STATE, (index + 1) * STATE)
+            later_ref[:, index * WIDE : (index + 1) * WIDE] = group_out(
+                PER_CHUNK + index, base_ref[at, :], later_diagonal_ref, later_queries_ref, entry_ref
+            )
+        copies[1].start()
+        for copy in copies:
+            copy.wait()
 
 
 def finish_later_kernel(
-    second_ref, base_ref, decay_ref, diagonal_ref, queries_ref, entry_ref, before_ref, out_hbm, out_ref, sems
+    second_ref, base_ref, decay_ref, diagonal_ref, queries_ref, entry_ref, before_ref, done_hbm, out_hbm, out_ref, sems
 ):
-    copies = [
-        pltpu.make_async_copy(before_ref, out_hbm.at[0, :, pl.ds(0, HALF)], sems.at[PER_CHUNK])
-    ]
-    copies[0].start()
-    for index in range(PER_CHUNK):
-        group = PER_CHUNK + index
-        at = slice(index * STATE, (index + 1) * STATE)
-        decay = decay_ref[index * 8 : index * 8 + 1, :]
-        total = base_ref[at, :] + decay * second_ref[at, :].astype(f32)
-        here = pl.ds(index * WIDE, WIDE)
-        out_ref[:, here] = group_out(group, total, diagonal_ref, queries_ref, entry_ref)
-        copy = pltpu.make_async_copy(
-            out_ref.at[:, here], out_hbm.at[0, :, pl.ds(group * WIDE, WIDE)], sems.at[index]
-        )
-        copy.start()
-        copies.append(copy)
-    for copy in copies:
-        copy.wait()
-
-
-def call(kernel, outs, in_specs, cost, args, out_specs=None, scratch=()):
+    @pl.when(lax.axis_index("ctx") > LAST_LOW)
+    def _():
+        copies = [
+            pltpu.make_async_copy(before_ref, out_hbm.at[0, :, pl.ds(0, HALF)], sems.at[PER_CHUNK])
+        ]
+        copies[0].start()
+        for index in range(PER_CHUNK):
+            group = PER_CHUNK + index
+            at = slice(index * STATE, (index + 1) * STATE)
+            decay = decay_ref[index * 8 : index * 8 + 1, :]
+            total = base_ref[at, :] + decay * second_ref[at, :].astype(f32)
+            here = pl.ds(index * WIDE, WIDE)
+            out_ref[:, here] = group_out(group, total, diagonal_ref, queries_ref, entry_ref)
+            copy = pltpu.make_async_copy(
+                out_ref.at[:, here], out_hbm.at[0, :, pl.ds(group * WIDE, WIDE)], sems.at[index]
+            )
+            copy.start()
+            copies.append(copy)
+        for copy in copies:
+            copy.wait()
+
+
+def call(kernel, outs, in_specs, cost, args, out_specs=None, scratch=(), aliases={}):
     return pl.pallas_call(
         kernel,
         out_shape=outs,
         in_specs=in_specs,
         out_specs=out_specs or jax.tree.map(lambda _: VMEM, outs),
         scratch_shapes=scratch,
+        input_output_aliases=aliases,
         compiler_params=pltpu.CompilerParams(vmem_limit_bytes=24 * 1024 * 1024),
         cost_estimate=pl.CostEstimate(flops=cost[0], bytes_accessed=cost[1], transcendentals=0),
     )(*args)
@@ -575,28 +610,43 @@
         (own1, first1, scale, extra),
     )
     second1 = permuted(sent1, onward)
-    diagonal1, queries1, known, scale = call(
+    out_shape = sds((1, count, VALUES), bf16)
+    diagonal1, queries1, known, scale, out = call(
         diagonal_later_kernel,
-        diagonal_outs + (sds((16, WIDE), f32), sds((8, VALUES), f32)),
-        [VMEM] * 9,
+        diagonal_outs + (sds((16, WIDE), f32), sds((8, VALUES), f32), out_shape),
+        [VMEM] * 10,
         (200_000_000, 2_000_000),
-        (conv1, key1, raw_queries, edge, decay, gain, first1, table, gates),
-    )
-    out0, base, decay = call(
+        (conv1, key1, raw_queries, edge, decay, gain, first1, table, gates, diagonal0),
+        out_specs=(VMEM, VMEM, VMEM, VMEM, HBM),
+        scratch=(pltpu.VMEM((count, VALUES), bf16), pltpu.SemaphoreType.DMA((CHUNKS,))),
+    )
+    out, out0, base, decay = call(
         finish_first_kernel,
-        (sds((count, HALF), bf16), sds((ROWS, WIDE), f32), sds((8 * PER_CHUNK, WIDE), f32)),
-        [VMEM] * 11,
+        (
+            out_shape,
+            sds((count, HALF), bf16),
+            sds((ROWS, WIDE), f32),
+            sds((8 * PER_CHUNK, WIDE), f32),
+        ),
+        [VMEM] * 13 + [HBM],
         (50_000_000, 2_000_000),
-        (first0, first1, second0, early, table, known, gates, scale, diagonal0, queries0, entry),
+        (
+            first0, first1, second0, early, table, known, gates, scale,
+            diagonal0, queries0, diagonal1, queries1, entry, out,
+        ),
+        out_specs=(HBM, VMEM, VMEM, VMEM),
+        scratch=(pltpu.VMEM((count, HALF), bf16), pltpu.SemaphoreType.DMA((2,))),
+        aliases={13: 0},
     )
     return call(
         finish_later_kernel,
-        sds((1, count, VALUES), bf16),
-        [VMEM] * 7,
+        out_shape,
+        [VMEM] * 7 + [HBM],
         (50_000_000, 2_000_000),
-        (second1, base, decay, diagonal1, queries1, entry, out0),
+        (second1, base, decay, diagonal1, queries1, entry, out0, out),
         out_specs=HBM,
         scratch=(pltpu.VMEM((count, HALF), bf16), pltpu.SemaphoreType.DMA((PER_CHUNK + 1,))),
+        aliases={7: 0},
     )
 
 

time: 19.7 us -> 18.8 us (0.954)
  waiting for transfers between devices: 5.15 us -> 4.2 us
    ppermute x3, waiting for transfers between devices: 4.87 us -> 3.91 us  [permuted(): return lax.ppermute(array, ('ctx', 'lane'), table)]
  transfers between devices with their start and end apart: 5 -> 5, of which waited for: 3 -> 3; matrix products, arithmetic and copies ran while one was open for 0% -> 0% of each run, Pallas kernels for 24% -> 31%
where the time goes in v6:
time: 18.8 us; the launch traced here: 18.6 us
  Pallas kernels  7.56 us (40%)
  starting transfers between devices  6.79 us (36%)
  waiting for transfers between devices  4.2 us (22%)
    pallas_call x9, Pallas kernels, call(): pl.pallas_call(kernel, out_shape=outs, in_specs=in_specs, out_specs=out_s...  7.56 us
    ppermute x3, waiting for transfers between devices, permuted(): return lax.ppermute(array, ('ctx', 'lane'), table)  3.91 us
    ppermute x3, starting transfers between devices, permuted(): return lax.ppermute(array, ('ctx', 'lane'), table)  3.27 us
    ppermute x1, starting transfers between devices, shard_near(): first1 = lax.ppermute(own1, 'ctx', ring)  1.92 us
    ppermute x1, starting transfers between devices, shard_near(): first0 = lax.ppermute(own0, 'ctx', ring)  1.6 us
  transfers between devices with their start and end apart: 5, of which 3 were waited for; matrix products, arithmetic and copies ran while one was open for 0% of the time, Pallas kernels for 31%

profile of v6, /device:TPU:2, one launch (start us, length us, event | category | flops | bytes accessed | tf_op | source)
XLA Modules:
  0.0 18.6 jit_solution(6278207668456535384)
XLA Ops:
  0.0 1.8 %shard_map.73 = (bf16[128,1024]{1,0:T(8,128)(2,1)S(1)}, bf16[128,128]{1,0:T(8,128)(2,1)S(1)}, f32[64,128]{1,0:T(8,128)S(1)}, bf16[144,512]{1,0:T(8,128)(2,1)S(1)...) custom-call(s32[1,4]{1,0:T(1,128)} %lengths_hbm.1, ...), custom_call_target="tpu_custom_call" | custom-call | flops 40000000 | bytes 2000000 | tf_op jit(solution)/shard_map/pallas_call | solution.py:487
  1.9 1.6 %collective-permute-start.1 = (bf16[144,512]{1,0:T(8,128)(2,1)S(1)}, bf16[144,512]{1,0:T(8,128)(2,1)S(1)}, u32[]{:S(2)}, u32[]{:S(2)}) collective-permute-start(bf16[144,512]{1,0:T(8,128)(2,1)S(1)} %get-tuple-element.46.before_ref.own_ref), channel_id=1, source_target_pairs={{0,2},{2,4},{4,6},{6,8},{8,10},{10,12},{12,14},{14,0},{1,3},{3,5},... | collective-permute-start | bytes 442376 | tf_op jit(solution)/shard_map/ppermute | solution.py:557
  3.5 0.7 %shard_map.74 = (bf16[128,1024]{1,0:T(8,128)(2,1)S(1)}, bf16[128,128]{1,0:T(8,128)(2,1)S(1)}, bf16[144,512]{1,0:T(8,128)(2,1)S(1)}, bf16[272,512]{1,0:T(8,128)(2,1)S(1)}) custom-call(bf16[128,2560]{1,0:T(8,128)(2,1)S(1)} %get-tuple-element.40.x_ref, bf16[4,2560]{1,0:T(4,128)(2,1)S(1)} %get-tuple-element.41.weight_ref, ...), custom_call_target="tpu_custom_call" | custom-call | flops 40000000 | bytes 2000000 | tf_op jit(solution)/shard_map/pallas_call | solution.py:487
  4.1 0.1 collective-permute-start.4
  4.2 1.9 %collective-permute-start = (bf16[144,512]{1,0:T(8,128)(2,1)S(1)}, bf16[144,512]{1,0:T(8,128)(2,1)S(1)}, u32[]{:S(2)}, u32[]{:S(2)}) collective-permute-start(bf16[144,512]{1,0:T(8,128)(2,1)S(1)} %get-tuple-element.47.later_ref.own_ref), channel_id=1, source_target_pairs={{0,2},{2,4},{4,6},{6,8},{8,10},{10,12},{12,14},{14,0},{1,3},{3,5},... | collective-permute-start | bytes 442376 | tf_op jit(solution)/shard_map/ppermute | solution.py:571
  6.1 1.5 %shard_map.75 = (bf16[128,256]{1,0:T(8,128)(2,1)S(1)}, f32[7,16,512]{2,1,0:T(8,128)S(1)}, f32[16,512]{1,0:T(8,128)S(1)}, f32[8,2048]{1,0:T(8,128)S(1)}, f32[64,1...) custom-call(bf16[144,512]{1,0:T(8,128)(2,1)S(1)} %get-tuple-element.47.later_ref.own_ref, ...), custom_call_target="tpu_custom_call" | custom-call | flops 100000000 | bytes 1000000 | tf_op jit(solution)/shard_map/pallas_call | solution.py:487
  7.7 0.0 collective-permute-done.1.got_ref.first0_ref
  7.7 0.3 %shard_map.76 = (bf16[144,512]{1,0:T(8,128)(2,1)S(1)}, f32[8,2560]{1,0:T(8,128)S(1)}) custom-call(bf16[144,512]{1,0:T(8,128)(2,1)S(1)} %get-tuple-element.46.before_ref.own_ref, bf16[144,512]{1,0:T(8,128)(2,1)S(1)} %collective-permute-done.1.got_ref.first0_ref, f32[7,16,512]{2,1,0:T(8,128)S(1)} %get-tuple-element.53.table_ref, ...), custom_call_target="tpu_custom_call" | custom-call | flops 1000000 | bytes 1000000 | tf_op jit(solution)/shard_map/pallas_call | solution.py:487
  7.9 1.6 %collective-permute-start.3 = (bf16[144,512]{1,0:T(8,128)(2,1)S(1)}, bf16[144,512]{1,0:T(8,128)(2,1)S(1)}, u32[]{:S(2)}, u32[]{:S(2)}) collective-permute-start(bf16[144,512]{1,0:T(8,128)(2,1)S(1)} %get-tuple-element.59), channel_id=1, source_target_pairs={{0,1},{1,0},{2,6},{3,7},{4,8},{5,9},{6,10},{7,11},{8,12},{9,13},{1... | collective-permute-start | bytes 442376 | tf_op jit(solution)/shard_map/ppermute | solution.py:509
  9.5 0.8 %shard_map.77 = (f32[128,1024]{1,0:T(8,128)S(1)}, bf16[128,128]{1,0:T(8,128)(2,1)S(1)}, f32[128,512]{1,0:T(8,128)S(1)}) custom-call(bf16[128,1024]{1,0:T(8,128)(2,1)S(1)} %get-tuple-element.50.conv_ref, bf16[128,128]{1,0:T(8,128)(2,1)S(1)} %get-tuple-element.51.key_ref, bf16[128,256]{1,0:T(8,128)(2,1)S(1)} %get-tuple-element.52.raw_queries_ref, ...), custom_call_target="tpu_custom_call" | custom-call | flops 200000000 | bytes 2000000 | tf_op jit(solution)/shard_map/pallas_call | solution.py:487
  10.4 0.3 %collective-permute-done.got_ref.later_ref.first1_ref = bf16[144,512]{1,0:T(8,128)(2,1)S(1)} collective-permute-done((bf16[144,512]{1,0:T(8,128)(2,1)S(1)}, bf16[144,512]{1,0:T(8,128)(2,1)S(1)}, u32[]{:S(2)}, u32[]{:S(2)}) %collective-permute-start) | collective-permute-done | bytes 147488 | tf_op jit(solution)/shard_map/ppermute | solution.py:571
  10.7 0.1 shard_map.78
  10.7 1.6 %collective-permute-start.2 = (bf16[128,512]{1,0:T(8,128)(2,1)S(1)}, bf16[128,512]{1,0:T(8,128)(2,1)S(1)}, u32[]{:S(2)}, u32[]{:S(2)}) collective-permute-start(bf16[128,512]{1,0:T(8,128)(2,1)S(1)} %shard_map.78), channel_id=1, source_target_pairs={{0,1},{1,0},{2,6},{3,7},{4,8},{5,9},{6,10},{7,11},{8,12},{9,13},{1... | collective-permute-start | bytes 393224 | tf_op jit(solution)/shard_map/ppermute | solution.py:509
  12.3 0.8 %shard_map.79 = (f32[128,1024]{1,0:T(8,128)S(1)}, bf16[128,128]{1,0:T(8,128)(2,1)S(1)}, f32[16,512]{1,0:T(8,128)S(1)}, f32[8,2048]{1,0:T(8,128)S(1)}, bf16[1,128,2048]{2,1,0:T(8,128)(2,1)}) custom-call(bf16[128,1024]{1,0:T(8,128)(2,1)S(1)} %get-tuple-element.61.conv_ref, bf16[128,128]{1,0:T(8,128)(2,1)S(1)} %get-tuple-element.62.key_ref, ...), custom_call_target="tpu_custom_call" | custom-call | flops 200000000 | bytes 2000000 | tf_op jit(solution)/shard_map/pallas_call | solution.py:487
  13.1 0.0 collective-permute-done.4.early_ref
  13.2 3.5 %collective-permute-done.3.second_ref = bf16[144,512]{1,0:T(8,128)(2,1)S(1)} collective-permute-done((bf16[144,512]{1,0:T(8,128)(2,1)S(1)}, bf16[144,512]{1,0:T(8,128)(2,1)S(1)}, u32[]{:S(2)}, u32[]{:S(2)}) %collective-permute-start.3) | collective-permute-done | bytes 147488 | tf_op jit(solution)/shard_map/ppermute | solution.py:509
  16.6 1.5 %shard_map.80 = (bf16[1,128,2048]{2,1,0:T(8,128)(2,1)}, bf16[128,1024]{1,0:T(8,128)(2,1)S(1)}, f32[128,512]{1,0:T(8,128)S(1)}, f32[16,512]{1,0:T(8,128)S(1)}) custom-call(bf16[144,512]{1,0:T(8,128)(2,1)S(1)} %collective-permute-done.1.got_ref.first0_ref, ...), custom_call_target="tpu_custom_call", output_to_operand_aliasing={{0}: (13, {})} | custom-call | flops 50000000 | bytes 2000000 | tf_op jit(solution)/shard_map/pallas_call | solution.py:487
  18.2 0.4 %collective-permute-done.2.second_ref = bf16[128,512]{1,0:T(8,128)(2,1)S(1)} collective-permute-done((bf16[128,512]{1,0:T(8,128)(2,1)S(1)}, bf16[128,512]{1,0:T(8,128)(2,1)S(1)}, u32[]{:S(2)}, u32[]{:S(2)}) %collective-permute-start.2) | collective-permute-done | bytes 131104 | tf_op jit(solution)/shard_map/ppermute | solution.py:509
  (1 shorter events, 0.0 us)
Async XLA Ops:
  1.9 5.8 %collective-permute-start.1 = (bf16[144,512]{1,0:T(8,128)(2,1)S(1)}, bf16[144,512]{1,0:T(8,128)(2,1)S(1)}, u32[]{:S(2)}, u32[]{:S(2)}) collective-permute-start(bf16[144,512]{1,0:T(8,128)(2,1)S(1)} %get-tuple-element.46.before_ref.own_ref), channel_id=1, source_target_pairs={{0,2},{2,4},{4,6},{6,8},{8,10},{10,12},{12,14},{14,0},{1,3},{3,5},... | collective-permute-start | bytes 442376 | tf_op jit(solution)/shard_map/ppermute | solution.py:557
  4.1 9.0 %collective-permute-start.4 = (bf16[272,512]{1,0:T(8,128)(2,1)S(1)}, bf16[272,512]{1,0:T(8,128)(2,1)S(1)}, u32[]{:S(2)}, u32[]{:S(2)}) collective-permute-start(bf16[272,512]{1,0:T(8,128)(2,1)S(1)} %get-tuple-element.60), channel_id=1, source_target_pairs={{0,4},{1,5},{2,3},{3,2},{4,0},{5,1},{6,7},{7,6},{8,9},{9,8},{10,11... | collective-permute-start | bytes 835592 | tf_op jit(solution)/shard_map/ppermute | solution.py:509
  4.2 6.4 %collective-permute-start = (bf16[144,512]{1,0:T(8,128)(2,1)S(1)}, bf16[144,512]{1,0:T(8,128)(2,1)S(1)}, u32[]{:S(2)}, u32[]{:S(2)}) collective-permute-start(bf16[144,512]{1,0:T(8,128)(2,1)S(1)} %get-tuple-element.47.later_ref.own_ref), channel_id=1, source_target_pairs={{0,2},{2,4},{4,6},{6,8},{8,10},{10,12},{12,14},{14,0},{1,3},{3,5},... | collective-permute-start | bytes 442376 | tf_op jit(solution)/shard_map/ppermute | solution.py:571
  7.9 8.7 %collective-permute-start.3 = (bf16[144,512]{1,0:T(8,128)(2,1)S(1)}, bf16[144,512]{1,0:T(8,128)(2,1)S(1)}, u32[]{:S(2)}, u32[]{:S(2)}) collective-permute-start(bf16[144,512]{1,0:T(8,128)(2,1)S(1)} %get-tuple-element.59), channel_id=1, source_target_pairs={{0,1},{1,0},{2,6},{3,7},{4,8},{5,9},{6,10},{7,11},{8,12},{9,13},{1... | collective-permute-start | bytes 442376 | tf_op jit(solution)/shard_map/ppermute | solution.py:509
  10.7 7.9 %collective-permute-start.2 = (bf16[128,512]{1,0:T(8,128)(2,1)S(1)}, bf16[128,512]{1,0:T(8,128)(2,1)S(1)}, u32[]{:S(2)}, u32[]{:S(2)}) collective-permute-start(bf16[128,512]{1,0:T(8,128)(2,1)S(1)} %shard_map.78), channel_id=1, source_target_pairs={{0,1},{1,0},{2,6},{3,7},{4,8},{5,9},{6,10},{7,11},{8,12},{9,13},{1... | collective-permute-start | bytes 393224 | tf_op jit(solution)/shard_map/ppermute | solution.py:509

commit v7 on v6

--- a/solution.py
+++ b/solution.py
@@ -241,9 +241,18 @@
     return head_lanes(jnp.concatenate(rows + [jnp.zeros((12, 128), f32)], axis=0).astype(bf16))
 
 
+def causal_mask(count):
+    return iota((count, count), 0) >= iota((count, count), 1)
+
+
+def token_decay(at, across_ref, down_ref, causal):
+    gap = down_ref[:, at : at + 1] - across_ref[at : at + 1, :]
+    return jnp.exp2(jnp.where(causal, gap, -1e30))
+
+
 def prepare_kernel(
     later_ref, x_ref, weight_ref, bias_ref, cumulative_ref, step_ref, skip_ref, gates_ref,
-    queries_ref, table_ref, known_ref, scale_ref, decay_ref, entry_ref, gain_ref, pads_ref,
+    queries_ref, table_ref, known_ref, scale_ref, decay_ref, across_ref, down_ref, entry_ref, gain_ref, pads_ref,
 ):
     clear(pads_ref)
     weight, bias = half_taps(weight_ref, bias_ref)
@@ -276,13 +285,11 @@
     known_ref[...] = known_part(later_ref[HEAD_AT : HEAD_AT + 16, :].astype(f32), table_ref)
     scale_ref[...] = edge_scales(later_ref[HEAD_AT : HEAD_AT + 16, :]) * gates_ref[:1, :1]
     cumulative = cumulative_ref[...] * LOG2E
-    across = cumulative - jnp.log2(step_ref[...])
-    down = cumulative.T
-    count = down.shape[0]
-    causal = iota((count, count), 0) >= iota((count, count), 1)
-    for at in range(HEADS):
-        gap = down[:, at : at + 1] - across[at : at + 1, :]
-        decay_ref[at] = jnp.exp2(jnp.where(causal, gap, -1e30))
+    across_ref[...] = cumulative - jnp.log2(step_ref[...])
+    down_ref[...] = cumulative.T
+    causal = causal_mask(across_ref.shape[1])
+    for at in range(HEADS // CHUNKS):
+        decay_ref[at] = token_decay(at, across_ref, down_ref, causal)
     matrix = spread_matrix()
     entry = jnp.exp2(cumulative)
     for group in range(BC_GROUPS):
@@ -337,7 +344,7 @@
     combine_chunk(own_ref, got_ref, decays, extras, sent_ref)
 
 
-def diagonal_chunk(chunk, conv_ref, key_ref, raw_queries_ref, edge_ref, decay_ref, gain_ref, diagonal_ref, queries_ref):
+def diagonal_chunk(chunk, conv_ref, key_ref, raw_queries_ref, edge_ref, decay_of, gain_ref, diagonal_ref, queries_ref):
     count = conv_ref.shape[0]
     edge_row = iota((count, 128), 0) < EDGE
     lane_head = iota((count, 128), 1) // HEAD_DIM
@@ -361,7 +368,7 @@
             values = patched(conv_ref[:, at : at + 128], j)
             weights, parts = [], []
             for k in range(4):
-                weights.append((decay_ref[4 * j + k] * scores).astype(bf16))
+                weights.append((decay_of(4 * j + k) * scores).astype(bf16))
                 parts.append(jnp.where(lane_head == k, values, 0.0).astype(bf16))
             total = dot(jnp.concatenate(weights, axis=1), jnp.concatenate(parts, axis=0))
             diagonal_ref[:, at : at + 128] = total + gain_ref[:1, j * 128 : (j + 1) * 128] * values
@@ -378,17 +385,25 @@
         extra_ref[index * STATE : (index + 1) * STATE, :] = edge_state(
             edge_ref[:, cols], keys, own_scale_ref[:, cols], group
         )
-    diagonal_chunk(0, conv_ref, key_ref, raw_queries_ref, edge_ref, decay_ref, gain_ref, diagonal_ref, queries_ref)
+    diagonal_chunk(
+        0, conv_ref, key_ref, raw_queries_ref, edge_ref, lambda at: decay_ref[at], gain_ref, diagonal_ref, queries_ref
+    )
 
 
 def diagonal_later_kernel(
-    conv_ref, key_ref, raw_queries_ref, edge_ref, decay_ref, gain_ref, later_ref, table_ref, gates_ref, before_ref,
+    conv_ref, key_ref, raw_queries_ref, edge_ref, across_ref, down_ref, gain_ref, later_ref, table_ref, gates_ref,
+    before_ref,
     diagonal_ref, queries_ref, known_ref, scale_ref, out_hbm, out_ref, sems,
 ):
     head_rows = later_ref[HEAD_AT : HEAD_AT + 16, :]
     known_ref[...] = known_part(head_rows.astype(f32), table_ref)
     scale_ref[...] = edge_scales(head_rows) * gates_ref[1:2, :1]
-    diagonal_chunk(1, conv_ref, key_ref, raw_queries_ref, edge_ref, decay_ref, gain_ref, diagonal_ref, queries_ref)
+    causal = causal_mask(conv_ref.shape[0])
+    diagonal_chunk(
+        1, conv_ref, key_ref, raw_queries_ref, edge_ref,
+        lambda at: token_decay(at, across_ref, down_ref, causal),
+        gain_ref, diagonal_ref, queries_ref,
+    )
 
     @pl.when(lax.axis_index("ctx") == 0)
     def _():
@@ -570,14 +585,16 @@
     )
     first1 = lax.ppermute(own1, "ctx", ring)
     early = permuted(early, {0: 2, 2: 0})
-    raw_queries, table, known, scale, decay, entry, gain = call(
+    raw_queries, table, known, scale, decay, across, down, entry, gain = call(
         prepare_kernel,
         (
             sds((count, GROUPED), bf16),
             sds((7, 16, WIDE), f32),
             sds((16, WIDE), f32),
             sds((8, VALUES), f32),
-            sds((HEADS, count, count), f32),
+            sds((HEADS // CHUNKS, count, count), f32),
+            sds((HEADS, count), f32),
+            sds((count, HEADS), f32),
             sds((count, VALUES), f32),
             sds((8, VALUES), f32),
         ),
@@ -614,9 +631,9 @@
     diagonal1, queries1, known, scale, out = call(
         diagonal_later_kernel,
         diagonal_outs + (sds((16, WIDE), f32), sds((8, VALUES), f32), out_shape),
-        [VMEM] * 10,
+        [VMEM] * 11,
         (200_000_000, 2_000_000),
-        (conv1, key1, raw_queries, edge, decay, gain, first1, table, gates, diagonal0),
+        (conv1, key1, raw_queries, edge, across, down, gain, first1, table, gates, diagonal0),
         out_specs=(VMEM, VMEM, VMEM, VMEM, HBM),
         scratch=(pltpu.VMEM((count, VALUES), bf16), pltpu.SemaphoreType.DMA((CHUNKS,))),
     )

time: 18.8 us -> 18.8 us (level)
  the two profiles are of different devices: /device:TPU:2 before, /device:TPU:0 now
where the time goes in v7:
time: 18.8 us; the launch traced here: 18.4 us
  waiting for transfers between devices  7.09 us (38%)
  Pallas kernels  6.47 us (34%)
  starting transfers between devices  4.79 us (25%)
    pallas_call x9, Pallas kernels, call(): pl.pallas_call(kernel, out_shape=outs, in_specs=in_specs, out_specs=out_s...  6.47 us
    ppermute x1, waiting for transfers between devices, shard_near(): first0 = lax.ppermute(own0, 'ctx', ring)  3.58 us
    ppermute x1, waiting for transfers between devices, shard_near(): first1 = lax.ppermute(own1, 'ctx', ring)  3.5 us
    ppermute x1, starting transfers between devices, shard_near(): first0 = lax.ppermute(own0, 'ctx', ring)  2.99 us
    ppermute x3, starting transfers between devices, permuted(): return lax.ppermute(array, ('ctx', 'lane'), table)  1.75 us
  transfers between devices with their start and end apart: 5, of which 2 were waited for; matrix products, arithmetic and copies ran while one was open for 0% of the time, Pallas kernels for 25%

profile of v7, /device:TPU:0, one launch (start us, length us, event | category | flops | bytes accessed | tf_op | source)
XLA Modules:
  0.0 18.4 jit_solution(12579856881065565401)
XLA Ops:
  0.0 1.8 %shard_map.73 = (bf16[128,1024]{1,0:T(8,128)(2,1)S(1)}, bf16[128,128]{1,0:T(8,128)(2,1)S(1)}, f32[64,128]{1,0:T(8,128)S(1)}, bf16[144,512]{1,0:T(8,128)(2,1)S(1)...) custom-call(s32[1,4]{1,0:T(1,128)} %lengths_hbm.1, ...), custom_call_target="tpu_custom_call" | custom-call | flops 40000000 | bytes 2000000 | tf_op jit(solution)/shard_map/pallas_call | solution.py:502
  1.9 3.0 %collective-permute-start.1 = (bf16[144,512]{1,0:T(8,128)(2,1)S(1)}, bf16[144,512]{1,0:T(8,128)(2,1)S(1)}, u32[]{:S(2)}, u32[]{:S(2)}) collective-permute-start(bf16[144,512]{1,0:T(8,128)(2,1)S(1)} %get-tuple-element.48.before_ref.own_ref), channel_id=1, source_target_pairs={{0,2},{2,4},{4,6},{6,8},{8,10},{10,12},{12,14},{14,0},{1,3},{3,5},... | collective-permute-start | bytes 442376 | tf_op jit(solution)/shard_map/ppermute | solution.py:572
  4.8 0.7 %shard_map.74 = (bf16[128,1024]{1,0:T(8,128)(2,1)S(1)}, bf16[128,128]{1,0:T(8,128)(2,1)S(1)}, bf16[144,512]{1,0:T(8,128)(2,1)S(1)}, bf16[272,512]{1,0:T(8,128)(2,1)S(1)}) custom-call(bf16[128,2560]{1,0:T(8,128)(2,1)S(1)} %get-tuple-element.42.x_ref, bf16[4,2560]{1,0:T(4,128)(2,1)S(1)} %get-tuple-element.43.weight_ref, ...), custom_call_target="tpu_custom_call" | custom-call | flops 40000000 | bytes 2000000 | tf_op jit(solution)/shard_map/pallas_call | solution.py:502
  5.5 1.6 %collective-permute-start.4 = (bf16[272,512]{1,0:T(8,128)(2,1)S(1)}, bf16[272,512]{1,0:T(8,128)(2,1)S(1)}, u32[]{:S(2)}, u32[]{:S(2)}) collective-permute-start(bf16[272,512]{1,0:T(8,128)(2,1)S(1)} %get-tuple-element.62), channel_id=1, source_target_pairs={{0,4},{1,5},{2,3},{3,2},{4,0},{5,1},{6,7},{7,6},{8,9},{9,8},{10,11... | collective-permute-start | bytes 835592 | tf_op jit(solution)/shard_map/ppermute | solution.py:524
  7.2 0.0 collective-permute-start
  7.2 0.9 %shard_map.75 = (bf16[128,256]{1,0:T(8,128)(2,1)S(1)}, f32[7,16,512]{2,1,0:T(8,128)S(1)}, f32[16,512]{1,0:T(8,128)S(1)}, f32[8,2048]{1,0:T(8,128)S(1)}, f32[32,1...) custom-call(bf16[144,512]{1,0:T(8,128)(2,1)S(1)} %get-tuple-element., ...), custom_call_target="tpu_custom_call" | custom-call | flops 100000000 | bytes 1000000 | tf_op jit(solution)/shard_map/pallas_call | solution.py:502
  8.1 3.6 %collective-permute-done.1.got_ref.first0_ref = bf16[144,512]{1,0:T(8,128)(2,1)S(1)} collective-permute-done((bf16[144,512]{1,0:T(8,128)(2,1)S(1)}, bf16[144,512]{1,0:T(8,128)(2,1)S(1)}, u32[]{:S(2)}, u32[]{:S(2)}) %collective-permute-start.1) | collective-permute-done | bytes 147488 | tf_op jit(solution)/shard_map/ppermute | solution.py:572
  11.7 0.3 %shard_map.76 = (bf16[144,512]{1,0:T(8,128)(2,1)S(1)}, f32[8,2560]{1,0:T(8,128)S(1)}) custom-call(bf16[144,512]{1,0:T(8,128)(2,1)S(1)} %get-tuple-element.48.before_ref.own_ref, bf16[144,512]{1,0:T(8,128)(2,1)S(1)} %collective-permute-done.1.got_ref.first0_ref, f32[7,16,512]{2,1,0:T(8,128)S(1)} %get-tuple-element.55.table_ref, ...), custom_call_target="tpu_custom_call" | custom-call | flops 1000000 | bytes 1000000 | tf_op jit(solution)/shard_map/pallas_call | solution.py:502
  12.0 0.1 collective-permute-start.3
  12.1 0.8 %shard_map.77 = (f32[128,1024]{1,0:T(8,128)S(1)}, bf16[128,128]{1,0:T(8,128)(2,1)S(1)}, f32[128,512]{1,0:T(8,128)S(1)}) custom-call(bf16[128,1024]{1,0:T(8,128)(2,1)S(1)} %get-tuple-element.52.conv_ref, bf16[128,128]{1,0:T(8,128)(2,1)S(1)} %get-tuple-element.53.key_ref, bf16[128,256]{1,0:T(8,128)(2,1)S(1)} %get-tuple-element.54.raw_queries_ref, ...), custom_call_target="tpu_custom_call" | custom-call | flops 200000000 | bytes 2000000 | tf_op jit(solution)/shard_map/pallas_call | solution.py:502
  12.9 3.5 %collective-permute-done.got_ref.later_ref.first1_ref = bf16[144,512]{1,0:T(8,128)(2,1)S(1)} collective-permute-done((bf16[144,512]{1,0:T(8,128)(2,1)S(1)}, bf16[144,512]{1,0:T(8,128)(2,1)S(1)}, u32[]{:S(2)}, u32[]{:S(2)}) %collective-permute-start) | collective-permute-done | bytes 147488 | tf_op jit(solution)/shard_map/ppermute | solution.py:586
  16.4 0.1 shard_map.78
  16.5 0.1 collective-permute-start.2
  16.5 1.8 %shard_map.79 = (f32[128,1024]{1,0:T(8,128)S(1)}, bf16[128,128]{1,0:T(8,128)(2,1)S(1)}, f32[16,512]{1,0:T(8,128)S(1)}, f32[8,2048]{1,0:T(8,128)S(1)}, bf16[1,128,2048]{2,1,0:T(8,128)(2,1)}) custom-call(bf16[128,1024]{1,0:T(8,128)(2,1)S(1)} %get-tuple-element.63.conv_ref, bf16[128,128]{1,0:T(8,128)(2,1)S(1)} %get-tuple-element.64.key_ref, ...), custom_call_target="tpu_custom_call" | custom-call | flops 200000000 | bytes 2000000 | tf_op jit(solution)/shard_map/pallas_call | solution.py:502
  18.3 0.0 collective-permute-done.4.early_ref
  18.3 0.0 collective-permute-done.3.second_ref
  18.4 0.0 collective-permute-done.2.second_ref
  (2 shorter events, 0.1 us)
Async XLA Ops:
  1.9 9.9 %collective-permute-start.1 = (bf16[144,512]{1,0:T(8,128)(2,1)S(1)}, bf16[144,512]{1,0:T(8,128)(2,1)S(1)}, u32[]{:S(2)}, u32[]{:S(2)}) collective-permute-start(bf16[144,512]{1,0:T(8,128)(2,1)S(1)} %get-tuple-element.48.before_ref.own_ref), channel_id=1, source_target_pairs={{0,2},{2,4},{4,6},{6,8},{8,10},{10,12},{12,14},{14,0},{1,3},{3,5},... | collective-permute-start | bytes 442376 | tf_op jit(solution)/shard_map/ppermute | solution.py:572
  5.5 12.8 %collective-permute-start.4 = (bf16[272,512]{1,0:T(8,128)(2,1)S(1)}, bf16[272,512]{1,0:T(8,128)(2,1)S(1)}, u32[]{:S(2)}, u32[]{:S(2)}) collective-permute-start(bf16[272,512]{1,0:T(8,128)(2,1)S(1)} %get-tuple-element.62), channel_id=1, source_target_pairs={{0,4},{1,5},{2,3},{3,2},{4,0},{5,1},{6,7},{7,6},{8,9},{9,8},{10,11... | collective-permute-start | bytes 835592 | tf_op jit(solution)/shard_map/ppermute | solution.py:524
  7.2 9.2 %collective-permute-start = (bf16[144,512]{1,0:T(8,128)(2,1)S(1)}, bf16[144,512]{1,0:T(8,128)(2,1)S(1)}, u32[]{:S(2)}, u32[]{:S(2)}) collective-permute-start(bf16[144,512]{1,0:T(8,128)(2,1)S(1)} %get-tuple-element.49.later_ref.own_ref), channel_id=1, source_target_pairs={{0,2},{2,4},{4,6},{6,8},{8,10},{10,12},{12,14},{14,0},{1,3},{3,5},... | collective-permute-start | bytes 442376 | tf_op jit(solution)/shard_map/ppermute | solution.py:586
  12.0 6.3 %collective-permute-start.3 = (bf16[144,512]{1,0:T(8,128)(2,1)S(1)}, bf16[144,512]{1,0:T(8,128)(2,1)S(1)}, u32[]{:S(2)}, u32[]{:S(2)}) collective-permute-start(bf16[144,512]{1,0:T(8,128)(2,1)S(1)} %get-tuple-element.61), channel_id=1, source_target_pairs={{0,1},{1,0},{2,6},{3,7},{4,8},{5,9},{6,10},{7,11},{8,12},{9,13},{1... | collective-permute-start | bytes 442376 | tf_op jit(solution)/shard_map/ppermute | solution.py:524
  16.5 1.9 %collective-permute-start.2 = (bf16[128,512]{1,0:T(8,128)(2,1)S(1)}, bf16[128,512]{1,0:T(8,128)(2,1)S(1)}, u32[]{:S(2)}, u32[]{:S(2)}) collective-permute-start(bf16[128,512]{1,0:T(8,128)(2,1)S(1)} %shard_map.78), channel_id=1, source_target_pairs={{0,1},{1,0},{2,6},{3,7},{4,8},{5,9},{6,10},{7,11},{8,12},{9,13},{1... | collective-permute-start | bytes 393224 | tf_op jit(solution)/shard_map/ppermute | solution.py:524

commit v8 on v7

--- a/solution.py
+++ b/solution.py
@@ -252,7 +252,7 @@
 
 def prepare_kernel(
     later_ref, x_ref, weight_ref, bias_ref, cumulative_ref, step_ref, skip_ref, gates_ref,
-    queries_ref, table_ref, known_ref, scale_ref, decay_ref, across_ref, down_ref, entry_ref, gain_ref, pads_ref,
+    queries_ref, table_ref, known_ref, scale_ref, across_ref, down_ref, entry_ref, gain_ref, pads_ref,
 ):
     clear(pads_ref)
     weight, bias = half_taps(weight_ref, bias_ref)
@@ -287,9 +287,6 @@
     cumulative = cumulative_ref[...] * LOG2E
     across_ref[...] = cumulative - jnp.log2(step_ref[...])
     down_ref[...] = cumulative.T
-    causal = causal_mask(across_ref.shape[1])
-    for at in range(HEADS // CHUNKS):
-        decay_ref[at] = token_decay(at, across_ref, down_ref, causal)
     matrix = spread_matrix()
     entry = jnp.exp2(cumulative)
     for group in range(BC_GROUPS):
@@ -375,7 +372,7 @@
 
 
 def diagonal_first_kernel(
-    conv_ref, key_ref, raw_queries_ref, edge_ref, decay_ref, gain_ref, own_scale_ref,
+    conv_ref, key_ref, raw_queries_ref, edge_ref, across_ref, down_ref, gain_ref, own_scale_ref,
     diagonal_ref, queries_ref, extra_ref,
 ):
     keys = edge_ref[:, BC_GROUPS * WIDE :]
@@ -385,8 +382,11 @@
         extra_ref[index * STATE : (index + 1) * STATE, :] = edge_state(
             edge_ref[:, cols], keys, own_scale_ref[:, cols], group
         )
+    causal = causal_mask(conv_ref.shape[0])
     diagonal_chunk(
-        0, conv_ref, key_ref, raw_queries_ref, edge_ref, lambda at: decay_ref[at], gain_ref, diagonal_ref, queries_ref
+        0, conv_ref, key_ref, raw_queries_ref, edge_ref,
+        lambda at: token_decay(at, across_ref, down_ref, causal),
+        gain_ref, diagonal_ref, queries_ref,
     )
 
 
@@ -585,14 +585,13 @@
     )
     first1 = lax.ppermute(own1, "ctx", ring)
     early = permuted(early, {0: 2, 2: 0})
-    raw_queries, table, known, scale, decay, across, down, entry, gain = call(
+    raw_queries, table, known, scale, across, down, entry, gain = call(
         prepare_kernel,
         (
             sds((count, GROUPED), bf16),
             sds((7, 16, WIDE), f32),
             sds((16, WIDE), f32),
             sds((8, VALUES), f32),
-            sds((HEADS // CHUNKS, count, count), f32),
             sds((HEADS, count), f32),
             sds((count, HEADS), f32),
             sds((count, VALUES), f32),
@@ -615,9 +614,9 @@
     diagonal0, queries0, extra = call(
         diagonal_first_kernel,
         diagonal_outs + (sds((ROWS, WIDE), f32),),
-        [VMEM] * 7,
+        [VMEM] * 8,
         (200_000_000, 2_000_000),
-        (conv0, key0, raw_queries, edge, decay, gain, scale),
+        (conv0, key0, raw_queries, edge, across, down, gain, scale),
     )
     sent1 = call(
         combine_later_kernel,

time: 18.8 us -> 18.8 us (level)
  Pallas kernels: 6.47 us -> 6.22 us
  waiting for transfers between devices: 7.09 us -> 7.34 us
    ppermute x1, waiting for transfers between devices: 3.58 us -> 3.98 us  [shard_near(): first0 = lax.ppermute(own0, 'ctx', ring)]
    pallas_call x9, Pallas kernels: 6.47 us -> 6.22 us  [call(): pl.pallas_call(kernel, out_shape=outs, in_specs=in_specs, out_specs=out_s...]
  transfers between devices with their start and end apart: 5 -> 5, of which waited for: 2 -> 2; matrix products, arithmetic and copies ran while one was open for 0% -> 0% of each run, Pallas kernels for 25% -> 24%
where the time goes in v8:
time: 18.8 us; the launch traced here: 18.4 us
  waiting for transfers between devices  7.34 us (39%)
  Pallas kernels  6.22 us (33%)
  starting transfers between devices  4.78 us (25%)
    pallas_call x9, Pallas kernels, call(): pl.pallas_call(kernel, out_shape=outs, in_specs=in_specs, out_specs=out_s...  6.22 us
    ppermute x1, waiting for transfers between devices, shard_near(): first0 = lax.ppermute(own0, 'ctx', ring)  3.98 us
    ppermute x1, waiting for transfers between devices, shard_near(): first1 = lax.ppermute(own1, 'ctx', ring)  3.35 us
    ppermute x1, starting transfers between devices, shard_near(): first0 = lax.ppermute(own0, 'ctx', ring)  2.99 us
    ppermute x3, starting transfers between devices, permuted(): return lax.ppermute(array, ('ctx', 'lane'), table)  1.75 us
  transfers between devices with their start and end apart: 5, of which 2 were waited for; matrix products, arithmetic and copies ran while one was open for 0% of the time, Pallas kernels for 24%

profile of v8, /device:TPU:0, one launch (start us, length us, event | category | flops | bytes accessed | tf_op | source)
XLA Modules:
  0.0 18.4 jit_solution(1117552441965147941)
XLA Ops:
  0.0 1.8 %shard_map.73 = (bf16[128,1024]{1,0:T(8,128)(2,1)S(1)}, bf16[128,128]{1,0:T(8,128)(2,1)S(1)}, f32[64,128]{1,0:T(8,128)S(1)}, bf16[144,512]{1,0:T(8,128)(2,1)S(1)...) custom-call(s32[1,4]{1,0:T(1,128)} %lengths_hbm.1, ...), custom_call_target="tpu_custom_call" | custom-call | flops 40000000 | bytes 2000000 | tf_op jit(solution)/shard_map/pallas_call | solution.py:502
  1.9 3.0 %collective-permute-start.1 = (bf16[144,512]{1,0:T(8,128)(2,1)S(1)}, bf16[144,512]{1,0:T(8,128)(2,1)S(1)}, u32[]{:S(2)}, u32[]{:S(2)}) collective-permute-start(bf16[144,512]{1,0:T(8,128)(2,1)S(1)} %get-tuple-element.47.before_ref.own_ref), channel_id=1, source_target_pairs={{0,2},{2,4},{4,6},{6,8},{8,10},{10,12},{12,14},{14,0},{1,3},{3,5},... | collective-permute-start | bytes 442376 | tf_op jit(solution)/shard_map/ppermute | solution.py:572
  4.8 0.7 %shard_map.74 = (bf16[128,1024]{1,0:T(8,128)(2,1)S(1)}, bf16[128,128]{1,0:T(8,128)(2,1)S(1)}, bf16[144,512]{1,0:T(8,128)(2,1)S(1)}, bf16[272,512]{1,0:T(8,128)(2,1)S(1)}) custom-call(bf16[128,2560]{1,0:T(8,128)(2,1)S(1)} %get-tuple-element.41.x_ref, bf16[4,2560]{1,0:T(4,128)(2,1)S(1)} %get-tuple-element.42.weight_ref, ...), custom_call_target="tpu_custom_call" | custom-call | flops 40000000 | bytes 2000000 | tf_op jit(solution)/shard_map/pallas_call | solution.py:502
  5.5 1.6 %collective-permute-start.4 = (bf16[272,512]{1,0:T(8,128)(2,1)S(1)}, bf16[272,512]{1,0:T(8,128)(2,1)S(1)}, u32[]{:S(2)}, u32[]{:S(2)}) collective-permute-start(bf16[272,512]{1,0:T(8,128)(2,1)S(1)} %get-tuple-element.62), channel_id=1, source_target_pairs={{0,4},{1,5},{2,3},{3,2},{4,0},{5,1},{6,7},{7,6},{8,9},{9,8},{10,11... | collective-permute-start | bytes 835592 | tf_op jit(solution)/shard_map/ppermute | solution.py:524
  7.2 0.0 collective-permute-start
  7.2 0.5 %shard_map.75 = (bf16[128,256]{1,0:T(8,128)(2,1)S(1)}, f32[7,16,512]{2,1,0:T(8,128)S(1)}, f32[16,512]{1,0:T(8,128)S(1)}, f32[8,2048]{1,0:T(8,128)S(1)}, f32[64,1...) custom-call(bf16[144,512]{1,0:T(8,128)(2,1)S(1)} %get-tuple-element.48.later_ref.own_ref, ...), custom_call_target="tpu_custom_call" | custom-call | flops 100000000 | bytes 1000000 | tf_op jit(solution)/shard_map/pallas_call | solution.py:502
  7.8 4.0 %collective-permute-done.1.got_ref.first0_ref = bf16[144,512]{1,0:T(8,128)(2,1)S(1)} collective-permute-done((bf16[144,512]{1,0:T(8,128)(2,1)S(1)}, bf16[144,512]{1,0:T(8,128)(2,1)S(1)}, u32[]{:S(2)}, u32[]{:S(2)}) %collective-permute-start.1) | collective-permute-done | bytes 147488 | tf_op jit(solution)/shard_map/ppermute | solution.py:572
  11.7 0.3 %shard_map.76 = (bf16[144,512]{1,0:T(8,128)(2,1)S(1)}, f32[8,2560]{1,0:T(8,128)S(1)}) custom-call(bf16[144,512]{1,0:T(8,128)(2,1)S(1)} %get-tuple-element.47.before_ref.own_ref, bf16[144,512]{1,0:T(8,128)(2,1)S(1)} %collective-permute-done.1.got_ref.first0_ref, f32[7,16,512]{2,1,0:T(8,128)S(1)} %get-tuple-element.54.table_ref, ...), custom_call_target="tpu_custom_call" | custom-call | flops 1000000 | bytes 1000000 | tf_op jit(solution)/shard_map/pallas_call | solution.py:502
  12.0 0.1 collective-permute-start.3
  12.1 1.0 %shard_map.77 = (f32[128,1024]{1,0:T(8,128)S(1)}, bf16[128,128]{1,0:T(8,128)(2,1)S(1)}, f32[128,512]{1,0:T(8,128)S(1)}) custom-call(bf16[128,1024]{1,0:T(8,128)(2,1)S(1)} %get-tuple-element.51.conv_ref, bf16[128,128]{1,0:T(8,128)(2,1)S(1)} %get-tuple-element.52.key_ref, bf16[128,256]{1,0:T(8,128)(2,1)S(1)} %get-tuple-element.53.raw_queries_ref, ...), custom_call_target="tpu_custom_call" | custom-call | flops 200000000 | bytes 2000000 | tf_op jit(solution)/shard_map/pallas_call | solution.py:502
  13.1 3.4 %collective-permute-done.got_ref.later_ref.first1_ref = bf16[144,512]{1,0:T(8,128)(2,1)S(1)} collective-permute-done((bf16[144,512]{1,0:T(8,128)(2,1)S(1)}, bf16[144,512]{1,0:T(8,128)(2,1)S(1)}, u32[]{:S(2)}, u32[]{:S(2)}) %collective-permute-start) | collective-permute-done | bytes 147488 | tf_op jit(solution)/shard_map/ppermute | solution.py:586
  16.4 0.1 shard_map.78
  16.5 0.1 collective-permute-start.2
  16.5 1.7 %shard_map.79 = (f32[128,1024]{1,0:T(8,128)S(1)}, bf16[128,128]{1,0:T(8,128)(2,1)S(1)}, f32[16,512]{1,0:T(8,128)S(1)}, f32[8,2048]{1,0:T(8,128)S(1)}, bf16[1,128,2048]{2,1,0:T(8,128)(2,1)}) custom-call(bf16[128,1024]{1,0:T(8,128)(2,1)S(1)} %get-tuple-element.63.conv_ref, bf16[128,128]{1,0:T(8,128)(2,1)S(1)} %get-tuple-element.64.key_ref, ...), custom_call_target="tpu_custom_call" | custom-call | flops 200000000 | bytes 2000000 | tf_op jit(solution)/shard_map/pallas_call | solution.py:502
  18.3 0.0 collective-permute-done.4.early_ref
  18.3 0.0 collective-permute-done.3.second_ref
  18.4 0.0 collective-permute-done.2.second_ref
  (2 shorter events, 0.1 us)
Async XLA Ops:
  1.9 9.9 %collective-permute-start.1 = (bf16[144,512]{1,0:T(8,128)(2,1)S(1)}, bf16[144,512]{1,0:T(8,128)(2,1)S(1)}, u32[]{:S(2)}, u32[]{:S(2)}) collective-permute-start(bf16[144,512]{1,0:T(8,128)(2,1)S(1)} %get-tuple-element.47.before_ref.own_ref), channel_id=1, source_target_pairs={{0,2},{2,4},{4,6},{6,8},{8,10},{10,12},{12,14},{14,0},{1,3},{3,5},... | collective-permute-start | bytes 442376 | tf_op jit(solution)/shard_map/ppermute | solution.py:572
  5.5 12.8 %collective-permute-start.4 = (bf16[272,512]{1,0:T(8,128)(2,1)S(1)}, bf16[272,512]{1,0:T(8,128)(2,1)S(1)}, u32[]{:S(2)}, u32[]{:S(2)}) collective-permute-start(bf16[272,512]{1,0:T(8,128)(2,1)S(1)} %get-tuple-element.62), channel_id=1, source_target_pairs={{0,4},{1,5},{2,3},{3,2},{4,0},{5,1},{6,7},{7,6},{8,9},{9,8},{10,11... | collective-permute-start | bytes 835592 | tf_op jit(solution)/shard_map/ppermute | solution.py:524
  7.2 9.2 %collective-permute-start = (bf16[144,512]{1,0:T(8,128)(2,1)S(1)}, bf16[144,512]{1,0:T(8,128)(2,1)S(1)}, u32[]{:S(2)}, u32[]{:S(2)}) collective-permute-start(bf16[144,512]{1,0:T(8,128)(2,1)S(1)} %get-tuple-element.48.later_ref.own_ref), channel_id=1, source_target_pairs={{0,2},{2,4},{4,6},{6,8},{8,10},{10,12},{12,14},{14,0},{1,3},{3,5},... | collective-permute-start | bytes 442376 | tf_op jit(solution)/shard_map/ppermute | solution.py:586
  12.0 6.3 %collective-permute-start.3 = (bf16[144,512]{1,0:T(8,128)(2,1)S(1)}, bf16[144,512]{1,0:T(8,128)(2,1)S(1)}, u32[]{:S(2)}, u32[]{:S(2)}) collective-permute-start(bf16[144,512]{1,0:T(8,128)(2,1)S(1)} %get-tuple-element.61), channel_id=1, source_target_pairs={{0,1},{1,0},{2,6},{3,7},{4,8},{5,9},{6,10},{7,11},{8,12},{9,13},{1... | collective-permute-start | bytes 442376 | tf_op jit(solution)/shard_map/ppermute | solution.py:524
  16.5 1.9 %collective-permute-start.2 = (bf16[128,512]{1,0:T(8,128)(2,1)S(1)}, bf16[128,512]{1,0:T(8,128)(2,1)S(1)}, u32[]{:S(2)}, u32[]{:S(2)}) collective-permute-start(bf16[128,512]{1,0:T(8,128)(2,1)S(1)} %shard_map.78), channel_id=1, source_target_pairs={{0,1},{1,0},{2,6},{3,7},{4,8},{5,9},{6,10},{7,11},{8,12},{9,13},{1... | collective-permute-start | bytes 393224 | tf_op jit(solution)/shard_map/ppermute | solution.py:524
